TPU v7x, 32 devices: a whole 2x2x4 slice. The times are simulated.
32 devices in a mesh: star: 4 (over y, core), cad: 8 (over z, x).
Axes of the slice: x: 2, y: 2, z: 4, core: 2. Of those that a mesh axis runs over, the one named last changes fastest.
Arguments:
- light: float32 [16384, 2048], P('star', 'cad'), may hold values from -2000 to 2000
- quality: int32 [2048], P('cad'), may hold values 0 or 1
- star_factors: float32 [16384, 128], P('star', 'cad'), may hold values from -6 to 6
- cadence_factors: float32 [2048, 128], P('cad', 'star'), may hold values from -6 to 6
Outputs:
- star_gradient: float32 [16384, 128], P('star', 'cad')
- cadence_gradient: float32 [2048, 128], P('cad', 'star')
- loss: float32 [], replicated
All inputs are finite; a program needn't handle non-finite values. No bound on the sum of `quality` on one device may be relied on, other than what follows from the above.
Results may differ from a plain program's by a relative error of at most 0.0003.
Values sent between devices are 32-bit elements; how exact they have to be, the bound alone decides.
No kernel may reach another device: no remote copies, remote signals or barrier semaphores. Data moves between devices by JAX's collectives and lax.ppermute only.
A program may use at most 64 MiB of HBM per device.

v0:
```python
import jax
import jax.numpy as jnp
from jax import lax
from jax.sharding import PartitionSpec as P


def on_device(light, quality, star_factors, cadence_factors):
    star_count = light.shape[0] * lax.axis_size("star")
    cad_count = light.shape[1] * lax.axis_size("cad")
    star_loads = lax.all_gather(star_factors, "cad", axis=1, tiled=True)
    cad_loads = lax.all_gather(cadence_factors, "star", axis=1, tiled=True)
    predicted = jnp.dot(
        star_loads, cad_loads.T, precision=lax.Precision.HIGHEST, preferred_element_type=jnp.float32
    )
    residual = light - predicted
    ratio = 1.0 + (residual * 0.5) ** 2
    good = quality.astype(jnp.float32)[None, :]
    weighted = good * residual / ratio
    loss_part = jnp.sum(good * 2.0 * jnp.log(ratio))
    star_term = jnp.dot(
        weighted, cad_loads, precision=lax.Precision.HIGHEST, preferred_element_type=jnp.float32
    )
    cad_term = jnp.dot(
        weighted.T, star_loads, precision=lax.Precision.HIGHEST, preferred_element_type=jnp.float32
    )
    star_width = star_factors.shape[1]
    cad_width = cadence_factors.shape[1]
    star_full, loss_cad = lax.psum((star_term, loss_part), "cad")
    cad_full, loss_all = lax.psum((cad_term, loss_cad), "star")
    star_sum = lax.dynamic_slice_in_dim(
        star_full, lax.axis_index("cad") * star_width, star_width, 1
    )
    cad_sum = lax.dynamic_slice_in_dim(cad_full, lax.axis_index("star") * cad_width, cad_width, 1)
    star_gradient = -star_sum / jnp.sqrt(jnp.float32(cad_count))
    cadence_gradient = -cad_sum / jnp.sqrt(jnp.float32(star_count))
    loss = loss_all / (jnp.float32(star_count) * jnp.float32(cad_count))
    return (star_gradient, cadence_gradient, loss)


def solution(mesh):
    in_specs = (P("star", "cad"), P("cad"), P("star", "cad"), P("cad", "star"))
    out_specs = (P("star", "cad"), P("cad", "star"), P())
    return jax.shard_map(
        on_device, mesh=mesh, in_specs=in_specs, out_specs=out_specs, check_vma=False
    )
```

profile of v0, /device:TPU:0, one launch (start us, length us, event | category | flops | bytes accessed | tf_op | source)
XLA Modules:
  0.0 221.4 jit_solution(8103959761742515088)
XLA Ops:
  7.2 0.0 all-gather.2.cloned.1.call-start
  7.2 0.7 all-gather.2.cloned.1.call-update
  7.9 0.0 all-reduce.5.cloned.1.call-start
  7.9 0.7 convert_element_type.3
  8.6 6.7 %all_gather.7 = f32[256,128]{0,1:T(8,128)S(1)} all-gather(f32[256,32]{0,1:T(8,128)} %param.7), channel_id=1, replica_groups=mesh['star'=4,'cad'=8] {'star'}, dimensions={1}, use_global_device_ids=true | all-gather | bytes 163840 | tf_op jit(solution)/shard_map/all_gather | solution.py:11
  15.3 0.7 broadcast_multiply_fusion
  16.0 46.1 %all-gather.2.cloned.1.call-done = f32[4096,128]{0,1:T(8,128)} async-done(((f32[4096,16]{0,1:T(8,128)}), f32[4096,128]{0,1:T(8,128)}) %all-gather.2.cloned.1.call-update) | async-done | bytes 2097168 | tf_op jit(solution)/shard_map/all_gather | solution.py:10
  62.1 0.0 copy-start.1
  62.1 8.0 %multiply_reduce_fusion = (f32[]{:T(128)}, f32[4096,256]{1,0:T(8,128)S(1)}) fusion(f32[256]{0:T(256)S(1)} %broadcast_multiply_fusion, f32[4096,256]{1,0:T(8,128)} %param.4, f32[4096,128]{0,1:T(8,128)} %all-gather.2.cloned.1.call-done, f32[256,128]{0,1:T(8,128)S(1)} %all_gather.7), kind=kOutput, calls=%fused_computation.1 | convolution fusion | flops 1616904192 | bytes 10617860 | tf_op jit(solution)/shard_map/dot_general | solution.py:12
  70.1 0.0 copy-start
  70.1 1.9 copy-done
  72.1 0.0 copy-done.1
  72.1 4.0 %fusion = f32[256,128]{0,1:T(8,128)} fusion(f32[4096,128]{0,1:T(8,128)S(1)} %copy-done.1, f32[4096,256]{1,0:T(8,128)S(1)} %get-tuple-element.4, f32[256]{0:T(256)S(1)} %convert_element_type.3), kind=kOutput, calls=%fused_computation.4 | convolution fusion | flops 1615855616 | bytes 6423552 | tf_op jit(solution)/shard_map/dot_general | solution.py:23
  76.1 0.0 all-reduce.5.cloned.1.call-update
  76.1 0.2 all-reduce.3.cloned.1.call-start
  76.3 8.8 %fusion.1 = f32[4096,128]{0,1:T(8,128)} fusion(f32[256,128]{0,1:T(8,128)S(1)} %all_gather.7, f32[4096,256]{1,0:T(8,128)} %copy-done, f32[256]{0:T(256)S(1)} %convert_element_type.3), kind=kOutput, calls=%fused_computation.5 | convolution fusion | flops 1615855616 | bytes 6423552 | tf_op jit(solution)/shard_map/dot_general | solution.py:20
  85.1 0.0 all-reduce.3.cloned.1.call-update
  85.1 19.6 %psum.30 = f32[]{:T(128)} all-reduce(f32[]{:T(128)} %get-tuple-element.3), channel_id=1, replica_groups=mesh['star'=4,'cad'=8] {'cad'}, use_global_device_ids=true, to_apply=%region_3.0 | all-reduce | flops 1 | bytes 8 | tf_op jit(solution)/shard_map/psum | solution.py:28
  104.7 6.3 %psum.31 = f32[]{:T(128)} all-reduce(f32[]{:T(128)} %psum.30), channel_id=1, replica_groups=mesh['star'=4,'cad'=8] {'star'}, use_global_device_ids=true, to_apply=%region_4.0 | all-reduce | flops 1 | bytes 8 | tf_op jit(solution)/shard_map/psum | solution.py:29
  111.6 0.0 all-reduce.5.cloned.1.call-done
  111.7 1.4 negate_multiply_fusion.1
  113.0 99.1 %all-reduce.3.cloned.1.call-done = f32[4096,128]{0,1:T(8,128)} async-done(((f32[4096,128]{0,1:T(8,128)}), f32[4096,128]{0,1:T(8,128)}) %all-reduce.3.cloned.1.call-update) | async-done | bytes 2097168 | tf_op jit(solution)/shard_map/psum | solution.py:28
  212.1 1.7 negate_multiply_fusion
Async XLA Ops:
  7.2 55.0 %all-gather.2.cloned.1.call-start = ((), (), s32[]{:S(2)}) async-start(), calls=%async_computation | async-start | bytes 2359296 | tf_op jit(solution)/shard_map/all_gather | solution.py:10
  7.9 103.7 %all-reduce.5.cloned.1.call-start = ((), (), s32[]{:S(2)}) async-start(), calls=%async_computation.2 | async-start | bytes 262144 | tf_op jit(solution)/shard_map/psum | solution.py:29
  62.1 9.9 %copy-start.1 = (f32[4096,128]{0,1:T(8,128)S(1)}, f32[4096,128]{0,1:T(8,128)}, u32[]{:S(2)}) copy-start(f32[4096,128]{0,1:T(8,128)} %all-gather.2.cloned.1.call-done) | copy-start | bytes 6291460
  70.1 1.9 copy-start
  76.1 136.0 %all-reduce.3.cloned.1.call-start = ((), (), s32[]{:S(2)}) async-start(), calls=%async_computation.1 | async-start | bytes 4194304 | tf_op jit(solution)/shard_map/psum | solution.py:28
Sparse Core Ops, SparseCore 0:
  10.1 51.9 all-gather.1
  76.2 29.8 all-reduce.4
  110.2 101.8 all-reduce.2
where the time goes:
time: 222 us; the launch traced here: 221 us
  waiting for transfers between devices  146 us (66%)
  blocking collectives  32.5 us (15%)
  matrix products  20.8 us (9%)
  between operations  15.5 us (7%)
  other arithmetic  4.42 us (2%)
    psum x1, waiting for transfers between devices, on_device(): star_full, loss_cad = lax.psum((star_term, loss_part), 'cad')  99.1 us
    all_gather x1, waiting for transfers between devices, on_device(): star_loads = lax.all_gather(star_factors, 'cad', axis=1, tiled=True)  46.1 us
    psum x1, blocking collectives, on_device(): star_full, loss_cad = lax.psum((star_term, loss_part), 'cad')  19.6 us
    dot_general x1, matrix products, on_device(): jnp.dot(weighted, cad_loads, precision=lax.Precision.HIGHEST, preferred_e...  8.77 us
    dot_general x1, matrix products, on_device(): jnp.dot(star_loads, cad_loads.T, precision=lax.Precision.HIGHEST, preferr...  8 us
    all_gather x1, blocking collectives, on_device(): cad_loads = lax.all_gather(cadence_factors, 'star', axis=1, tiled=True)  6.71 us
    psum x1, blocking collectives, on_device(): cad_full, loss_all = lax.psum((cad_term, loss_cad), 'star')  6.27 us
  transfers between devices with their start and end apart: 3, of which 2 were waited for; matrix products, arithmetic and copies ran while one was open for 5% of the time, Pallas kernels for 0%

commit v1 on v0

v1 whole, which is shorter than its diff:
```python
import functools

import jax
import jax.numpy as jnp
from jax import lax
from jax.experimental import pallas as pl
from jax.experimental.pallas import tpu as pltpu
from jax.sharding import PartitionSpec as P

F32 = jnp.float32
BF16 = jnp.bfloat16


def two(x):
    hi = x.astype(BF16)
    return hi, (x - hi.astype(F32)).astype(BF16)


def three(x):
    hi = x.astype(BF16)
    rest = x - hi.astype(F32)
    mid = rest.astype(BF16)
    return hi, mid, (rest - mid.astype(F32)).astype(BF16)


def mm(a, b, ca, cb):
    return lax.dot_general(a, b, (((ca,), (cb,)), ((), ())), preferred_element_type=F32)


def body(scale, cad_scale, star_slots, cad_slots, n_star, n_cad, *refs):
    stars, cads = refs[:n_star], refs[n_star : n_star + n_cad]
    light, quality = refs[n_star + n_cad : n_star + n_cad + 2]
    outs = refs[n_star + n_cad + 2 :]
    star_out, cad_out, loss_out = outs[:n_star], outs[n_star : n_star + n_cad], outs[n_star + n_cad]
    whole, c3, cg, acc, lacc = outs[n_star + n_cad + 1 :]
    step = pl.program_id(0)
    rows = stars[0].shape[0]
    crows = cads[0].shape[0]
    rank = rows * n_star

    @pl.when(step == 0)
    def _():
        for k, ref in enumerate(cads):
            whole[pl.ds(pl.multiple_of(cad_slots(k) * crows, crows), crows), :] = ref[...]
        good = quality[...].astype(F32)
        for k in range(n_star):
            block = whole[pl.ds(pl.multiple_of(star_slots(k) * rows, rows), rows), :]
            hi, mid, lo = three(block)
            at = pl.ds(k * rows, rows)
            c3[0, at, :], c3[1, at, :], c3[2, at, :] = hi, mid, lo
            ghi, glo = two(block * (good * scale))
            cg[0, at, :], cg[1, at, :] = ghi, glo
        acc[...] = jnp.zeros_like(acc)
        lacc[...] = jnp.zeros_like(lacc)

    s = jnp.concatenate([r[...] for r in stars], 0)
    st = s.T
    hi, mid, lo = three(st)
    chi, cmid, clo = c3[0], c3[1], c3[2]
    right = jnp.concatenate([chi, cmid], 0)
    pred = (
        mm(jnp.concatenate([hi, lo], 1), jnp.concatenate([clo, chi], 0), 1, 0)
        + mm(jnp.concatenate([mid, mid], 1), right, 1, 0)
        + mm(jnp.concatenate([hi, hi], 1), right, 1, 0)
    )
    residual = light[...] - pred
    ratio = 1.0 + (residual * 0.5) ** 2
    weighted = residual / ratio
    whi, wlo = two(weighted)
    g = cg[...]
    both = mm(jnp.concatenate([g[0], g[1]], 0), whi, 1, 1)
    term = both[:rank] + both[rank:] + mm(g[0], wlo, 1, 1)
    for k, ref in enumerate(star_out):
        ref[...] = term[k * rows : (k + 1) * rows]
    shi, slo = two(s)
    both = mm(jnp.concatenate([shi, slo], 0), whi, 1, 0)
    acc[...] += both[:rank] + both[rank:] + mm(shi, wlo, 1, 0)
    n = ratio.shape[0] // 4
    prod = (ratio[:n] * ratio[n : 2 * n]) * (ratio[2 * n : 3 * n] * ratio[3 * n :])
    lacc[...] += jnp.sum(jnp.log(prod).reshape(n // 8, 8, -1), 0)

    @pl.when(step == pl.num_programs(0) - 1)
    def _():
        good = quality[...].astype(F32)
        for k in range(n_star):
            whole[pl.ds(pl.multiple_of(star_slots(k) * rows, rows), rows), :] = acc[k * rows : (k + 1) * rows]
        for k, ref in enumerate(cad_out):
            ref[...] = whole[pl.ds(pl.multiple_of(cad_slots(k) * crows, crows), crows), :] * (good * cad_scale)
        loss_out[...] = lacc[...] * good


def compute(pieces, cads, light, quality, scale, cad_scale, star_slots, cad_slots, chunk, chunks):
    rows, n = pieces[0].shape
    crows, nc = cads[0].shape
    rank = rows * len(pieces)
    bs = min(2048, n)
    first = chunk * (n // bs)
    const = lambda shape: pl.BlockSpec(shape, lambda i: (0, 0))
    piece = pl.BlockSpec((rows, bs), lambda i: (0, i))
    return pl.pallas_call(
        functools.partial(body, scale, cad_scale, star_slots, cad_slots, len(pieces), len(cads)),
        grid=(n // bs,),
        in_specs=[piece] * len(pieces) + [const((crows, nc))] * len(cads) + [pl.BlockSpec((bs, nc), lambda i: (first + i, 0)), const((1, nc))],
        out_specs=[piece] * len(pieces) + [const((crows, nc))] * len(cads) + [const((8, nc))],
        out_shape=[jax.ShapeDtypeStruct((rows, n), F32)] * len(pieces)
        + [jax.ShapeDtypeStruct((crows, nc), F32)] * len(cads) + [jax.ShapeDtypeStruct((8, nc), F32)],
        scratch_shapes=[pltpu.VMEM((rank, nc), F32), pltpu.VMEM((3, rank, nc), BF16), pltpu.VMEM((2, rank, nc), BF16),
                        pltpu.VMEM((rank, nc), F32), pltpu.VMEM((8, nc), F32)],
        compiler_params=pltpu.CompilerParams(vmem_limit_bytes=32 << 20),
    )(*pieces, *cads, light, quality)


CHUNKS = 1


def ring_order(n):
    return list(range(0, n, 2)) + list(range(1, n, 2))[::-1]


def shift(x, order, by):
    n = len(order)
    return lax.ppermute(x, "cad", [(order[p], order[(p + by) % n]) for p in range(n)])


def swap(x, axis, bit):
    return lax.ppermute(x, axis, [(i, i ^ bit) for i in range(lax.axis_size(axis))])


def ring_program(light, quality, star_t, cad_t):
    n, m = lax.axis_size("cad"), lax.axis_size("star")
    order = ring_order(n)
    stars = star_t.shape[1]
    width = stars // CHUNKS
    scale = -1.0 / float(light.shape[1] * n) ** 0.5
    cad_scale = -1.0 / float(stars * m) ** 0.5

    def star_slots(k):
        me = lax.axis_index("cad")
        place = jnp.where(me % 2 == 0, me // 2, n - 1 - me // 2)
        source = lax.rem(place + (n - k), n)
        return jnp.where(source < n // 2, 2 * source, 2 * (n - 1 - source) + 1)

    def cad_slots(k):
        return jnp.bitwise_xor(lax.axis_index("star"), k)

    with jax.named_scope("gather_cadence_factors"):
        cads = [cad_t]
        bit = 1
        while bit < m:
            got = swap(jnp.concatenate(cads, 0) if len(cads) > 1 else cads[0], "star", bit)
            cads = cads + [got[k * cad_t.shape[0] : (k + 1) * cad_t.shape[0]] for k in range(len(cads))]
            bit *= 2

    chunks = []
    for c in range(CHUNKS):
        own = star_t[:, c * width : (c + 1) * width]
        up = n // 2 if c % 2 == 0 else n // 2 - 1
        pieces = {0: own}
        with jax.named_scope("gather_star_factors"):
            for s in range(1, n // 2 + 1):
                if s <= up:
                    pieces[s] = shift(pieces[s - 1], order, 1)
                if s <= n - 1 - up:
                    pieces[n - s] = shift(pieces[(n - s + 1) % n], order, -1)
        chunks.append([pieces[k] for k in range(n)])

    stars_out, cads_out, loss_out = [], None, None
    for c in range(CHUNKS):
        up = n // 2 if c % 2 == 0 else n // 2 - 1
        got = compute(chunks[c], cads, light, quality.reshape(1, -1), scale, cad_scale, star_slots, cad_slots, c, CHUNKS)
        terms = got[:n]
        if cads_out is None:
            cads_out, loss_out = got[n : n + m], got[n + m]
        else:
            cads_out = [a + b for a, b in zip(cads_out, got[n : n + m])]
            loss_out = loss_out + got[n + m]
        with jax.named_scope("scatter_star_gradient"):
            upward = downward = None
            for s in range(n // 2, 0, -1):
                if s <= up:
                    mine = terms[n - s]
                    upward = shift(mine if upward is None else mine + upward, order, 1)
                if s <= n - 1 - up:
                    mine = terms[s]
                    downward = shift(mine if downward is None else mine + downward, order, -1)
            stars_out.append(terms[0] + upward + downward)

    with jax.named_scope("scatter_cadence_gradient"):
        bit = m // 2
        parts = list(cads_out)
        while bit:
            sent = swap(jnp.concatenate(parts[bit:] + [loss_out], 0), "star", bit)
            rows = cad_t.shape[0]
            parts = [parts[k] + sent[k * rows : (k + 1) * rows] for k in range(bit)]
            loss_out = loss_out + sent[bit * rows :]
            bit //= 2
        bit = 1
        while bit < n:
            loss_out = loss_out + swap(loss_out, "cad", bit)
            bit *= 2
    total = float(light.shape[0] * m) * float(light.shape[1] * n)
    loss = jnp.sum(loss_out) * (2.0 / total)
    star_gradient = stars_out[0] if CHUNKS == 1 else jnp.concatenate(stars_out, 1)
    return (star_gradient.T, parts[0].T, loss)


def whole_program(light, quality, star_t, cad_t):
    n, m = lax.axis_size("cad"), lax.axis_size("star")
    scale = -1.0 / float(light.shape[1] * n) ** 0.5
    cad_scale = -1.0 / float(light.shape[0] * m) ** 0.5
    stars = lax.all_gather(star_t, "cad", axis=0, tiled=True)
    cads = lax.all_gather(cad_t, "star", axis=0, tiled=True)
    first = lambda k: 0
    star, cad, loss = compute([stars], [cads], light, quality.reshape(1, -1), scale, cad_scale, first, first, 0, 1)
    star_gradient = lax.psum_scatter(star, "cad", scatter_dimension=0, tiled=True)
    cadence_gradient = lax.psum_scatter(cad, "star", scatter_dimension=0, tiled=True)
    total = float(light.shape[0] * m) * float(light.shape[1] * n)
    loss = lax.psum(jnp.sum(loss), ("star", "cad")) * (2.0 / total)
    return (star_gradient.T, cadence_gradient.T, loss)


def on_device(light, quality, star_factors, cadence_factors):
    n, m = lax.axis_size("cad"), lax.axis_size("star")
    ring = n % 2 == 0 and n & (n - 1) == 0 and m & (m - 1) == 0
    ring = ring and star_factors.shape[1] % 16 == 0 and cadence_factors.shape[1] % 16 == 0
    program = ring_program if ring else whole_program
    return program(light, quality, star_factors.T, cadence_factors.T)


def solution(mesh):
    in_specs = (P("star", "cad"), P("cad"), P("star", "cad"), P("cad", "star"))
    out_specs = (P("star", "cad"), P("cad", "star"), P())
    return jax.shard_map(
        on_device, mesh=mesh, in_specs=in_specs, out_specs=out_specs, check_vma=False
    )
```

time: 222 us -> 82 us (0.37)
  waiting for transfers between devices: 146 us -> 41.9 us
  blocking collectives: 32.5 us -> 0 us
  starting transfers between devices: 0.3 us -> 22 us
  matrix products: 20.8 us -> 0 us
  between operations: 15.5 us -> 2.49 us
  Pallas kernels: 0 us -> 7.69 us
  local copies, waits for them, and re-layouts: 1.93 us -> 4.58 us
    psum x2 -> x0, waiting for transfers between devices: 99.1 us -> none  [the longest x1 99.1 us: on_device(): star_full, loss_cad = lax.psum((star_term, loss_part), 'cad')]
    all_gather x1 -> x0, waiting for transfers between devices: 46.1 us -> none  [on_device(): star_loads = lax.all_gather(star_factors, 'cad', axis=1, tiled=True)]
    ppermute x0 -> x21, waiting for transfers between devices: none -> 41.9 us  [the longest x14 30.8 us: shift(): lax.ppermute(x, 'cad', [(order[p], order[(p + by) % n]) for p in range(n)])]
    psum x2 -> x0, blocking collectives: 25.8 us -> none  [the longest x1 19.6 us: on_device(): star_full, loss_cad = lax.psum((star_term, loss_part), 'cad')]
    ppermute x0 -> x21, starting transfers between devices: none -> 22 us  [the longest x14 16.9 us: shift(): lax.ppermute(x, 'cad', [(order[p], order[(p + by) % n]) for p in range(n)])]
    dot_general x3 -> x0, matrix products: 20.8 us -> none  [the longest x1 8.77 us: on_device(): jnp.dot(weighted, cad_loads, precision=lax.Precision.HIGHEST, preferred_e...]
    pallas_call x0 -> x1, Pallas kernels: none -> 7.69 us  [compute(): pl.pallas_call(functools.partial(body, scale, cad_scale, star_slots, cad_...]
    all_gather x1 -> x0, blocking collectives: 6.71 us -> none  [on_device(): cad_loads = lax.all_gather(cadence_factors, 'star', axis=1, tiled=True)]
  transfers between devices with their start and end apart: 3 -> 21, of which waited for: 2 -> 14; matrix products, arithmetic and copies ran while one was open for 5% -> 3% of each run, Pallas kernels for 0% -> 0%
where the time goes in v1:
time: 82 us; the launch traced here: 81.6 us
  waiting for transfers between devices  41.9 us (51%)
  starting transfers between devices  22 us (27%)
  Pallas kernels  7.69 us (9%)
  local copies, waits for them, and re-layouts  4.58 us (6%)
  other arithmetic  2.91 us (4%)
  between operations  2.49 us (3%)
    ppermute x14, waiting for transfers between devices, shift(): lax.ppermute(x, 'cad', [(order[p], order[(p + by) % n]) for p in range(n)])  30.8 us
    ppermute x14, starting transfers between devices, shift(): lax.ppermute(x, 'cad', [(order[p], order[(p + by) % n]) for p in range(n)])  16.9 us
    ppermute x7, waiting for transfers between devices, swap(): lax.ppermute(x, axis, [(i, i ^ bit) for i in range(lax.axis_size(axis))])  11.1 us
    pallas_call x1, Pallas kernels, compute(): pl.pallas_call(functools.partial(body, scale, cad_scale, star_slots, cad_...  7.69 us
    ppermute x7, starting transfers between devices, swap(): lax.ppermute(x, axis, [(i, i ^ bit) for i in range(lax.axis_size(axis))])  5.11 us
    unnamed x8, local copies, waits for them, and re-layouts  4.57 us
  transfers between devices with their start and end apart: 21, of which 14 were waited for; matrix products, arithmetic and copies ran while one was open for 3% of the time, Pallas kernels for 0%

profile of v1, /device:TPU:0, one launch (start us, length us, event | category | flops | bytes accessed | tf_op | source)
XLA Modules:
  0.0 81.6 jit_solution(9427663263172988441)
XLA Ops:
  0.6 3.1 %collective-permute-start = (f32[16,4096]{1,0:T(8,128)}, f32[16,4096]{1,0:T(8,128)S(1)}, u32[]{:S(2)}, u32[]{:S(2)}) collective-permute-start(f32[16,4096]{1,0:T(8,128)} %bitcast.7), channel_id=1, source_target_pairs={{0,2},{2,4},{4,6},{6,7},{7,5},{5,3},{3,1},{1,0},{8,10},{10,12},{12... | collective-permute-start | bytes 786440 | tf_op jit(solution)/shard_map/gather_star_factors/ppermute | solution.py:122
  3.7 0.0 collective-permute-start.4
  3.7 6.4 %collective-permute-done.refs_1_ = f32[16,4096]{1,0:T(8,128)S(1)} collective-permute-done((f32[16,4096]{1,0:T(8,128)}, f32[16,4096]{1,0:T(8,128)S(1)}, u32[]{:S(2)}, u32[]{:S(2)}) %collective-permute-start) | collective-permute-done | bytes 262176 | tf_op jit(solution)/shard_map/gather_star_factors/ppermute | solution.py:122
  10.1 1.8 %collective-permute-start.1 = (f32[16,4096]{1,0:T(8,128)S(1)}, f32[16,4096]{1,0:T(8,128)S(1)}, u32[]{:S(2)}, u32[]{:S(2)}) collective-permute-start(f32[16,4096]{1,0:T(8,128)S(1)} %collective-permute-done.refs_1_), channel_id=1, source_target_pairs={{0,2},{2,4},{4,6},{6,7},{7,5},{5,3},{3,1},{1,0},{8,10},{10,12},{12... | collective-permute-start | bytes 786440 | tf_op jit(solution)/shard_map/gather_star_factors/ppermute | solution.py:122
  12.0 0.0 collective-permute-done.4.refs_7_
  12.0 0.2 collective-permute-start.5
  12.2 5.5 %collective-permute-done.1.refs_2_ = f32[16,4096]{1,0:T(8,128)S(1)} collective-permute-done((f32[16,4096]{1,0:T(8,128)S(1)}, f32[16,4096]{1,0:T(8,128)S(1)}, u32[]{:S(2)}, u32[]{:S(2)}) %collective-permute-start.1) | collective-permute-done | bytes 262176 | tf_op jit(solution)/shard_map/gather_star_factors/ppermute | solution.py:122
  17.6 1.5 %collective-permute-start.2 = (f32[16,4096]{1,0:T(8,128)S(1)}, f32[16,4096]{1,0:T(8,128)S(1)}, u32[]{:S(2)}, u32[]{:S(2)}) collective-permute-start(f32[16,4096]{1,0:T(8,128)S(1)} %collective-permute-done.1.refs_2_), channel_id=1, source_target_pairs={{0,2},{2,4},{4,6},{6,7},{7,5},{5,3},{3,1},{1,0},{8,10},{10,12},{12... | collective-permute-start | bytes 786440 | tf_op jit(solution)/shard_map/gather_star_factors/ppermute | solution.py:122
  19.1 0.0 collective-permute-start.7
  19.1 1.4 %collective-permute-done.7.refs_9_ = f32[32,256]{1,0:T(8,128)S(1)} collective-permute-done((f32[32,256]{1,0:T(8,128)}, f32[32,256]{1,0:T(8,128)S(1)}, u32[]{:S(2)}, u32[]{:S(2)}) %collective-permute-start.7) | collective-permute-done | bytes 32800 | tf_op jit(solution)/shard_map/gather_cadence_factors/ppermute | solution.py:126
  20.6 0.8 pad_maximum_fusion.1
  21.3 1.5 %collective-permute-start.8 = (f32[64,256]{1,0:T(8,128)S(1)}, f32[64,256]{1,0:T(8,128)S(1)}, u32[]{:S(2)}, u32[]{:S(2)}) collective-permute-start(f32[64,256]{1,0:T(8,128)S(1)} %pad_maximum_fusion.1), channel_id=1, source_target_pairs={{0,16},{8,24},{16,0},{24,8},{1,17},{9,25},{17,1},{25,9},{2,18},{10... | collective-permute-start | bytes 196616 | tf_op jit(solution)/shard_map/gather_cadence_factors/ppermute | solution.py:126
  22.8 0.0 collective-permute-done.5.refs_6_
  22.8 0.5 collective-permute-start.6
  23.3 0.9 %collective-permute-done.2.refs_3_ = f32[16,4096]{1,0:T(8,128)S(1)} collective-permute-done((f32[16,4096]{1,0:T(8,128)S(1)}, f32[16,4096]{1,0:T(8,128)S(1)}, u32[]{:S(2)}, u32[]{:S(2)}) %collective-permute-start.2) | collective-permute-done | bytes 262176 | tf_op jit(solution)/shard_map/gather_star_factors/ppermute | solution.py:122
  24.2 1.3 %collective-permute-start.3 = (f32[16,4096]{1,0:T(8,128)S(1)}, f32[16,4096]{1,0:T(8,128)S(1)}, u32[]{:S(2)}, u32[]{:S(2)}) collective-permute-start(f32[16,4096]{1,0:T(8,128)S(1)} %collective-permute-done.2.refs_3_), channel_id=1, source_target_pairs={{0,2},{2,4},{4,6},{6,7},{7,5},{5,3},{3,1},{1,0},{8,10},{10,12},{12... | collective-permute-start | bytes 786440 | tf_op jit(solution)/shard_map/gather_star_factors/ppermute | solution.py:122
  25.5 0.1 collective-permute-done.8
  25.6 5.3 %collective-permute-done.6.refs_5_ = f32[16,4096]{1,0:T(8,128)S(1)} collective-permute-done((f32[16,4096]{1,0:T(8,128)S(1)}, f32[16,4096]{1,0:T(8,128)S(1)}, u32[]{:S(2)}, u32[]{:S(2)}) %collective-permute-start.6) | collective-permute-done | bytes 262176 | tf_op jit(solution)/shard_map/gather_star_factors/ppermute | solution.py:122
  30.9 0.2 collective-permute-done.3.refs_4_
  31.1 2.2 %copy-done = f32[4096,256]{1,0:T(8,128)S(1)} copy-done((f32[4096,256]{1,0:T(8,128)S(1)}, f32[4096,256]{1,0:T(8,128)}, u32[]{:S(2)}) %copy-start) | copy-done | bytes 4194328
  33.3 0.9 %copy-done.1 = f32[4096,16]{0,1:T(8,128)S(1)} copy-done((f32[4096,16]{0,1:T(8,128)S(1)}, f32[4096,16]{0,1:T(8,128)}, u32[]{:S(2)}) %copy-start.1) | copy-done | bytes 262168
  34.3 0.8 copy-done.2
  35.0 0.7 copy-done.3
  35.7 7.7 %shard_map.67 = (f32[16,4096]{1,0:T(8,128)S(1)}, f32[16,4096]{1,0:T(8,128)S(1)}, f32[16,4096]{1,0:T(8,128)S(1)}, f32[16,4096]{1,0:T(8,128)S(1)}, f32[16,4096]{1,...) custom-call(f32[16,4096]{1,0:T(8,128)S(1)} %bitcast.9, ...), custom_call_target="tpu_custom_call" | custom-call | tf_op jit(solution)/shard_map/pallas_call | solution.py:100
  43.4 0.8 collective-permute-start.16
  44.2 1.6 %collective-permute-start.9 = (f32[16,4096]{1,0:T(8,128)S(1)}, f32[16,4096]{1,0:T(8,128)S(1)}, u32[]{:S(2)}, u32[]{:S(2)}) collective-permute-start(f32[16,4096]{1,0:T(8,128)S(1)} %get-tuple-element.20), channel_id=1, source_target_pairs={{0,2},{2,4},{4,6},{6,7},{7,5},{5,3},{3,1},{1,0},{8,10},{10,12},{12... | collective-permute-start | bytes 786440 | tf_op jit(solution)/shard_map/scatter_star_gradient/ppermute | solution.py:122
  45.8 0.4 collective-permute-start.13
  46.2 1.6 %collective-permute-done.16 = f32[72,256]{1,0:T(8,128)S(1)} collective-permute-done((f32[72,256]{1,0:T(8,128)S(1)}, f32[72,256]{1,0:T(8,128)S(1)}, u32[]{:S(2)}, u32[]{:S(2)}) %collective-permute-start.16) | collective-permute-done | bytes 73760 | tf_op jit(solution)/shard_map/scatter_cadence_gradient/ppermute | solution.py:126
  47.8 2.9 %collective-permute-done.9 = f32[16,4096]{1,0:T(8,128)S(1)} collective-permute-done((f32[16,4096]{1,0:T(8,128)S(1)}, f32[16,4096]{1,0:T(8,128)S(1)}, u32[]{:S(2)}, u32[]{:S(2)}) %collective-permute-start.9) | collective-permute-done | bytes 262176 | tf_op jit(solution)/shard_map/scatter_star_gradient/ppermute | solution.py:122
  50.8 1.6 %collective-permute-start.10 = (f32[16,4096]{1,0:T(8,128)S(1)}, f32[16,4096]{1,0:T(8,128)S(1)}, u32[]{:S(2)}, u32[]{:S(2)}) collective-permute-start(f32[16,4096]{1,0:T(8,128)S(1)} %add.45), channel_id=1, source_target_pairs={{0,2},{2,4},{4,6},{6,7},{7,5},{5,3},{3,1},{1,0},{8,10},{10,12},{12... | collective-permute-start | bytes 786440 | tf_op jit(solution)/shard_map/scatter_star_gradient/ppermute | solution.py:122
  52.4 0.0 collective-permute-start.17
  52.5 0.9 %collective-permute-start.14 = (f32[16,4096]{1,0:T(8,128)S(1)}, f32[16,4096]{1,0:T(8,128)S(1)}, u32[]{:S(2)}, u32[]{:S(2)}) collective-permute-start(f32[16,4096]{1,0:T(8,128)S(1)} %add.49), channel_id=1, source_target_pairs={{0,1},{2,0},{4,2},{6,4},{7,6},{5,7},{3,5},{1,3},{8,9},{10,8},{12,1... | collective-permute-start | bytes 786440 | tf_op jit(solution)/shard_map/scatter_star_gradient/ppermute | solution.py:122
  53.4 5.1 %collective-permute-done.10 = f32[16,4096]{1,0:T(8,128)S(1)} collective-permute-done((f32[16,4096]{1,0:T(8,128)S(1)}, f32[16,4096]{1,0:T(8,128)S(1)}, u32[]{:S(2)}, u32[]{:S(2)}) %collective-permute-start.10) | collective-permute-done | bytes 262176 | tf_op jit(solution)/shard_map/scatter_star_gradient/ppermute | solution.py:122
  58.5 1.3 %collective-permute-start.11 = (f32[16,4096]{1,0:T(8,128)S(1)}, f32[16,4096]{1,0:T(8,128)S(1)}, u32[]{:S(2)}, u32[]{:S(2)}) collective-permute-start(f32[16,4096]{1,0:T(8,128)S(1)} %add.46), channel_id=1, source_target_pairs={{0,2},{2,4},{4,6},{6,7},{7,5},{5,3},{3,1},{1,0},{8,10},{10,12},{12... | collective-permute-start | bytes 786440 | tf_op jit(solution)/shard_map/scatter_star_gradient/ppermute | solution.py:122
  59.8 0.0 collective-permute-done.17
  59.9 1.1 %collective-permute-start.18 = (f32[8,256]{1,0:T(8,128)S(1)}, f32[8,256]{1,0:T(8,128)S(1)}, u32[]{:S(2)}, u32[]{:S(2)}) collective-permute-start(f32[8,256]{1,0:T(8,128)S(1)} %slice_add_fusion.3), channel_id=1, source_target_pairs={{0,1},{1,0},{2,3},{3,2},{4,5},{5,4},{6,7},{7,6},{8,9},{9,8},{10,11... | collective-permute-start | bytes 24584 | tf_op jit(solution)/shard_map/scatter_cadence_gradient/ppermute | solution.py:126
  61.0 4.3 %collective-permute-done.18 = f32[8,256]{1,0:T(8,128)S(1)} collective-permute-done((f32[8,256]{1,0:T(8,128)S(1)}, f32[8,256]{1,0:T(8,128)S(1)}, u32[]{:S(2)}, u32[]{:S(2)}) %collective-permute-start.18) | collective-permute-done | bytes 8224 | tf_op jit(solution)/shard_map/scatter_cadence_gradient/ppermute | solution.py:126
  65.3 0.0 collective-permute-start.19
  65.3 3.6 %collective-permute-done.19 = f32[8,256]{1,0:T(8,128)S(1)} collective-permute-done((f32[8,256]{1,0:T(8,128)S(1)}, f32[8,256]{1,0:T(8,128)S(1)}, u32[]{:S(2)}, u32[]{:S(2)}) %collective-permute-start.19) | collective-permute-done | bytes 8224 | tf_op jit(solution)/shard_map/scatter_cadence_gradient/ppermute | solution.py:126
  69.0 1.7 %collective-permute-start.20 = (f32[8,256]{1,0:T(8,128)S(1)}, f32[8,256]{1,0:T(8,128)S(1)}, u32[]{:S(2)}, u32[]{:S(2)}) collective-permute-start(f32[8,256]{1,0:T(8,128)S(1)} %add.58), channel_id=1, source_target_pairs={{0,4},{1,5},{2,6},{3,7},{4,0},{5,1},{6,2},{7,3},{8,12},{9,13},{10,... | collective-permute-start | bytes 24584 | tf_op jit(solution)/shard_map/scatter_cadence_gradient/ppermute | solution.py:126
  70.7 2.6 %collective-permute-start.15 = (f32[16,4096]{1,0:T(8,128)S(1)}, f32[16,4096]{1,0:T(8,128)S(1)}, u32[]{:S(2)}, u32[]{:S(2)}) collective-permute-start(f32[16,4096]{1,0:T(8,128)S(1)} %add.50), channel_id=1, source_target_pairs={{0,1},{2,0},{4,2},{6,4},{7,6},{5,7},{3,5},{1,3},{8,9},{10,8},{12,1... | collective-permute-start | bytes 786440 | tf_op jit(solution)/shard_map/scatter_star_gradient/ppermute | solution.py:122
  73.3 0.1 collective-permute-start.12
  73.4 0.6 fusion
  74.0 0.0 collective-permute-done.20
  74.0 0.6 add_reduce_fusion
  75.3 1.9 %collective-permute-done.15 = f32[16,4096]{1,0:T(8,128)S(1)} collective-permute-done((f32[16,4096]{1,0:T(8,128)S(1)}, f32[16,4096]{1,0:T(8,128)S(1)}, u32[]{:S(2)}, u32[]{:S(2)}) %collective-permute-start.15) | collective-permute-done | bytes 262176 | tf_op jit(solution)/shard_map/scatter_star_gradient/ppermute | solution.py:122
  77.2 2.6 %collective-permute-done.12 = f32[16,4096]{1,0:T(8,128)S(1)} collective-permute-done((f32[16,4096]{1,0:T(8,128)S(1)}, f32[16,4096]{1,0:T(8,128)S(1)}, u32[]{:S(2)}, u32[]{:S(2)}) %collective-permute-start.12) | collective-permute-done | bytes 262176 | tf_op jit(solution)/shard_map/scatter_star_gradient/ppermute | solution.py:122
  79.7 0.7 add_bitcast_fusion
  (20 shorter events, 0.2 us)
Async XLA Ops:
  0.6 9.5 %collective-permute-start = (f32[16,4096]{1,0:T(8,128)}, f32[16,4096]{1,0:T(8,128)S(1)}, u32[]{:S(2)}, u32[]{:S(2)}) collective-permute-start(f32[16,4096]{1,0:T(8,128)} %bitcast.7), channel_id=1, source_target_pairs={{0,2},{2,4},{4,6},{6,7},{7,5},{5,3},{3,1},{1,0},{8,10},{10,12},{12... | collective-permute-start | bytes 786440 | tf_op jit(solution)/shard_map/gather_star_factors/ppermute | solution.py:122
  3.7 8.3 %collective-permute-start.4 = (f32[16,4096]{1,0:T(8,128)}, f32[16,4096]{1,0:T(8,128)S(1)}, u32[]{:S(2)}, u32[]{:S(2)}) collective-permute-start(f32[16,4096]{1,0:T(8,128)} %bitcast.8), channel_id=1, source_target_pairs={{0,1},{2,0},{4,2},{6,4},{7,6},{5,7},{3,5},{1,3},{8,9},{10,8},{12,1... | collective-permute-start | bytes 786440 | tf_op jit(solution)/shard_map/gather_star_factors/ppermute | solution.py:122
  10.1 7.5 %collective-permute-start.1 = (f32[16,4096]{1,0:T(8,128)S(1)}, f32[16,4096]{1,0:T(8,128)S(1)}, u32[]{:S(2)}, u32[]{:S(2)}) collective-permute-start(f32[16,4096]{1,0:T(8,128)S(1)} %collective-permute-done.refs_1_), channel_id=1, source_target_pairs={{0,2},{2,4},{4,6},{6,7},{7,5},{5,3},{3,1},{1,0},{8,10},{10,12},{12... | collective-permute-start | bytes 786440 | tf_op jit(solution)/shard_map/gather_star_factors/ppermute | solution.py:122
  12.0 10.9 %collective-permute-start.5 = (f32[16,4096]{1,0:T(8,128)S(1)}, f32[16,4096]{1,0:T(8,128)S(1)}, u32[]{:S(2)}, u32[]{:S(2)}) collective-permute-start(f32[16,4096]{1,0:T(8,128)S(1)} %collective-permute-done.4.refs_7_), channel_id=1, source_target_pairs={{0,1},{2,0},{4,2},{6,4},{7,6},{5,7},{3,5},{1,3},{8,9},{10,8},{12,1... | collective-permute-start | bytes 786440 | tf_op jit(solution)/shard_map/gather_star_factors/ppermute | solution.py:122
  17.6 6.6 %collective-permute-start.2 = (f32[16,4096]{1,0:T(8,128)S(1)}, f32[16,4096]{1,0:T(8,128)S(1)}, u32[]{:S(2)}, u32[]{:S(2)}) collective-permute-start(f32[16,4096]{1,0:T(8,128)S(1)} %collective-permute-done.1.refs_2_), channel_id=1, source_target_pairs={{0,2},{2,4},{4,6},{6,7},{7,5},{5,3},{3,1},{1,0},{8,10},{10,12},{12... | collective-permute-start | bytes 786440 | tf_op jit(solution)/shard_map/gather_star_factors/ppermute | solution.py:122
  19.1 1.4 %collective-permute-start.7 = (f32[32,256]{1,0:T(8,128)}, f32[32,256]{1,0:T(8,128)S(1)}, u32[]{:S(2)}, u32[]{:S(2)}) collective-permute-start(f32[32,256]{1,0:T(8,128)} %bitcast.10), channel_id=1, source_target_pairs={{0,8},{8,0},{16,24},{24,16},{1,9},{9,1},{17,25},{25,17},{2,10},{10... | collective-permute-start | bytes 98312 | tf_op jit(solution)/shard_map/gather_cadence_factors/ppermute | solution.py:126
  21.3 4.3 %collective-permute-start.8 = (f32[64,256]{1,0:T(8,128)S(1)}, f32[64,256]{1,0:T(8,128)S(1)}, u32[]{:S(2)}, u32[]{:S(2)}) collective-permute-start(f32[64,256]{1,0:T(8,128)S(1)} %pad_maximum_fusion.1), channel_id=1, source_target_pairs={{0,16},{8,24},{16,0},{24,8},{1,17},{9,25},{17,1},{25,9},{2,18},{10... | collective-permute-start | bytes 196616 | tf_op jit(solution)/shard_map/gather_cadence_factors/ppermute | solution.py:126
  22.8 8.1 %collective-permute-start.6 = (f32[16,4096]{1,0:T(8,128)S(1)}, f32[16,4096]{1,0:T(8,128)S(1)}, u32[]{:S(2)}, u32[]{:S(2)}) collective-permute-start(f32[16,4096]{1,0:T(8,128)S(1)} %collective-permute-done.5.refs_6_), channel_id=1, source_target_pairs={{0,1},{2,0},{4,2},{6,4},{7,6},{5,7},{3,5},{1,3},{8,9},{10,8},{12,1... | collective-permute-start | bytes 786440 | tf_op jit(solution)/shard_map/gather_star_factors/ppermute | solution.py:122
  24.2 6.9 %collective-permute-start.3 = (f32[16,4096]{1,0:T(8,128)S(1)}, f32[16,4096]{1,0:T(8,128)S(1)}, u32[]{:S(2)}, u32[]{:S(2)}) collective-permute-start(f32[16,4096]{1,0:T(8,128)S(1)} %collective-permute-done.2.refs_3_), channel_id=1, source_target_pairs={{0,2},{2,4},{4,6},{6,7},{7,5},{5,3},{3,1},{1,0},{8,10},{10,12},{12... | collective-permute-start | bytes 786440 | tf_op jit(solution)/shard_map/gather_star_factors/ppermute | solution.py:122
  31.1 2.2 %copy-start = (f32[4096,256]{1,0:T(8,128)S(1)}, f32[4096,256]{1,0:T(8,128)}, u32[]{:S(2)}) copy-start(f32[4096,256]{1,0:T(8,128)} %refs_12_.1) | copy-start | bytes 12582916
  33.3 0.9 %copy-start.1 = (f32[4096,16]{0,1:T(8,128)S(1)}, f32[4096,16]{0,1:T(8,128)}, u32[]{:S(2)}) copy-start(f32[4096,16]{0,1:T(8,128)} %param.6) | copy-start | bytes 786436
  34.2 0.8 copy-start.2
  35.0 0.7 copy-start.3
  43.4 4.4 %collective-permute-start.16 = (f32[72,256]{1,0:T(8,128)S(1)}, f32[72,256]{1,0:T(8,128)S(1)}, u32[]{:S(2)}, u32[]{:S(2)}) collective-permute-start(f32[72,256]{1,0:T(8,128)S(1)} %pad_maximum_fusion), channel_id=1, source_target_pairs={{0,16},{8,24},{16,0},{24,8},{1,17},{9,25},{17,1},{25,9},{2,18},{10... | collective-permute-start | bytes 221192 | tf_op jit(solution)/shard_map/scatter_cadence_gradient/ppermute | solution.py:126
  44.2 6.6 %collective-permute-start.9 = (f32[16,4096]{1,0:T(8,128)S(1)}, f32[16,4096]{1,0:T(8,128)S(1)}, u32[]{:S(2)}, u32[]{:S(2)}) collective-permute-start(f32[16,4096]{1,0:T(8,128)S(1)} %get-tuple-element.20), channel_id=1, source_target_pairs={{0,2},{2,4},{4,6},{6,7},{7,5},{5,3},{3,1},{1,0},{8,10},{10,12},{12... | collective-permute-start | bytes 786440 | tf_op jit(solution)/shard_map/scatter_star_gradient/ppermute | solution.py:122
  45.8 6.7 %collective-permute-start.13 = (f32[16,4096]{1,0:T(8,128)S(1)}, f32[16,4096]{1,0:T(8,128)S(1)}, u32[]{:S(2)}, u32[]{:S(2)}) collective-permute-start(f32[16,4096]{1,0:T(8,128)S(1)} %get-tuple-element.23), channel_id=1, source_target_pairs={{0,1},{2,0},{4,2},{6,4},{7,6},{5,7},{3,5},{1,3},{8,9},{10,8},{12,1... | collective-permute-start | bytes 786440 | tf_op jit(solution)/shard_map/scatter_star_gradient/ppermute | solution.py:122
  50.8 7.7 %collective-permute-start.10 = (f32[16,4096]{1,0:T(8,128)S(1)}, f32[16,4096]{1,0:T(8,128)S(1)}, u32[]{:S(2)}, u32[]{:S(2)}) collective-permute-start(f32[16,4096]{1,0:T(8,128)S(1)} %add.45), channel_id=1, source_target_pairs={{0,2},{2,4},{4,6},{6,7},{7,5},{5,3},{3,1},{1,0},{8,10},{10,12},{12... | collective-permute-start | bytes 786440 | tf_op jit(solution)/shard_map/scatter_star_gradient/ppermute | solution.py:122
  52.4 7.4 %collective-permute-start.17 = (f32[40,256]{1,0:T(8,128)S(1)}, f32[40,256]{1,0:T(8,128)S(1)}, u32[]{:S(2)}, u32[]{:S(2)}) collective-permute-start(f32[40,256]{1,0:T(8,128)S(1)} %pad_maximum_fusion.2), channel_id=1, source_target_pairs={{0,8},{8,0},{16,24},{24,16},{1,9},{9,1},{17,25},{25,17},{2,10},{10... | collective-permute-start | bytes 122888 | tf_op jit(solution)/shard_map/scatter_cadence_gradient/ppermute | solution.py:126
  52.5 18.2 %collective-permute-start.14 = (f32[16,4096]{1,0:T(8,128)S(1)}, f32[16,4096]{1,0:T(8,128)S(1)}, u32[]{:S(2)}, u32[]{:S(2)}) collective-permute-start(f32[16,4096]{1,0:T(8,128)S(1)} %add.49), channel_id=1, source_target_pairs={{0,1},{2,0},{4,2},{6,4},{7,6},{5,7},{3,5},{1,3},{8,9},{10,8},{12,1... | collective-permute-start | bytes 786440 | tf_op jit(solution)/shard_map/scatter_star_gradient/ppermute | solution.py:122
  58.5 14.8 %collective-permute-start.11 = (f32[16,4096]{1,0:T(8,128)S(1)}, f32[16,4096]{1,0:T(8,128)S(1)}, u32[]{:S(2)}, u32[]{:S(2)}) collective-permute-start(f32[16,4096]{1,0:T(8,128)S(1)} %add.46), channel_id=1, source_target_pairs={{0,2},{2,4},{4,6},{6,7},{7,5},{5,3},{3,1},{1,0},{8,10},{10,12},{12... | collective-permute-start | bytes 786440 | tf_op jit(solution)/shard_map/scatter_star_gradient/ppermute | solution.py:122
  59.9 5.4 %collective-permute-start.18 = (f32[8,256]{1,0:T(8,128)S(1)}, f32[8,256]{1,0:T(8,128)S(1)}, u32[]{:S(2)}, u32[]{:S(2)}) collective-permute-start(f32[8,256]{1,0:T(8,128)S(1)} %slice_add_fusion.3), channel_id=1, source_target_pairs={{0,1},{1,0},{2,3},{3,2},{4,5},{5,4},{6,7},{7,6},{8,9},{9,8},{10,11... | collective-permute-start | bytes 24584 | tf_op jit(solution)/shard_map/scatter_cadence_gradient/ppermute | solution.py:126
  65.3 3.7 %collective-permute-start.19 = (f32[8,256]{1,0:T(8,128)S(1)}, f32[8,256]{1,0:T(8,128)S(1)}, u32[]{:S(2)}, u32[]{:S(2)}) collective-permute-start(f32[8,256]{1,0:T(8,128)S(1)} %add.57), channel_id=1, source_target_pairs={{0,2},{1,3},{2,0},{3,1},{4,6},{5,7},{6,4},{7,5},{8,10},{9,11},{10,... | collective-permute-start | bytes 24584 | tf_op jit(solution)/shard_map/scatter_cadence_gradient/ppermute | solution.py:126
  69.0 5.1 %collective-permute-start.20 = (f32[8,256]{1,0:T(8,128)S(1)}, f32[8,256]{1,0:T(8,128)S(1)}, u32[]{:S(2)}, u32[]{:S(2)}) collective-permute-start(f32[8,256]{1,0:T(8,128)S(1)} %add.58), channel_id=1, source_target_pairs={{0,4},{1,5},{2,6},{3,7},{4,0},{5,1},{6,2},{7,3},{8,12},{9,13},{10,... | collective-permute-start | bytes 24584 | tf_op jit(solution)/shard_map/scatter_cadence_gradient/ppermute | solution.py:126
  70.7 6.5 %collective-permute-start.15 = (f32[16,4096]{1,0:T(8,128)S(1)}, f32[16,4096]{1,0:T(8,128)S(1)}, u32[]{:S(2)}, u32[]{:S(2)}) collective-permute-start(f32[16,4096]{1,0:T(8,128)S(1)} %add.50), channel_id=1, source_target_pairs={{0,1},{2,0},{4,2},{6,4},{7,6},{5,7},{3,5},{1,3},{8,9},{10,8},{12,1... | collective-permute-start | bytes 786440 | tf_op jit(solution)/shard_map/scatter_star_gradient/ppermute | solution.py:122
  73.3 6.4 %collective-permute-start.12 = (f32[16,4096]{1,0:T(8,128)S(1)}, f32[16,4096]{1,0:T(8,128)S(1)}, u32[]{:S(2)}, u32[]{:S(2)}) collective-permute-start(f32[16,4096]{1,0:T(8,128)S(1)} %add.47), channel_id=1, source_target_pairs={{0,2},{2,4},{4,6},{6,7},{7,5},{5,3},{3,1},{1,0},{8,10},{10,12},{12... | collective-permute-start | bytes 786440 | tf_op jit(solution)/shard_map/scatter_star_gradient/ppermute | solution.py:122

commit v2 on v0

v2 whole, which is shorter than its diff:
```python
import functools

import jax
import jax.numpy as jnp
from jax import lax
from jax.experimental import pallas as pl
from jax.experimental.pallas import tpu as pltpu
from jax.sharding import PartitionSpec as P

F32 = jnp.float32
BF16 = jnp.bfloat16
SUB = 512


def two(x):
    hi = x.astype(BF16)
    return hi, (x - hi.astype(F32)).astype(BF16)


def three(x):
    hi = x.astype(BF16)
    rest = x - hi.astype(F32)
    mid = rest.astype(BF16)
    return hi, mid, (rest - mid.astype(F32)).astype(BF16)


def mm(a, b, ca, cb):
    return lax.dot_general(a, b, (((ca,), (cb,)), ((), ())), preferred_element_type=F32)


def rank_rows(k, rows):
    return pl.ds(pl.multiple_of(k * rows, rows), rows)


def stage_body(light_in, quality_in, cad_in, light, quality, cad, sem):
    copies = [
        pltpu.make_async_copy(cad_in, cad, sem.at[0]),
        pltpu.make_async_copy(quality_in, quality, sem.at[1]),
        pltpu.make_async_copy(light_in, light, sem.at[2]),
    ]
    for copy in copies:
        copy.start()
    for copy in copies:
        copy.wait()


def stage(light, quality, cad_t):
    given = (light, quality, cad_t)
    return pl.pallas_call(
        stage_body,
        in_specs=[pl.BlockSpec(memory_space=pl.ANY)] * 3,
        out_specs=[pl.BlockSpec(memory_space=pltpu.VMEM)] * 3,
        out_shape=[jax.ShapeDtypeStruct(x.shape, x.dtype) for x in given],
        scratch_shapes=[pltpu.SemaphoreType.DMA((3,))],
        cost_estimate=pl.CostEstimate(flops=0, bytes_accessed=1 << 10, transcendentals=0),
        compiler_params=pltpu.CompilerParams(vmem_limit_bytes=16 << 20),
    )(*given)


def body(plan, *refs):
    scale, cad_scale, star_slot, cad_slot, n_star, n_cad, offset, first, last = plan
    refs = list(refs)
    take = lambda count: [refs.pop(0) for _ in range(count)]
    light, quality = take(2)
    stars, cads = take(n_star), take(n_cad)
    before = [] if first else take(2)
    halves = [] if first else take(n_star)
    star_out = take(n_star)
    ends = take(3) if last else take(2)
    whole, c3, cg, acc, lacc = refs
    rows, width = stars[0].shape[0], light.shape[0] // (1 if first and last else 2)
    crows = cads[0].shape[0]
    rank = rows * n_star
    sub = min(SUB, width)

    good = quality[...].astype(F32)
    for k, ref in enumerate(cads):
        whole[rank_rows(cad_slot(k), crows), :] = ref[...]
    for k in range(n_star):
        block = whole[rank_rows(star_slot(k), rows), :]
        at = pl.ds(k * rows, rows)
        c3[0, at, :], c3[1, at, :], c3[2, at, :] = three(block)
        cg[at, :], cg[pl.ds(rank + k * rows, rows), :] = two(block * (good * scale))
    if first:
        acc[...] = jnp.zeros_like(acc)
        lacc[...] = jnp.zeros_like(lacc)
    else:
        acc[...] = before[0][...]
        lacc[...] = before[1][...]

    chi, cmid, clo = c3[0], c3[1], c3[2]
    upper = jnp.concatenate([chi, cmid], 0)
    crossed = jnp.concatenate([clo, chi], 0)
    g = cg[...]
    for b in range(width // sub):
        at = pl.ds(b * sub, sub)
        s = jnp.concatenate([r[:, pl.ds((offset if r.shape[1] > width else 0) + b * sub, sub)] for r in stars], 0)
        hi, mid, lo = three(s.T)
        pred = (
            mm(jnp.concatenate([hi, lo], 1), crossed, 1, 0)
            + mm(jnp.concatenate([mid, mid], 1), upper, 1, 0)
            + mm(jnp.concatenate([hi, hi], 1), upper, 1, 0)
        )
        residual = light[pl.ds(offset + b * sub, sub), :] - pred
        ratio = 1.0 + (residual * 0.5) ** 2
        whi, wlo = two(residual / ratio)
        both = mm(g, whi, 1, 1)
        term = both[:rank] + both[rank:] + mm(g[:rank], wlo, 1, 1)
        for k, ref in enumerate(star_out):
            start = ref.shape[1] // width * width - width + b * sub
            ref[:, pl.ds(start, sub)] = term[k * rows : (k + 1) * rows]
        shi, slo = two(s)
        both = mm(jnp.concatenate([shi, slo], 0), whi, 1, 0)
        acc[...] += both[:rank] + both[rank:] + mm(shi, wlo, 1, 0)
        q = sub // 4
        prod = (ratio[:q] * ratio[q : 2 * q]) * (ratio[2 * q : 3 * q] * ratio[3 * q :])
        lacc[...] += jnp.sum(jnp.log(prod).reshape(q // 8, 8, -1), 0)

    if last:
        for k in range(n_star):
            whole[rank_rows(star_slot(k), rows), :] = acc[k * rows : (k + 1) * rows]
        keep, send, loss = ends
        mine = max(n_cad // 2, 1)
        for k in range(n_cad):
            ref, place = (keep, k) if k < mine else (send, k - mine)
            ref[pl.ds(place * crows, crows), :] = whole[rank_rows(cad_slot(k), crows), :] * (good * cad_scale)
        sums = lacc[...] * good
        lanes = sum(sums[:, c : c + 128] for c in range(0, sums.shape[1], 128))
        loss[...] = lanes
        if not first:
            for ref, half in zip(star_out, halves, strict=True):
                ref[:, :width] = half[...]
                ref[:8, ref.shape[1] - 128 :] = lanes
                ref[8:, ref.shape[1] - 128 :] = jnp.zeros((rows - 8, 128), F32)
    else:
        ends[0][...] = acc[...]
        ends[1][...] = lacc[...]


def compute(stars, cads, light, quality, before, scale, cad_scale, star_slot, cad_slot, chunk, chunks):
    rows, width = stars[0].shape[0], light.shape[0] // chunks
    crows, nc = cads[0].shape
    n_star, n_cad = len(stars), len(cads)
    rank = rows * n_star
    first, last = chunk == 0, chunk == chunks - 1
    plan = (scale, cad_scale, star_slot, cad_slot, n_star, n_cad, chunk * width, first, last)
    sds = lambda *shape: jax.ShapeDtypeStruct(shape, F32)
    mine = max(n_cad // 2, 1)
    ends = [sds(crows * mine, nc), sds(crows * max(n_cad - mine, 1), nc), sds(8, 128)] if last else [sds(rank, nc), sds(8, nc)]
    given = [light, quality] + stars + cads + list(before)
    terms = [sds(rows, width if first else 2 * width + 128)] * n_star
    vmem = pl.BlockSpec(memory_space=pltpu.VMEM)
    macs = width * nc * rank
    return pl.pallas_call(
        functools.partial(body, plan),
        in_specs=[vmem] * len(given),
        out_specs=[vmem] * (n_star + len(ends)),
        out_shape=terms + ends,
        scratch_shapes=[
            pltpu.VMEM((rank, nc), F32),
            pltpu.VMEM((3, rank, nc), BF16),
            pltpu.VMEM((2 * rank, nc), BF16),
            pltpu.VMEM((rank, nc), F32),
            pltpu.VMEM((8, nc), F32),
        ],
        compiler_params=pltpu.CompilerParams(vmem_limit_bytes=32 << 20),
        cost_estimate=pl.CostEstimate(flops=24 * macs, bytes_accessed=4 * width * (nc + 2 * rank), transcendentals=width * nc),
    )(*given)


def small_call(body_of, given, shapes, limit=4):
    vmem = pl.BlockSpec(memory_space=pltpu.VMEM)
    return pl.pallas_call(
        body_of,
        in_specs=[vmem] * len(given),
        out_specs=[vmem] * len(shapes),
        out_shape=[jax.ShapeDtypeStruct(shape, F32) for shape in shapes],
        cost_estimate=pl.CostEstimate(flops=0, bytes_accessed=1 << 10, transcendentals=0),
        compiler_params=pltpu.CompilerParams(vmem_limit_bytes=limit << 20),
    )(*given)


def empty_body(*refs):
    pass


def hold(x, *after):
    anywhere = pl.BlockSpec(memory_space=pl.ANY)
    return pl.pallas_call(
        empty_body,
        in_specs=[anywhere] * (1 + len(after)),
        out_specs=anywhere,
        out_shape=jax.ShapeDtypeStruct(x.shape, x.dtype),
        input_output_aliases={0: 0},
        cost_estimate=pl.CostEstimate(flops=0, bytes_accessed=1 << 10, transcendentals=0),
        compiler_params=pltpu.CompilerParams(vmem_limit_bytes=1 << 20),
    )(x, *after)


def halve_body(keep, got, keep_out, send_out):
    rows = keep_out.shape[0]
    keep_out[...] = keep[:rows] + got[:rows]
    send_out[...] = keep[rows:] + got[rows:]


def halve(keep, got):
    shape = (keep.shape[0] // 2, keep.shape[1])
    return small_call(halve_body, [keep, got], [shape, shape])


def last_stars_body(mine, up, back, out, loss):
    width = out.shape[1]
    out[...] = mine[:, :width] + up[:, :width] + back[:, :width]
    loss[...] = mine[:8, width:] + up[:8, width:] + back[:8, width:]


def last_stars(mine, up, back):
    rows, width = mine.shape
    return small_call(last_stars_body, [mine, up, back], [(rows, width - 128), (8, 128)])


def last_loss_body(factor, *refs):
    refs[-1][...] = jnp.sum(sum(ref[...] for ref in refs[:-1]), keepdims=True) * factor


def last_loss(losses, factor):
    return small_call(functools.partial(last_loss_body, factor), losses, [(1, 1)])[0]


def ring_order(n):
    return list(range(0, n, 2)) + list(range(1, n, 2))[::-1]


def shift(x, core=0):
    m, n = lax.axis_size("star"), lax.axis_size("cad")
    order = ring_order(n)
    pairs = []
    for i in range(m):
        way = 1 if i % 2 == 0 else -1
        source, target = i ^ int(core < 0), i ^ int(core > 0)
        pairs += [(source * n + order[p], target * n + order[(p + way) % n]) for p in range(n)]
    return lax.ppermute(x, ("star", "cad"), pairs)


def swap(x, axis, bit):
    return lax.ppermute(x, axis, [(i, i ^ bit) for i in range(lax.axis_size(axis))])


def ring_program(light, quality, star_t, cad_t):
    n, m = lax.axis_size("cad"), lax.axis_size("star")
    count, nc = light.shape
    half = count // 2
    scale = -1.0 / float(nc * n) ** 0.5
    cad_scale = -1.0 / float(count * m) ** 0.5
    factor = 2.0 / (float(count * m) * float(nc * n))

    def star_slot(k):
        me = lax.axis_index("cad")
        place = jnp.where(me % 2 == 0, me // 2, n - 1 - me // 2)
        back = jnp.where(lax.axis_index("star") % 2 == 0, n - k, k)
        source = lax.rem(place + back, n)
        return jnp.where(source < n // 2, 2 * source, 2 * (n - 1 - source) + 1)

    def cad_slot(k):
        return jnp.bitwise_xor(lax.axis_index("star"), k)

    light, quality, cad_t = stage(light, quality.reshape(1, -1), cad_t)

    with jax.named_scope("gather_cadence_factors"):
        cads = [cad_t] + [swap(cad_t, "star", bit) for bit in range(1, m)]

    far = n // 2
    pieces = [star_t] + [None] * (n - 1)
    with jax.named_scope("gather_star_factors"):
        beside = swap(star_t, "star", 1)
        for s in range(1, far):
            pieces[s] = shift(pieces[s - 1])
            if s == 1:
                beside = shift(beside)
                pieces[s], beside = hold(pieces[s], light), hold(beside, light)
            elif s < far - 1:
                beside = shift(beside)
                pieces[s] = hold(pieces[s], *cads[1:])
            else:
                beside = shift(beside, 1)
            pieces[n - s] = swap(beside, "star", 1) if s < far - 1 else beside
        far_a, far_b = shift(pieces[far - 1][:, :half]), shift(pieces[far - 1][:, half:])

    pieces[far] = far_a
    got = compute(pieces, cads, light, quality, (), scale, cad_scale, star_slot, cad_slot, 0, 2)
    terms, before = got[:n], got[n:]
    pieces[far] = far_b
    got = compute(pieces, cads, light, quality, list(before) + list(terms), scale, cad_scale, star_slot, cad_slot, 1, 2)
    terms, (keep, send, loss) = got[:n], got[n:]

    with jax.named_scope("scatter_star_gradient"):
        up = shift(terms[far])
        beside = shift(swap(terms[far - 1], "star", 1))
        keep, send = halve(keep, swap(send, "star", 2))
        for s in range(far - 1, 0, -1):
            message = terms[n - s] + up
            if s < far - 1:
                message = hold(message, waiting, *([cad_gradient] if s == 1 else []))
            up = shift(message)
            if s > 1:
                waiting = hold(swap(terms[s - 1], "star", 1) + beside, message, *([keep] if s == 3 else []))
                beside = shift(waiting)
            if s == 2:
                cad_gradient = keep + swap(send, "star", 1)
        beside = swap(beside, "star", 1)
        star_gradient, loss = last_stars(terms[0], up, beside)
    with jax.named_scope("sum_loss"):
        total = last_loss([loss] + [swap(loss, "star", bit) for bit in range(1, m)], factor)
    return (star_gradient.T, cad_gradient.T, total[0, 0])


def whole_program(light, quality, star_t, cad_t):
    n, m = lax.axis_size("cad"), lax.axis_size("star")
    count, nc = light.shape
    scale = -1.0 / float(nc * n) ** 0.5
    cad_scale = -1.0 / float(count * m) ** 0.5
    stars = [lax.all_gather(star_t, "cad", axis=0, tiled=True)]
    cads = [lax.all_gather(cad_t, "star", axis=0, tiled=True)]
    first = lambda k: 0
    star, cad, _, loss = compute(stars, cads, light, quality.reshape(1, -1), (), scale, cad_scale, first, first, 0, 1)
    star_gradient = lax.psum_scatter(star, "cad", scatter_dimension=0, tiled=True)
    cadence_gradient = lax.psum_scatter(cad, "star", scatter_dimension=0, tiled=True)
    loss = lax.psum(jnp.sum(loss), ("star", "cad")) * (2.0 / (float(count * m) * float(nc * n)))
    return (star_gradient.T, cadence_gradient.T, loss)


def on_device(light, quality, star_factors, cadence_factors):
    ring = lax.axis_size("cad") == 8 and lax.axis_size("star") == 4
    program = ring_program if ring else whole_program
    return program(light, quality, star_factors.T, cadence_factors.T)


def solution(mesh):
    in_specs = (P("star", "cad"), P("cad"), P("star", "cad"), P("cad", "star"))
    out_specs = (P("star", "cad"), P("cad", "star"), P())
    return jax.shard_map(
        on_device, mesh=mesh, in_specs=in_specs, out_specs=out_specs, check_vma=False
    )
```

time: 222 us -> 66 us (0.30)
  waiting for transfers between devices: 146 us -> 22.6 us
  blocking collectives: 32.5 us -> 0 us
  starting transfers between devices: 0.3 us -> 30.5 us
  matrix products: 20.8 us -> 0 us
  between operations: 15.5 us -> 0.78 us
  Pallas kernels: 0 us -> 7.99 us
  other arithmetic: 4.42 us -> 0.17 us
    psum x2 -> x0, waiting for transfers between devices: 99.1 us -> none  [the longest x1 99.1 us: on_device(): star_full, loss_cad = lax.psum((star_term, loss_part), 'cad')]
    all_gather x1 -> x0, waiting for transfers between devices: 46.1 us -> none  [on_device(): star_loads = lax.all_gather(star_factors, 'cad', axis=1, tiled=True)]
    ppermute x0 -> x30, starting transfers between devices: none -> 30.5 us  [the longest x15 24.8 us: shift(): return lax.ppermute(x, ('star', 'cad'), pairs)]
    psum x2 -> x0, blocking collectives: 25.8 us -> none  [the longest x1 19.6 us: on_device(): star_full, loss_cad = lax.psum((star_term, loss_part), 'cad')]
    ppermute x0 -> x30, waiting for transfers between devices: none -> 22.6 us  [the longest x15 15.4 us: shift(): return lax.ppermute(x, ('star', 'cad'), pairs)]
    dot_general x3 -> x0, matrix products: 20.8 us -> none  [the longest x1 8.77 us: on_device(): jnp.dot(weighted, cad_loads, precision=lax.Precision.HIGHEST, preferred_e...]
    pallas_call x0 -> x13, Pallas kernels: none -> 7.99 us  [the longest x2 6.26 us: compute(): pl.pallas_call(functools.partial(body, plan), in_specs=[vmem] * len(given...]
    all_gather x1 -> x0, blocking collectives: 6.71 us -> none  [on_device(): cad_loads = lax.all_gather(cadence_factors, 'star', axis=1, tiled=True)]
  transfers between devices with their start and end apart: 3 -> 30, of which waited for: 2 -> 15; matrix products, arithmetic and copies ran while one was open for 5% -> 0% of each run, Pallas kernels for 0% -> 5%
where the time goes in v2:
time: 66 us; the launch traced here: 65.7 us
  starting transfers between devices  30.5 us (46%)
  waiting for transfers between devices  22.6 us (34%)
  Pallas kernels  7.99 us (12%)
  local copies, waits for them, and re-layouts  3.65 us (6%)
  between operations  0.78 us (1%)
    ppermute x15, starting transfers between devices, shift(): return lax.ppermute(x, ('star', 'cad'), pairs)  24.8 us
    ppermute x15, waiting for transfers between devices, shift(): return lax.ppermute(x, ('star', 'cad'), pairs)  15.4 us
    ppermute x15, waiting for transfers between devices, swap(): lax.ppermute(x, axis, [(i, i ^ bit) for i in range(lax.axis_size(axis))])  7.18 us
    pallas_call x2, Pallas kernels, compute(): pl.pallas_call(functools.partial(body, plan), in_specs=[vmem] * len(given...  6.26 us
    ppermute x15, starting transfers between devices, swap(): lax.ppermute(x, axis, [(i, i ^ bit) for i in range(lax.axis_size(axis))])  5.79 us
    unnamed x10, local copies, waits for them, and re-layouts  3.63 us
    pallas_call x3, Pallas kernels, small_call(): pl.pallas_call(body_of, in_specs=[vmem] * len(given), out_specs=[vmem] *...  1.4 us
  transfers between devices with their start and end apart: 30, of which 15 were waited for; matrix products, arithmetic and copies ran while one was open for 0% of the time, Pallas kernels for 5%

profile of v2, /device:TPU:0, one launch (start us, length us, event | category | flops | bytes accessed | tf_op | source)
XLA Modules:
  0.0 65.7 jit_solution(12156707966759484678)
XLA Ops:
  0.6 0.5 collective-permute-start.7
  1.1 2.6 %collective-permute-start = (f32[16,4096]{1,0:T(8,128)}, f32[16,4096]{1,0:T(8,128)S(1)}, u32[]{:S(2)}, u32[]{:S(2)}) collective-permute-start(f32[16,4096]{1,0:T(8,128)} %bitcast.7), channel_id=1, source_target_pairs={{0,2},{2,4},{4,6},{6,7},{7,5},{5,3},{3,1},{1,0},{8,9},{10,8},{12,1... | collective-permute-start | bytes 786440 | tf_op jit(solution)/shard_map/gather_star_factors/ppermute | solution.py:242
  3.8 1.7 %collective-permute-start.8 = (f32[16,4096]{1,0:T(8,128)S(1)}, f32[16,4096]{1,0:T(8,128)S(1)}, u32[]{:S(2)}, u32[]{:S(2)}) collective-permute-start(f32[16,4096]{1,0:T(8,128)S(1)} %collective-permute-done.7), channel_id=1, source_target_pairs={{0,2},{2,4},{4,6},{6,7},{7,5},{5,3},{3,1},{1,0},{8,9},{10,8},{12,1... | collective-permute-start | bytes 786440 | tf_op jit(solution)/shard_map/gather_star_factors/ppermute | solution.py:242
  5.5 2.2 %copy-done = f32[4096,256]{1,0:T(8,128)S(1)} copy-done((f32[4096,256]{1,0:T(8,128)S(1)}, f32[4096,256]{1,0:T(8,128)}, u32[]{:S(2)}) %copy-start) | copy-done | bytes 4194328
  7.7 0.8 %copy-done.3 = f32[256,32]{0,1:T(8,128)S(1)} copy-done((f32[256,32]{0,1:T(8,128)S(1)}, f32[256,32]{0,1:T(8,128)}, u32[]{:S(2)}) %copy-start.3) | copy-done | bytes 32792
  8.4 0.7 %copy-done.4 = s32[256]{0:T(256)S(1)} copy-done((s32[256]{0:T(256)S(1)}, s32[256]{0:T(256)}, u32[]{:S(2)}) %copy-start.4) | copy-done | bytes 1048
  9.1 0.3 shard_map.67
  9.4 0.0 copy-start.1
  9.5 1.6 %collective-permute-start.1 = (f32[16,4096]{1,0:T(8,128)S(1)}, f32[16,4096]{1,0:T(8,128)S(1)}, u32[]{:S(2)}, u32[]{:S(2)}) collective-permute-start(f32[16,4096]{1,0:T(8,128)S(1)} %gather_star_factors.3.refs_3_), channel_id=1, source_target_pairs={{0,2},{2,4},{4,6},{6,7},{7,5},{5,3},{3,1},{1,0},{8,9},{10,8},{12,1... | collective-permute-start | bytes 786440 | tf_op jit(solution)/shard_map/gather_star_factors/ppermute | solution.py:242
  11.1 0.6 collective-permute-start.4
  11.7 0.9 %collective-permute-start.3 = (f32[32,256]{1,0:T(8,128)S(1)}, f32[32,256]{1,0:T(8,128)S(1)}, u32[]{:S(2)}, u32[]{:S(2)}) collective-permute-start(f32[32,256]{1,0:T(8,128)S(1)} %get-tuple-element.32.refs_10_), channel_id=1, source_target_pairs={{0,16},{8,24},{16,0},{24,8},{1,17},{9,25},{17,1},{25,9},{2,18},{10... | collective-permute-start | bytes 98312 | tf_op jit(solution)/shard_map/gather_cadence_factors/ppermute | solution.py:246
  12.6 0.3 collective-permute-start.2
  12.9 1.6 %collective-permute-start.9 = (f32[16,4096]{1,0:T(8,128)S(1)}, f32[16,4096]{1,0:T(8,128)S(1)}, u32[]{:S(2)}, u32[]{:S(2)}) collective-permute-start(f32[16,4096]{1,0:T(8,128)S(1)} %gather_star_factors.5), channel_id=1, source_target_pairs={{0,2},{2,4},{4,6},{6,7},{7,5},{5,3},{3,1},{1,0},{8,9},{10,8},{12,1... | collective-permute-start | bytes 786440 | tf_op jit(solution)/shard_map/gather_star_factors/ppermute | solution.py:242
  14.5 0.2 collective-permute-done.4.refs_3_.refs_13_
  14.7 1.2 %collective-permute-done.3.refs_2_.refs_12_ = f32[32,256]{1,0:T(8,128)S(1)} collective-permute-done((f32[32,256]{1,0:T(8,128)S(1)}, f32[32,256]{1,0:T(8,128)S(1)}, u32[]{:S(2)}, u32[]{:S(2)}) %collective-permute-start.3) | collective-permute-done | bytes 32800 | tf_op jit(solution)/shard_map/gather_cadence_factors/ppermute | solution.py:246
  15.9 1.5 %collective-permute-start.5 = (f32[16,4096]{1,0:T(8,128)S(1)}, f32[16,4096]{1,0:T(8,128)S(1)}, u32[]{:S(2)}, u32[]{:S(2)}) collective-permute-start(f32[16,4096]{1,0:T(8,128)S(1)} %gather_star_factors.4.refs_4_), channel_id=1, source_target_pairs={{0,2},{2,4},{4,6},{6,7},{7,5},{5,3},{3,1},{1,0},{8,9},{10,8},{12,1... | collective-permute-start | bytes 786440 | tf_op jit(solution)/shard_map/gather_star_factors/ppermute | solution.py:242
  17.5 1.9 %collective-permute-done.9 = f32[16,4096]{1,0:T(8,128)S(1)} collective-permute-done((f32[16,4096]{1,0:T(8,128)S(1)}, f32[16,4096]{1,0:T(8,128)S(1)}, u32[]{:S(2)}, u32[]{:S(2)}) %collective-permute-start.9) | collective-permute-done | bytes 262176 | tf_op jit(solution)/shard_map/gather_star_factors/ppermute | solution.py:242
  19.3 1.7 %collective-permute-start.10 = (f32[16,4096]{1,0:T(8,128)S(1)}, f32[16,4096]{1,0:T(8,128)S(1)}, u32[]{:S(2)}, u32[]{:S(2)}) collective-permute-start(f32[16,4096]{1,0:T(8,128)S(1)} %collective-permute-done.9), channel_id=1, source_target_pairs={{0,10},{2,12},{4,14},{6,15},{7,13},{5,11},{3,9},{1,8},{8,1},{10,0}... | collective-permute-start | bytes 786440 | tf_op jit(solution)/shard_map/gather_star_factors/ppermute | solution.py:242
  21.0 1.3 %collective-permute-done.5.refs_5_ = f32[16,4096]{1,0:T(8,128)S(1)} collective-permute-done((f32[16,4096]{1,0:T(8,128)S(1)}, f32[16,4096]{1,0:T(8,128)S(1)}, u32[]{:S(2)}, u32[]{:S(2)}) %collective-permute-start.5) | collective-permute-done | bytes 262176 | tf_op jit(solution)/shard_map/gather_star_factors/ppermute | solution.py:242
  22.4 1.5 %collective-permute-start.13 = (f32[16,2048]{1,0:T(8,128)S(1)}, f32[16,2048]{1,0:T(8,128)S(1)}, u32[]{:S(2)}, u32[]{:S(2)}) collective-permute-start(f32[16,2048]{1,0:T(8,128)S(1)} %get-tuple-element.57), channel_id=1, source_target_pairs={{0,2},{2,4},{4,6},{6,7},{7,5},{5,3},{3,1},{1,0},{8,9},{10,8},{12,1... | collective-permute-start | bytes 393224 | tf_op jit(solution)/shard_map/gather_star_factors/ppermute | solution.py:242
  23.9 1.6 %collective-permute-start.6 = (f32[16,2048]{1,0:T(8,128)S(1)}, f32[16,2048]{1,0:T(8,128)S(1)}, u32[]{:S(2)}, u32[]{:S(2)}) collective-permute-start(f32[16,2048]{1,0:T(8,128)S(1)} %get-tuple-element.58), channel_id=1, source_target_pairs={{0,2},{2,4},{4,6},{6,7},{7,5},{5,3},{3,1},{1,0},{8,9},{10,8},{12,1... | collective-permute-start | bytes 393224 | tf_op jit(solution)/shard_map/gather_star_factors/ppermute | solution.py:242
  25.5 1.9 %collective-permute-done.13.refs_6_ = f32[16,2048]{1,0:T(8,128)S(1)} collective-permute-done((f32[16,2048]{1,0:T(8,128)S(1)}, f32[16,2048]{1,0:T(8,128)S(1)}, u32[]{:S(2)}, u32[]{:S(2)}) %collective-permute-start.13) | collective-permute-done | bytes 131104 | tf_op jit(solution)/shard_map/gather_star_factors/ppermute | solution.py:242
  27.4 2.9 %shard_map.68 = (f32[16,2048]{1,0:T(8,128)S(1)}, f32[16,2048]{1,0:T(8,128)S(1)}, f32[16,2048]{1,0:T(8,128)S(1)}, f32[16,2048]{1,0:T(8,128)S(1)}, f32[16,2048]{1,...) custom-call(f32[4096,256]{1,0:T(8,128)S(1)} %get-tuple-element.30.re, ...), custom_call_target="tpu_custom_call" | custom-call | flops 1610612736 | bytes 4194304 | tf_op jit(solution)/shard_map/pallas_call | solution.py:154
  30.4 3.3 %shard_map.69 = (f32[16,4224]{1,0:T(8,128)S(1)}, f32[16,4224]{1,0:T(8,128)S(1)}, f32[16,4224]{1,0:T(8,128)S(1)}, f32[16,4224]{1,0:T(8,128)S(1)}, f32[16,4224]{1,...) custom-call(f32[4096,256]{1,0:T(8,128)S(1)} %get-tuple-element.30.re, ...), custom_call_target="tpu_custom_call" | custom-call | flops 1610612736 | bytes 4194304 | tf_op jit(solution)/shard_map/pallas_call | solution.py:154
  33.7 1.5 %collective-permute-start.14 = (f32[16,4224]{1,0:T(8,128)S(1)}, f32[16,4224]{1,0:T(8,128)S(1)}, u32[]{:S(2)}, u32[]{:S(2)}) collective-permute-start(f32[16,4224]{1,0:T(8,128)S(1)} %get-tuple-element.47), channel_id=1, source_target_pairs={{0,2},{2,4},{4,6},{6,7},{7,5},{5,3},{3,1},{1,0},{8,9},{10,8},{12,1... | collective-permute-start | bytes 811016 | tf_op jit(solution)/shard_map/scatter_star_gradient/ppermute | solution.py:242
  35.2 0.0 collective-permute-start.16
  35.2 0.0 collective-permute-done.17
  35.2 1.5 %collective-permute-start.18 = (f32[16,4224]{1,0:T(8,128)S(1)}, f32[16,4224]{1,0:T(8,128)S(1)}, u32[]{:S(2)}, u32[]{:S(2)}) collective-permute-start(f32[16,4224]{1,0:T(8,128)S(1)} %collective-permute-done.17), channel_id=1, source_target_pairs={{0,2},{2,4},{4,6},{6,7},{7,5},{5,3},{3,1},{1,0},{8,9},{10,8},{12,1... | collective-permute-start | bytes 811016 | tf_op jit(solution)/shard_map/scatter_star_gradient/ppermute | solution.py:242
  36.7 1.5 %collective-permute-start.19 = (f32[64,256]{1,0:T(8,128)S(1)}, f32[64,256]{1,0:T(8,128)S(1)}, u32[]{:S(2)}, u32[]{:S(2)}) collective-permute-start(f32[64,256]{1,0:T(8,128)S(1)} %get-tuple-element.51), channel_id=1, source_target_pairs={{0,16},{8,24},{16,0},{24,8},{1,17},{9,25},{17,1},{25,9},{2,18},{10... | collective-permute-start | bytes 196616 | tf_op jit(solution)/shard_map/scatter_star_gradient/ppermute | solution.py:246
  38.3 2.7 %collective-permute-done.19.got = f32[64,256]{1,0:T(8,128)S(1)} collective-permute-done((f32[64,256]{1,0:T(8,128)S(1)}, f32[64,256]{1,0:T(8,128)S(1)}, u32[]{:S(2)}, u32[]{:S(2)}) %collective-permute-start.19) | collective-permute-done | bytes 65568 | tf_op jit(solution)/shard_map/scatter_star_gradient/ppermute | solution.py:246
  41.1 1.6 %collective-permute-start.15 = (f32[16,4224]{1,0:T(8,128)S(1)}, f32[16,4224]{1,0:T(8,128)S(1)}, u32[]{:S(2)}, u32[]{:S(2)}) collective-permute-start(f32[16,4224]{1,0:T(8,128)S(1)} %add.18.refs_1_), channel_id=1, source_target_pairs={{0,2},{2,4},{4,6},{6,7},{7,5},{5,3},{3,1},{1,0},{8,9},{10,8},{12,1... | collective-permute-start | bytes 811016 | tf_op jit(solution)/shard_map/scatter_star_gradient/ppermute | solution.py:242
  42.7 0.4 collective-permute-done.18
  43.1 1.5 %collective-permute-start.22 = (f32[16,4224]{1,0:T(8,128)S(1)}, f32[16,4224]{1,0:T(8,128)S(1)}, u32[]{:S(2)}, u32[]{:S(2)}) collective-permute-start(f32[16,4224]{1,0:T(8,128)S(1)} %scatter_star_gradient.7.refs_1_), channel_id=1, source_target_pairs={{0,2},{2,4},{4,6},{6,7},{7,5},{5,3},{3,1},{1,0},{8,9},{10,8},{12,1... | collective-permute-start | bytes 811016 | tf_op jit(solution)/shard_map/scatter_star_gradient/ppermute | solution.py:242
  44.6 3.0 %collective-permute-done.15 = f32[16,4224]{1,0:T(8,128)S(1)} collective-permute-done((f32[16,4224]{1,0:T(8,128)S(1)}, f32[16,4224]{1,0:T(8,128)S(1)}, u32[]{:S(2)}, u32[]{:S(2)}) %collective-permute-start.15) | collective-permute-done | bytes 270368 | tf_op jit(solution)/shard_map/scatter_star_gradient/ppermute | solution.py:242
  47.6 1.6 %collective-permute-start.20 = (f32[16,4224]{1,0:T(8,128)S(1)}, f32[16,4224]{1,0:T(8,128)S(1)}, u32[]{:S(2)}, u32[]{:S(2)}) collective-permute-start(f32[16,4224]{1,0:T(8,128)S(1)} %scatter_star_gradient.8.refs_1_), channel_id=1, source_target_pairs={{0,2},{2,4},{4,6},{6,7},{7,5},{5,3},{3,1},{1,0},{8,9},{10,8},{12,1... | collective-permute-start | bytes 811016 | tf_op jit(solution)/shard_map/scatter_star_gradient/ppermute | solution.py:242
  49.2 1.3 %collective-permute-done.22 = f32[16,4224]{1,0:T(8,128)S(1)} collective-permute-done((f32[16,4224]{1,0:T(8,128)S(1)}, f32[16,4224]{1,0:T(8,128)S(1)}, u32[]{:S(2)}, u32[]{:S(2)}) %collective-permute-start.22) | collective-permute-done | bytes 270368 | tf_op jit(solution)/shard_map/scatter_star_gradient/ppermute | solution.py:242
  50.5 1.6 %collective-permute-start.25 = (f32[16,4224]{1,0:T(8,128)S(1)}, f32[16,4224]{1,0:T(8,128)S(1)}, u32[]{:S(2)}, u32[]{:S(2)}) collective-permute-start(f32[16,4224]{1,0:T(8,128)S(1)} %scatter_star_gradient.9.refs_1_), channel_id=1, source_target_pairs={{0,2},{2,4},{4,6},{6,7},{7,5},{5,3},{3,1},{1,0},{8,9},{10,8},{12,1... | collective-permute-start | bytes 811016 | tf_op jit(solution)/shard_map/scatter_star_gradient/ppermute | solution.py:242
  52.1 1.2 %collective-permute-done.23 = f32[32,256]{1,0:T(8,128)S(1)} collective-permute-done((f32[32,256]{1,0:T(8,128)S(1)}, f32[32,256]{1,0:T(8,128)S(1)}, u32[]{:S(2)}, u32[]{:S(2)}) %collective-permute-start.23) | collective-permute-done | bytes 32800 | tf_op jit(solution)/shard_map/scatter_star_gradient/ppermute | solution.py:246
  53.3 0.8 %collective-permute-done.20 = f32[16,4224]{1,0:T(8,128)S(1)} collective-permute-done((f32[16,4224]{1,0:T(8,128)S(1)}, f32[16,4224]{1,0:T(8,128)S(1)}, u32[]{:S(2)}, u32[]{:S(2)}) %collective-permute-start.20) | collective-permute-done | bytes 270368 | tf_op jit(solution)/shard_map/scatter_star_gradient/ppermute | solution.py:242
  54.2 1.6 %collective-permute-start.24 = (f32[16,4224]{1,0:T(8,128)S(1)}, f32[16,4224]{1,0:T(8,128)S(1)}, u32[]{:S(2)}, u32[]{:S(2)}) collective-permute-start(f32[16,4224]{1,0:T(8,128)S(1)} %scatter_star_gradient.10), channel_id=1, source_target_pairs={{0,2},{2,4},{4,6},{6,7},{7,5},{5,3},{3,1},{1,0},{8,9},{10,8},{12,1... | collective-permute-start | bytes 811016 | tf_op jit(solution)/shard_map/scatter_star_gradient/ppermute | solution.py:242
  55.8 1.3 %collective-permute-done.25 = f32[16,4224]{1,0:T(8,128)S(1)} collective-permute-done((f32[16,4224]{1,0:T(8,128)S(1)}, f32[16,4224]{1,0:T(8,128)S(1)}, u32[]{:S(2)}, u32[]{:S(2)}) %collective-permute-start.25) | collective-permute-done | bytes 270368 | tf_op jit(solution)/shard_map/scatter_star_gradient/ppermute | solution.py:242
  57.0 3.7 %collective-permute-done.24.up = f32[16,4224]{1,0:T(8,128)S(1)} collective-permute-done((f32[16,4224]{1,0:T(8,128)S(1)}, f32[16,4224]{1,0:T(8,128)S(1)}, u32[]{:S(2)}, u32[]{:S(2)}) %collective-permute-start.24) | collective-permute-done | bytes 270368 | tf_op jit(solution)/shard_map/scatter_star_gradient/ppermute | solution.py:242
  60.7 0.8 %scatter_star_gradient.11 = (f32[16,4096]{1,0:T(8,128)}, f32[8,128]{1,0:T(8,128)S(1)}) custom-call(f32[16,4224]{1,0:T(8,128)S(1)} %get-tuple-element.43.mine, f32[16,4224]{1,0:T(8,128)S(1)} %collective-permute-done.24.up, f32[16,4224]{1,0:T(8,128)S(1)} %collective-permute-done.26.back), custom_call_target="tpu_custom_call" | custom-call | bytes 1024 | tf_op jit(solution)/shard_map/scatter_star_gradient/pallas_call | solution.py:173
  61.5 1.6 %collective-permute-start.28 = (f32[8,128]{1,0:T(8,128)S(1)}, f32[8,128]{1,0:T(8,128)S(1)}, u32[]{:S(2)}, u32[]{:S(2)}) collective-permute-start(f32[8,128]{1,0:T(8,128)S(1)} %get-tuple-element.56.refs_0_), channel_id=1, source_target_pairs={{0,16},{8,24},{16,0},{24,8},{1,17},{9,25},{17,1},{25,9},{2,18},{10... | collective-permute-start | bytes 12296 | tf_op jit(solution)/shard_map/sum_loss/ppermute | solution.py:246
  63.0 0.3 collective-permute-start.27
  63.3 1.2 %collective-permute-done.29.refs_3_ = f32[8,128]{1,0:T(8,128)S(1)} collective-permute-done((f32[8,128]{1,0:T(8,128)S(1)}, f32[8,128]{1,0:T(8,128)S(1)}, u32[]{:S(2)}, u32[]{:S(2)}) %collective-permute-start.29) | collective-permute-done | bytes 4128 | tf_op jit(solution)/shard_map/sum_loss/ppermute | solution.py:246
  64.5 0.6 collective-permute-done.28.refs_2_
  65.1 0.6 sum_loss.1
  (42 shorter events, 0.3 us)
Async XLA Ops:
  0.6 3.2 %collective-permute-start.7 = (f32[16,4096]{1,0:T(8,128)}, f32[16,4096]{1,0:T(8,128)S(1)}, u32[]{:S(2)}, u32[]{:S(2)}) collective-permute-start(f32[16,4096]{1,0:T(8,128)} %bitcast.6), channel_id=1, source_target_pairs={{0,8},{8,0},{16,24},{24,16},{1,9},{9,1},{17,25},{25,17},{2,10},{10... | collective-permute-start | bytes 786440 | tf_op jit(solution)/shard_map/gather_star_factors/ppermute | solution.py:246
  1.1 8.3 %collective-permute-start = (f32[16,4096]{1,0:T(8,128)}, f32[16,4096]{1,0:T(8,128)S(1)}, u32[]{:S(2)}, u32[]{:S(2)}) collective-permute-start(f32[16,4096]{1,0:T(8,128)} %bitcast.7), channel_id=1, source_target_pairs={{0,2},{2,4},{4,6},{6,7},{7,5},{5,3},{3,1},{1,0},{8,9},{10,8},{12,1... | collective-permute-start | bytes 786440 | tf_op jit(solution)/shard_map/gather_star_factors/ppermute | solution.py:242
  3.8 9.2 %collective-permute-start.8 = (f32[16,4096]{1,0:T(8,128)S(1)}, f32[16,4096]{1,0:T(8,128)S(1)}, u32[]{:S(2)}, u32[]{:S(2)}) collective-permute-start(f32[16,4096]{1,0:T(8,128)S(1)} %collective-permute-done.7), channel_id=1, source_target_pairs={{0,2},{2,4},{4,6},{6,7},{7,5},{5,3},{3,1},{1,0},{8,9},{10,8},{12,1... | collective-permute-start | bytes 786440 | tf_op jit(solution)/shard_map/gather_star_factors/ppermute | solution.py:242
  5.5 2.2 %copy-start = (f32[4096,256]{1,0:T(8,128)S(1)}, f32[4096,256]{1,0:T(8,128)}, u32[]{:S(2)}) copy-start(f32[4096,256]{1,0:T(8,128)} %light_in.1) | copy-start | bytes 12582916
  7.7 0.8 %copy-start.3 = (f32[256,32]{0,1:T(8,128)S(1)}, f32[256,32]{0,1:T(8,128)}, u32[]{:S(2)}) copy-start(f32[256,32]{0,1:T(8,128)} %param.7) | copy-start | bytes 98308
  8.4 0.7 %copy-start.4 = (s32[256]{0:T(256)S(1)}, s32[256]{0:T(256)}, u32[]{:S(2)}) copy-start(s32[256]{0:T(256)} %param.5) | copy-start | bytes 3076
  9.4 18.0 %copy-start.1 = (f32[4096,16]{0,1:T(8,128)S(1)}, f32[4096,16]{0,1:T(8,128)}, u32[]{:S(2)}) copy-start(f32[4096,16]{0,1:T(8,128)} %param.6) | copy-start | bytes 786436
  9.5 6.5 %collective-permute-start.1 = (f32[16,4096]{1,0:T(8,128)S(1)}, f32[16,4096]{1,0:T(8,128)S(1)}, u32[]{:S(2)}, u32[]{:S(2)}) collective-permute-start(f32[16,4096]{1,0:T(8,128)S(1)} %gather_star_factors.3.refs_3_), channel_id=1, source_target_pairs={{0,2},{2,4},{4,6},{6,7},{7,5},{5,3},{3,1},{1,0},{8,9},{10,8},{12,1... | collective-permute-start | bytes 786440 | tf_op jit(solution)/shard_map/gather_star_factors/ppermute | solution.py:242
  11.1 3.6 %collective-permute-start.4 = (f32[32,256]{1,0:T(8,128)S(1)}, f32[32,256]{1,0:T(8,128)S(1)}, u32[]{:S(2)}, u32[]{:S(2)}) collective-permute-start(f32[32,256]{1,0:T(8,128)S(1)} %get-tuple-element.32.refs_10_), channel_id=1, source_target_pairs={{0,24},{8,16},{16,8},{24,0},{1,25},{9,17},{17,9},{25,1},{2,26},{10... | collective-permute-start | bytes 98312 | tf_op jit(solution)/shard_map/gather_cadence_factors/ppermute | solution.py:246
  11.7 4.2 %collective-permute-start.3 = (f32[32,256]{1,0:T(8,128)S(1)}, f32[32,256]{1,0:T(8,128)S(1)}, u32[]{:S(2)}, u32[]{:S(2)}) collective-permute-start(f32[32,256]{1,0:T(8,128)S(1)} %get-tuple-element.32.refs_10_), channel_id=1, source_target_pairs={{0,16},{8,24},{16,0},{24,8},{1,17},{9,25},{17,1},{25,9},{2,18},{10... | collective-permute-start | bytes 98312 | tf_op jit(solution)/shard_map/gather_cadence_factors/ppermute | solution.py:246
  12.6 3.3 %collective-permute-start.2 = (f32[32,256]{1,0:T(8,128)S(1)}, f32[32,256]{1,0:T(8,128)S(1)}, u32[]{:S(2)}, u32[]{:S(2)}) collective-permute-start(f32[32,256]{1,0:T(8,128)S(1)} %get-tuple-element.32.refs_10_), channel_id=1, source_target_pairs={{0,8},{8,0},{16,24},{24,16},{1,9},{9,1},{17,25},{25,17},{2,10},{10... | collective-permute-start | bytes 98312 | tf_op jit(solution)/shard_map/gather_cadence_factors/ppermute | solution.py:246
  12.9 6.4 %collective-permute-start.9 = (f32[16,4096]{1,0:T(8,128)S(1)}, f32[16,4096]{1,0:T(8,128)S(1)}, u32[]{:S(2)}, u32[]{:S(2)}) collective-permute-start(f32[16,4096]{1,0:T(8,128)S(1)} %gather_star_factors.5), channel_id=1, source_target_pairs={{0,2},{2,4},{4,6},{6,7},{7,5},{5,3},{3,1},{1,0},{8,9},{10,8},{12,1... | collective-permute-start | bytes 786440 | tf_op jit(solution)/shard_map/gather_star_factors/ppermute | solution.py:242
  15.9 6.4 %collective-permute-start.5 = (f32[16,4096]{1,0:T(8,128)S(1)}, f32[16,4096]{1,0:T(8,128)S(1)}, u32[]{:S(2)}, u32[]{:S(2)}) collective-permute-start(f32[16,4096]{1,0:T(8,128)S(1)} %gather_star_factors.4.refs_4_), channel_id=1, source_target_pairs={{0,2},{2,4},{4,6},{6,7},{7,5},{5,3},{3,1},{1,0},{8,9},{10,8},{12,1... | collective-permute-start | bytes 786440 | tf_op jit(solution)/shard_map/gather_star_factors/ppermute | solution.py:242
  17.5 8.0 %collective-permute-start.12 = (f32[16,4096]{1,0:T(8,128)S(1)}, f32[16,4096]{1,0:T(8,128)S(1)}, u32[]{:S(2)}, u32[]{:S(2)}) collective-permute-start(f32[16,4096]{1,0:T(8,128)S(1)} %gather_star_factors.5), channel_id=1, source_target_pairs={{0,8},{8,0},{16,24},{24,16},{1,9},{9,1},{17,25},{25,17},{2,10},{10... | collective-permute-start | bytes 786440 | tf_op jit(solution)/shard_map/gather_star_factors/ppermute | solution.py:246
  19.3 8.1 %collective-permute-start.11 = (f32[16,4096]{1,0:T(8,128)S(1)}, f32[16,4096]{1,0:T(8,128)S(1)}, u32[]{:S(2)}, u32[]{:S(2)}) collective-permute-start(f32[16,4096]{1,0:T(8,128)S(1)} %collective-permute-done.9), channel_id=1, source_target_pairs={{0,8},{8,0},{16,24},{24,16},{1,9},{9,1},{17,25},{25,17},{2,10},{10... | collective-permute-start | bytes 786440 | tf_op jit(solution)/shard_map/gather_star_factors/ppermute | solution.py:246
  19.3 8.1 %collective-permute-start.10 = (f32[16,4096]{1,0:T(8,128)S(1)}, f32[16,4096]{1,0:T(8,128)S(1)}, u32[]{:S(2)}, u32[]{:S(2)}) collective-permute-start(f32[16,4096]{1,0:T(8,128)S(1)} %collective-permute-done.9), channel_id=1, source_target_pairs={{0,10},{2,12},{4,14},{6,15},{7,13},{5,11},{3,9},{1,8},{8,1},{10,0}... | collective-permute-start | bytes 786440 | tf_op jit(solution)/shard_map/gather_star_factors/ppermute | solution.py:242
  22.4 5.0 %collective-permute-start.13 = (f32[16,2048]{1,0:T(8,128)S(1)}, f32[16,2048]{1,0:T(8,128)S(1)}, u32[]{:S(2)}, u32[]{:S(2)}) collective-permute-start(f32[16,2048]{1,0:T(8,128)S(1)} %get-tuple-element.57), channel_id=1, source_target_pairs={{0,2},{2,4},{4,6},{6,7},{7,5},{5,3},{3,1},{1,0},{8,9},{10,8},{12,1... | collective-permute-start | bytes 393224 | tf_op jit(solution)/shard_map/gather_star_factors/ppermute | solution.py:242
  23.9 6.4 %collective-permute-start.6 = (f32[16,2048]{1,0:T(8,128)S(1)}, f32[16,2048]{1,0:T(8,128)S(1)}, u32[]{:S(2)}, u32[]{:S(2)}) collective-permute-start(f32[16,2048]{1,0:T(8,128)S(1)} %get-tuple-element.58), channel_id=1, source_target_pairs={{0,2},{2,4},{4,6},{6,7},{7,5},{5,3},{3,1},{1,0},{8,9},{10,8},{12,1... | collective-permute-start | bytes 393224 | tf_op jit(solution)/shard_map/gather_star_factors/ppermute | solution.py:242
  33.7 1.5 %collective-permute-start.17 = (f32[16,4224]{1,0:T(8,128)S(1)}, f32[16,4224]{1,0:T(8,128)S(1)}, u32[]{:S(2)}, u32[]{:S(2)}) collective-permute-start(f32[16,4224]{1,0:T(8,128)S(1)} %get-tuple-element.49), channel_id=1, source_target_pairs={{0,8},{8,0},{16,24},{24,16},{1,9},{9,1},{17,25},{25,17},{2,10},{10... | collective-permute-start | bytes 811016 | tf_op jit(solution)/shard_map/scatter_star_gradient/ppermute | solution.py:246
  33.7 7.4 %collective-permute-start.14 = (f32[16,4224]{1,0:T(8,128)S(1)}, f32[16,4224]{1,0:T(8,128)S(1)}, u32[]{:S(2)}, u32[]{:S(2)}) collective-permute-start(f32[16,4224]{1,0:T(8,128)S(1)} %get-tuple-element.47), channel_id=1, source_target_pairs={{0,2},{2,4},{4,6},{6,7},{7,5},{5,3},{3,1},{1,0},{8,9},{10,8},{12,1... | collective-permute-start | bytes 811016 | tf_op jit(solution)/shard_map/scatter_star_gradient/ppermute | solution.py:242
  35.2 7.5 %collective-permute-start.16 = (f32[16,4224]{1,0:T(8,128)S(1)}, f32[16,4224]{1,0:T(8,128)S(1)}, u32[]{:S(2)}, u32[]{:S(2)}) collective-permute-start(f32[16,4224]{1,0:T(8,128)S(1)} %get-tuple-element.48), channel_id=1, source_target_pairs={{0,8},{8,0},{16,24},{24,16},{1,9},{9,1},{17,25},{25,17},{2,10},{10... | collective-permute-start | bytes 811016 | tf_op jit(solution)/shard_map/scatter_star_gradient/ppermute | solution.py:246
  35.2 7.8 %collective-permute-start.18 = (f32[16,4224]{1,0:T(8,128)S(1)}, f32[16,4224]{1,0:T(8,128)S(1)}, u32[]{:S(2)}, u32[]{:S(2)}) collective-permute-start(f32[16,4224]{1,0:T(8,128)S(1)} %collective-permute-done.17), channel_id=1, source_target_pairs={{0,2},{2,4},{4,6},{6,7},{7,5},{5,3},{3,1},{1,0},{8,9},{10,8},{12,1... | collective-permute-start | bytes 811016 | tf_op jit(solution)/shard_map/scatter_star_gradient/ppermute | solution.py:242
  36.7 4.3 %collective-permute-start.19 = (f32[64,256]{1,0:T(8,128)S(1)}, f32[64,256]{1,0:T(8,128)S(1)}, u32[]{:S(2)}, u32[]{:S(2)}) collective-permute-start(f32[64,256]{1,0:T(8,128)S(1)} %get-tuple-element.51), channel_id=1, source_target_pairs={{0,16},{8,24},{16,0},{24,8},{1,17},{9,25},{17,1},{25,9},{2,18},{10... | collective-permute-start | bytes 196616 | tf_op jit(solution)/shard_map/scatter_star_gradient/ppermute | solution.py:246
  38.3 11.0 %collective-permute-start.21 = (f32[16,4224]{1,0:T(8,128)S(1)}, f32[16,4224]{1,0:T(8,128)S(1)}, u32[]{:S(2)}, u32[]{:S(2)}) collective-permute-start(f32[16,4224]{1,0:T(8,128)S(1)} %get-tuple-element.53), channel_id=1, source_target_pairs={{0,8},{8,0},{16,24},{24,16},{1,9},{9,1},{17,25},{25,17},{2,10},{10... | collective-permute-start | bytes 811016 | tf_op jit(solution)/shard_map/scatter_star_gradient/ppermute | solution.py:246
  41.1 6.5 %collective-permute-start.15 = (f32[16,4224]{1,0:T(8,128)S(1)}, f32[16,4224]{1,0:T(8,128)S(1)}, u32[]{:S(2)}, u32[]{:S(2)}) collective-permute-start(f32[16,4224]{1,0:T(8,128)S(1)} %add.18.refs_1_), channel_id=1, source_target_pairs={{0,2},{2,4},{4,6},{6,7},{7,5},{5,3},{3,1},{1,0},{8,9},{10,8},{12,1... | collective-permute-start | bytes 811016 | tf_op jit(solution)/shard_map/scatter_star_gradient/ppermute | solution.py:242
  43.1 7.4 %collective-permute-start.22 = (f32[16,4224]{1,0:T(8,128)S(1)}, f32[16,4224]{1,0:T(8,128)S(1)}, u32[]{:S(2)}, u32[]{:S(2)}) collective-permute-start(f32[16,4224]{1,0:T(8,128)S(1)} %scatter_star_gradient.7.refs_1_), channel_id=1, source_target_pairs={{0,2},{2,4},{4,6},{6,7},{7,5},{5,3},{3,1},{1,0},{8,9},{10,8},{12,1... | collective-permute-start | bytes 811016 | tf_op jit(solution)/shard_map/scatter_star_gradient/ppermute | solution.py:242
  47.6 6.5 %collective-permute-start.20 = (f32[16,4224]{1,0:T(8,128)S(1)}, f32[16,4224]{1,0:T(8,128)S(1)}, u32[]{:S(2)}, u32[]{:S(2)}) collective-permute-start(f32[16,4224]{1,0:T(8,128)S(1)} %scatter_star_gradient.8.refs_1_), channel_id=1, source_target_pairs={{0,2},{2,4},{4,6},{6,7},{7,5},{5,3},{3,1},{1,0},{8,9},{10,8},{12,1... | collective-permute-start | bytes 811016 | tf_op jit(solution)/shard_map/scatter_star_gradient/ppermute | solution.py:242
  50.5 6.5 %collective-permute-start.25 = (f32[16,4224]{1,0:T(8,128)S(1)}, f32[16,4224]{1,0:T(8,128)S(1)}, u32[]{:S(2)}, u32[]{:S(2)}) collective-permute-start(f32[16,4224]{1,0:T(8,128)S(1)} %scatter_star_gradient.9.refs_1_), channel_id=1, source_target_pairs={{0,2},{2,4},{4,6},{6,7},{7,5},{5,3},{3,1},{1,0},{8,9},{10,8},{12,1... | collective-permute-start | bytes 811016 | tf_op jit(solution)/shard_map/scatter_star_gradient/ppermute | solution.py:242
  52.1 1.2 %collective-permute-start.23 = (f32[32,256]{1,0:T(8,128)S(1)}, f32[32,256]{1,0:T(8,128)S(1)}, u32[]{:S(2)}, u32[]{:S(2)}) collective-permute-start(f32[32,256]{1,0:T(8,128)S(1)} %get-tuple-element.54), channel_id=1, source_target_pairs={{0,8},{8,0},{16,24},{24,16},{1,9},{9,1},{17,25},{25,17},{2,10},{10... | collective-permute-start | bytes 98312 | tf_op jit(solution)/shard_map/scatter_star_gradient/ppermute | solution.py:246
  53.3 12.4 %copy-start.2 = (f32[32,256]{1,0:T(8,128)}, f32[32,256]{1,0:T(8,128)S(1)}, u32[]{:S(2)}) copy-start(f32[32,256]{1,0:T(8,128)S(1)} %add.23.refs_2_) | copy-start | bytes 98308
  54.2 6.5 %collective-permute-start.24 = (f32[16,4224]{1,0:T(8,128)S(1)}, f32[16,4224]{1,0:T(8,128)S(1)}, u32[]{:S(2)}, u32[]{:S(2)}) collective-permute-start(f32[16,4224]{1,0:T(8,128)S(1)} %scatter_star_gradient.10), channel_id=1, source_target_pairs={{0,2},{2,4},{4,6},{6,7},{7,5},{5,3},{3,1},{1,0},{8,9},{10,8},{12,1... | collective-permute-start | bytes 811016 | tf_op jit(solution)/shard_map/scatter_star_gradient/ppermute | solution.py:242
  57.0 3.7 %collective-permute-start.26 = (f32[16,4224]{1,0:T(8,128)S(1)}, f32[16,4224]{1,0:T(8,128)S(1)}, u32[]{:S(2)}, u32[]{:S(2)}) collective-permute-start(f32[16,4224]{1,0:T(8,128)S(1)} %collective-permute-done.25), channel_id=1, source_target_pairs={{0,8},{8,0},{16,24},{24,16},{1,9},{9,1},{17,25},{25,17},{2,10},{10... | collective-permute-start | bytes 811016 | tf_op jit(solution)/shard_map/scatter_star_gradient/ppermute | solution.py:246
  61.5 3.0 %collective-permute-start.29 = (f32[8,128]{1,0:T(8,128)S(1)}, f32[8,128]{1,0:T(8,128)S(1)}, u32[]{:S(2)}, u32[]{:S(2)}) collective-permute-start(f32[8,128]{1,0:T(8,128)S(1)} %get-tuple-element.56.refs_0_), channel_id=1, source_target_pairs={{0,24},{8,16},{16,8},{24,0},{1,25},{9,17},{17,9},{25,1},{2,26},{10... | collective-permute-start | bytes 12296 | tf_op jit(solution)/shard_map/sum_loss/ppermute | solution.py:246
  61.5 3.6 %collective-permute-start.28 = (f32[8,128]{1,0:T(8,128)S(1)}, f32[8,128]{1,0:T(8,128)S(1)}, u32[]{:S(2)}, u32[]{:S(2)}) collective-permute-start(f32[8,128]{1,0:T(8,128)S(1)} %get-tuple-element.56.refs_0_), channel_id=1, source_target_pairs={{0,16},{8,24},{16,0},{24,8},{1,17},{9,25},{17,1},{25,9},{2,18},{10... | collective-permute-start | bytes 12296 | tf_op jit(solution)/shard_map/sum_loss/ppermute | solution.py:246
  63.0 2.1 %collective-permute-start.27 = (f32[8,128]{1,0:T(8,128)S(1)}, f32[8,128]{1,0:T(8,128)S(1)}, u32[]{:S(2)}, u32[]{:S(2)}) collective-permute-start(f32[8,128]{1,0:T(8,128)S(1)} %get-tuple-element.56.refs_0_), channel_id=1, source_target_pairs={{0,8},{8,0},{16,24},{24,16},{1,9},{9,1},{17,25},{25,17},{2,10},{10... | collective-permute-start | bytes 12296 | tf_op jit(solution)/shard_map/sum_loss/ppermute | solution.py:246

commit v3 on v2

v3 whole, which is shorter than its diff:
```python
import functools

import jax
import jax.numpy as jnp
from jax import lax
from jax.experimental import pallas as pl
from jax.experimental.pallas import tpu as pltpu
from jax.sharding import PartitionSpec as P

F32 = jnp.float32
BF16 = jnp.bfloat16
SUB = 512


def two(x):
    hi = x.astype(BF16)
    return hi, (x - hi.astype(F32)).astype(BF16)


def three(x):
    hi = x.astype(BF16)
    rest = x - hi.astype(F32)
    mid = rest.astype(BF16)
    return hi, mid, (rest - mid.astype(F32)).astype(BF16)


def mm(a, b, ca, cb):
    return lax.dot_general(a, b, (((ca,), (cb,)), ((), ())), preferred_element_type=F32)


def rank_rows(k, rows):
    return pl.ds(pl.multiple_of(k * rows, rows), rows)


def stage_body(light_in, quality_in, cad_in, light, quality, cad, sem):
    copies = [
        pltpu.make_async_copy(cad_in, cad, sem.at[0]),
        pltpu.make_async_copy(quality_in, quality, sem.at[1]),
        pltpu.make_async_copy(light_in, light, sem.at[2]),
    ]
    for copy in copies:
        copy.start()
    for copy in copies:
        copy.wait()


def stage(light, quality, cad_t):
    given = (light, quality, cad_t)
    return pl.pallas_call(
        stage_body,
        in_specs=[pl.BlockSpec(memory_space=pl.ANY)] * 3,
        out_specs=[pl.BlockSpec(memory_space=pltpu.VMEM)] * 3,
        out_shape=[jax.ShapeDtypeStruct(x.shape, x.dtype) for x in given],
        scratch_shapes=[pltpu.SemaphoreType.DMA((3,))],
        cost_estimate=pl.CostEstimate(flops=0, bytes_accessed=1 << 10, transcendentals=0),
        compiler_params=pltpu.CompilerParams(vmem_limit_bytes=16 << 20),
    )(*given)


def place_cads(whole, cads, cad_slot):
    rows = cads[0].shape[0]
    for k, ref in enumerate(cads):
        whole[rank_rows(cad_slot(k), rows), :] = ref[...]


def of_slots(whole, star_slot, slots, rows):
    return jnp.concatenate([whole[rank_rows(star_slot(k), rows), :] for k in slots], 0)


def columns(refs, start, size):
    return jnp.concatenate([ref[:, pl.ds(start, size)] for ref in refs], 0)


def product_left(s):
    hi, mid, lo = three(s)
    return jnp.concatenate([hi, lo, mid, mid, hi, hi], 0)


def product_right(c):
    hi, mid, lo = three(c)
    return jnp.concatenate([lo, hi, hi, mid, hi, mid], 0)


def early_body(plan, *refs):
    star_slot, cad_slot, slots, n_cad = plan
    light, refs = refs[0], refs[1:]
    stars, cads = refs[: len(slots)], refs[len(slots) : len(slots) + n_cad]
    out, whole = refs[-2:]
    rows = stars[0].shape[0]
    place_cads(whole, cads, cad_slot)
    pad = -rows * len(slots) % 128
    block = of_slots(whole, star_slot, slots, rows)
    if pad:
        block = jnp.concatenate([block, jnp.zeros((pad, block.shape[1]), F32)], 0)
    right = product_right(block)
    for start in range(0, light.shape[0], SUB):
        s = columns(stars, start, SUB)
        if pad:
            s = jnp.concatenate([s, jnp.zeros((pad, SUB), F32)], 0)
        hi, mid, lo = three(s.T)
        left = jnp.concatenate([hi, lo, mid, mid, hi, hi], 1)
        at = pl.ds(start, SUB)
        out[at, :] = light[at, :] - mm(left, right, 1, 0)


def cells_body(plan, *refs):
    scale, star_slot, cad_slot, late, lead, n_cad, offset, first, last = plan
    refs = list(refs)
    take = lambda count: [refs.pop(0) for _ in range(count)]
    rest, quality = take(2)
    stars, cads = take(len(late)), take(n_cad)
    before = [] if first else take(1 + len(lead))
    whi_out, wlo_out, loss_out = take(3)
    terms = take(len(lead))
    whole, lacc = refs
    width = whi_out.shape[0]
    good = quality[...].astype(F32)
    place_cads(whole, cads, cad_slot)
    rows = stars[0].shape[0] if late else 0
    right = product_right(of_slots(whole, star_slot, late, rows)) if late else None
    ghi, glo = two(of_slots(whole, star_slot, lead, rows) * (good * scale)) if lead else (None, None)
    gt = jnp.concatenate([glo.T, ghi.T, ghi.T], 0) if lead else None
    lacc[...] = jnp.zeros_like(lacc) if first else before[0][...]
    for start in range(0, width, SUB):
        at = pl.ds(start, SUB)
        residual = rest[pl.ds(offset + start, SUB), :]
        if late:
            s = jnp.concatenate([r[:, pl.ds((offset if r.shape[1] > width else 0) + start, SUB)] for r in stars], 0)
            residual = residual - mm(product_left(s), right, 0, 0)
        ratio = 1.0 + (residual * 0.5) ** 2
        whi, wlo = two(residual / ratio)
        whi_out[at, :], wlo_out[at, :] = whi, wlo
        if lead:
            term = mm(jnp.concatenate([whi, wlo, whi], 1), gt, 1, 0).T
            for k, ref in enumerate(terms):
                to = pl.ds(start if first else width + start, SUB)
                ref[:, to] = term[k * rows : (k + 1) * rows]
        q = SUB // 4
        prod = (ratio[:q] * ratio[q : 2 * q]) * (ratio[2 * q : 3 * q] * ratio[3 * q :])
        lacc[...] += jnp.sum(jnp.log(prod).reshape(q // 8, 8, -1), 0)
    if not last:
        loss_out[...] = lacc[...]
        return
    sums = lacc[...] * good
    lanes = sum(sums[:, c : c + 128] for c in range(0, sums.shape[1], 128))
    loss_out[...] = lanes
    for ref, half in zip(terms, before[1:], strict=True):
        ref[:, :width] = half[...]
        put_lanes(ref, lanes)


def put_lanes(ref, lanes):
    ref[:8, ref.shape[1] - 128 :] = lanes
    ref[8:, ref.shape[1] - 128 :] = jnp.zeros((ref.shape[0] - 8, 128), F32)


def sums_body(plan, *refs):
    scale, cad_scale, star_slot, cad_slot, slots, n_star, n_cad, chunks = plan
    refs = list(refs)
    take = lambda count: [refs.pop(0) for _ in range(count)]
    parts, loss, quality = take(2 * chunks), take(1)[0], take(1)[0]
    stars, halves, cads = take(n_star), take(chunks - 1), take(n_cad)
    outs = take(len(slots))
    keep, send, whole, acc = refs
    rows, crows = stars[0].shape[0], cads[0].shape[0]
    width = parts[0].shape[0]
    good = quality[...].astype(F32)
    place_cads(whole, cads, cad_slot)
    ghi, glo = two(of_slots(whole, star_slot, slots, rows) * (good * scale))
    gt = jnp.concatenate([glo.T, ghi.T, ghi.T], 0)
    acc[...] = jnp.zeros_like(acc)
    for c in range(chunks):
        pieces = list(stars)
        if c:
            pieces[n_star // 2] = halves[c - 1]
        for start in range(0, width, SUB):
            at = pl.ds(start, SUB)
            whi, wlo = parts[2 * c][at, :], parts[2 * c + 1][at, :]
            term = mm(jnp.concatenate([whi, wlo, whi], 1), gt, 1, 0).T
            for k, ref in enumerate(outs):
                ref[:, pl.ds(c * width + start, SUB)] = term[k * rows : (k + 1) * rows]
            s = jnp.concatenate([r[:, pl.ds((c * width if r.shape[1] > width else 0) + start, SUB)] for r in pieces], 0)
            shi, slo = two(s)
            acc[...] += mm(jnp.concatenate([slo, shi, shi], 1), jnp.concatenate([whi, wlo, whi], 0), 1, 0)
    if chunks > 1:
        for ref in outs:
            put_lanes(ref, loss[...])
    for k in range(n_star):
        whole[rank_rows(star_slot(k), rows), :] = acc[k * rows : (k + 1) * rows]
    mine = max(n_cad // 2, 1)
    for k in range(n_cad):
        ref, place = (keep, k) if k < mine else (send, k - mine)
        ref[pl.ds(place * crows, crows), :] = whole[rank_rows(cad_slot(k), crows), :] * (good * cad_scale)


def big_call(body_of, given, out_shape, scratch, macs):
    vmem = pl.BlockSpec(memory_space=pltpu.VMEM)
    return pl.pallas_call(
        body_of,
        in_specs=[vmem] * len(given),
        out_specs=[vmem] * len(out_shape),
        out_shape=out_shape,
        scratch_shapes=scratch,
        compiler_params=pltpu.CompilerParams(vmem_limit_bytes=24 << 20),
        cost_estimate=pl.CostEstimate(flops=2 * macs, bytes_accessed=1 << 20, transcendentals=0),
    )(*given)


def sds(*shape, kind=F32):
    return jax.ShapeDtypeStruct(shape, kind)


def early(light, stars, cads, star_slot, cad_slot, slots):
    count, nc = light.shape
    rank = cads[0].shape[0] * len(cads)
    plan = (star_slot, cad_slot, slots, len(cads))
    scratch = [pltpu.VMEM((rank, nc), F32)]
    return big_call(functools.partial(early_body, plan), [light] + stars + cads, [sds(count, nc)], scratch, 6 * count * nc * rank)[0]


def cells(rest, quality, stars, cads, before, scale, star_slot, cad_slot, late, lead, chunk, chunks):
    count, nc = rest.shape
    width = count // chunks
    rank = cads[0].shape[0] * len(cads)
    rows = stars[0].shape[0] if stars else 0
    first, last = chunk == 0, chunk == chunks - 1
    plan = (scale, star_slot, cad_slot, late, lead, len(cads), chunk * width, first, last)
    out = [sds(width, nc, kind=BF16)] * 2 + [sds(8, 128) if last else sds(8, nc)]
    out += [sds(rows, width if first else count + 128)] * len(lead)
    scratch = [pltpu.VMEM((rank, nc), F32), pltpu.VMEM((8, nc), F32)]
    return list(big_call(functools.partial(cells_body, plan), [rest, quality] + stars + cads + before, out, scratch, 4 * width * nc * rank))


def sums(parts, loss, quality, stars, halves, cads, scale, cad_scale, star_slot, cad_slot, slots):
    chunks, nc = len(parts) // 2, parts[0].shape[1]
    count = parts[0].shape[0] * chunks
    n_star, n_cad = len(stars), len(cads)
    rows, crows = stars[0].shape[0], cads[0].shape[0]
    rank = rows * n_star
    mine = max(n_cad // 2, 1)
    plan = (scale, cad_scale, star_slot, cad_slot, slots, n_star, n_cad, chunks)
    out = [sds(rows, count + (128 if chunks > 1 else 0))] * len(slots)
    out += [sds(crows * mine, nc), sds(crows * max(n_cad - mine, 1), nc)]
    scratch = [pltpu.VMEM((rank, nc), F32), pltpu.VMEM((rank, nc), F32)]
    given = parts + [loss, quality] + stars + halves + cads
    return list(big_call(functools.partial(sums_body, plan), given, out, scratch, 6 * count * nc * rank))


def small_call(body_of, given, shapes, limit=4):
    vmem = pl.BlockSpec(memory_space=pltpu.VMEM)
    return pl.pallas_call(
        body_of,
        in_specs=[vmem] * len(given),
        out_specs=[vmem] * len(shapes),
        out_shape=[jax.ShapeDtypeStruct(shape, F32) for shape in shapes],
        cost_estimate=pl.CostEstimate(flops=0, bytes_accessed=1 << 10, transcendentals=0),
        compiler_params=pltpu.CompilerParams(vmem_limit_bytes=limit << 20),
    )(*given)


def empty_body(*refs):
    pass


def hold(x, *after):
    anywhere = pl.BlockSpec(memory_space=pl.ANY)
    return pl.pallas_call(
        empty_body,
        in_specs=[anywhere] * (1 + len(after)),
        out_specs=anywhere,
        out_shape=jax.ShapeDtypeStruct(x.shape, x.dtype),
        input_output_aliases={0: 0},
        cost_estimate=pl.CostEstimate(flops=0, bytes_accessed=1 << 10, transcendentals=0),
        compiler_params=pltpu.CompilerParams(vmem_limit_bytes=1 << 20),
    )(x, *after)


def halve_body(keep, got, keep_out, send_out):
    rows = keep_out.shape[0]
    keep_out[...] = keep[:rows] + got[:rows]
    send_out[...] = keep[rows:] + got[rows:]


def halve(keep, got):
    shape = (keep.shape[0] // 2, keep.shape[1])
    return small_call(halve_body, [keep, got], [shape, shape])


def add_part_body(mine, got, out, part):
    out[...] = mine[...] + got[...]
    part[...] = out[:8, out.shape[1] - 128 :]


def add_part(mine, got):
    return small_call(add_part_body, [mine, got], [mine.shape, (8, 128)])


def loss_part_body(loss, near, beside, out):
    out[...] = loss[...] + near[...] + beside[:8, beside.shape[1] - 128 :]


def loss_part(loss, near, beside):
    return small_call(loss_part_body, [loss, near, beside], [(8, 128)])[0]


def last_stars_body(factor, mine, up, back, *refs):
    *losses, out, total = refs
    width = out.shape[1]
    out[...] = mine[:, :width] + up[:, :width] + back[:, :width]
    total[...] = jnp.sum(sum(ref[...] for ref in losses), keepdims=True) * factor


def last_stars(mine, up, back, losses, factor):
    rows, width = mine.shape
    shapes = [(rows, width - 128), (1, 1)]
    return small_call(functools.partial(last_stars_body, factor), [mine, up, back] + losses, shapes)


def ring_order(n):
    return list(range(0, n, 2)) + list(range(1, n, 2))[::-1]


def shift(x, core=0, places=1):
    m, n = lax.axis_size("star"), lax.axis_size("cad")
    order = ring_order(n)
    pairs = []
    for i in range(m):
        way = places if i % 2 == 0 else -places
        source, target = i ^ int(core < 0), i ^ int(core > 0)
        pairs += [(source * n + order[p], target * n + order[(p + way) % n]) for p in range(n)]
    return lax.ppermute(x, ("star", "cad"), pairs)


def swap(x, axis, bit):
    return lax.ppermute(x, axis, [(i, i ^ bit) for i in range(lax.axis_size(axis))])


def ring_program(light, quality, star_t, cad_t):
    n, m = lax.axis_size("cad"), lax.axis_size("star")
    count, nc = light.shape
    half = count // 2
    scale = -1.0 / float(nc * n) ** 0.5
    cad_scale = -1.0 / float(count * m) ** 0.5
    factor = 2.0 / (float(count * m) * float(nc * n))

    def star_slot(k):
        me = lax.axis_index("cad")
        place = jnp.where(me % 2 == 0, me // 2, n - 1 - me // 2)
        back = jnp.where(lax.axis_index("star") % 2 == 0, n - k, k)
        source = lax.rem(place + back, n)
        return jnp.where(source < n // 2, 2 * source, 2 * (n - 1 - source) + 1)

    def cad_slot(k):
        return jnp.bitwise_xor(lax.axis_index("star"), k)

    light, quality, cad_t = stage(light, quality.reshape(1, -1), cad_t)

    with jax.named_scope("gather_cadence_factors"):
        cads = [cad_t] + [swap(cad_t, "star", bit) for bit in range(1, m)]

    far = n // 2
    pieces = [star_t] + [None] * (n - 1)
    with jax.named_scope("gather_star_factors"):
        beside = swap(star_t, "star", 1)
        for s in range(1, far):
            pieces[s] = shift(pieces[s - 1])
            if s == 1:
                beside = shift(beside)
                pieces[s], beside = hold(pieces[s], light), hold(beside, light)
            elif s < far - 1:
                beside = shift(beside)
                pieces[s] = hold(pieces[s], *cads[1:])
            else:
                beside = shift(beside, 1)
            pieces[n - s] = swap(beside, "star", 1) if s < far - 1 else beside
        far_a, far_b = shift(pieces[far - 1][:, :half]), shift(pieces[far - 1][:, half:])

    slots = [k for k in range(n) if k not in (far, far + 1)]
    rest = early(light, [pieces[k] for k in slots], cads, star_slot, cad_slot, slots)
    late, lead = [far, far + 1], [far, far - 1, far - 2]
    got_a = cells(rest, quality, [far_a, pieces[far + 1]], cads, [], scale, star_slot, cad_slot, late, lead, 0, 2)
    got_b = cells(rest, quality, [far_b, pieces[far + 1]], cads, got_a[2:], scale, star_slot, cad_slot, late, lead, 1, 2)
    loss = got_b[2]
    pieces[far] = far_a
    slots = [k for k in range(n) if k not in lead]
    second, third = swap(got_b[4], "star", 1), swap(got_b[5], "star", 1)
    loss = hold(loss, second)
    got = sums(got_a[:2] + got_b[:2], loss, quality, pieces, [far_b], cads, scale, cad_scale, star_slot, cad_slot, slots)
    terms = dict(zip(lead + slots, got_b[3:] + got[:-2], strict=True))
    keep, send = got[-2:]

    with jax.named_scope("scatter_star_gradient"):
        up, beside = shift(terms[far]), shift(second)
        up = shift(terms[far + 1] + up)
        message = third + beside
        keep, send = halve(keep, swap(hold(send, message), "star", 2))
        beside = shift(message)
        up = shift(hold(terms[far + 2] + up, message))
        cad_gradient = keep + swap(send, "star", 1)
        message = hold(swap(terms[1], "star", 1) + beside, keep)
        beside = shift(message)
        message, near = add_part(terms[far + 3], hold(up, message))
        near = shift(near)
        up = shift(message)
        back = swap(hold(beside, cad_gradient), "star", 1)
        part = loss_part(loss, near, beside)
        losses = [part] + [swap(part, "star", bit) for bit in range(1, m)]
        star_gradient, total = last_stars(terms[0], up, back, losses, factor)
    return (star_gradient.T, cad_gradient.T, total[0, 0])


def whole_program(light, quality, star_t, cad_t):
    n, m = lax.axis_size("cad"), lax.axis_size("star")
    count, nc = light.shape
    scale = -1.0 / float(nc * n) ** 0.5
    cad_scale = -1.0 / float(count * m) ** 0.5
    stars = [lax.all_gather(star_t, "cad", axis=0, tiled=True)]
    cads = [lax.all_gather(cad_t, "star", axis=0, tiled=True)]
    first = lambda k: 0
    light = early(light, stars, cads, first, first, [0])
    whi, wlo, loss = cells(light, quality.reshape(1, -1), [], cads, [], scale, first, first, [], [], 0, 1)
    parts = [whi, wlo]
    star, cad, _ = sums(parts, loss, quality.reshape(1, -1), stars, [], cads, scale, cad_scale, first, first, [0])
    star_gradient = lax.psum_scatter(star, "cad", scatter_dimension=0, tiled=True)
    cadence_gradient = lax.psum_scatter(cad, "star", scatter_dimension=0, tiled=True)
    loss = lax.psum(jnp.sum(loss), ("star", "cad")) * (2.0 / (float(count * m) * float(nc * n)))
    return (star_gradient.T, cadence_gradient.T, loss)


def on_device(light, quality, star_factors, cadence_factors):
    ring = lax.axis_size("cad") == 8 and lax.axis_size("star") == 4
    program = ring_program if ring else whole_program
    return program(light, quality, star_factors.T, cadence_factors.T)


def solution(mesh):
    in_specs = (P("star", "cad"), P("cad"), P("star", "cad"), P("cad", "star"))
    out_specs = (P("star", "cad"), P("cad", "star"), P())
    return jax.shard_map(
        on_device, mesh=mesh, in_specs=in_specs, out_specs=out_specs, check_vma=False
    )
```

time: 66 us -> 60.7 us (0.920)
  waiting for transfers between devices: 22.6 us -> 13.8 us
  starting transfers between devices: 30.5 us -> 32.5 us
  Pallas kernels: 7.99 us -> 9.56 us
    ppermute x15, waiting for transfers between devices: 7.18 us -> 2.74 us  [swap(): lax.ppermute(x, axis, [(i, i ^ bit) for i in range(lax.axis_size(axis))])]
    ppermute x15 -> x16, waiting for transfers between devices: 15.4 us -> 11.1 us  [shift(): return lax.ppermute(x, ('star', 'cad'), pairs)]
    pallas_call x2 -> x4, Pallas kernels: 6.26 us -> 8.43 us  [big_call(): pl.pallas_call(body_of, in_specs=[vmem] * len(given), out_specs=[vmem] *...]
    ppermute x15 -> x16, starting transfers between devices: 24.8 us -> 26.4 us  [shift(): return lax.ppermute(x, ('star', 'cad'), pairs)]
    pallas_call x3 -> x4, Pallas kernels: 1.4 us -> 0.8 us  [small_call(): pl.pallas_call(body_of, in_specs=[vmem] * len(given), out_specs=[vmem] *...]
  transfers between devices with their start and end apart: 30 -> 31, of which waited for: 15 -> 13; matrix products, arithmetic and copies ran while one was open for 0% -> 0% of each run, Pallas kernels for 5% -> 11%
where the time goes in v3:
time: 60.7 us; the launch traced here: 60.5 us
  starting transfers between devices  32.5 us (54%)
  waiting for transfers between devices  13.8 us (23%)
  Pallas kernels  9.56 us (16%)
  local copies, waits for them, and re-layouts  3.65 us (6%)
  between operations  0.8 us (1%)
    ppermute x16, starting transfers between devices, shift(): return lax.ppermute(x, ('star', 'cad'), pairs)  26.4 us
    ppermute x16, waiting for transfers between devices, shift(): return lax.ppermute(x, ('star', 'cad'), pairs)  11.1 us
    pallas_call x4, Pallas kernels, big_call(): pl.pallas_call(body_of, in_specs=[vmem] * len(given), out_specs=[vmem] *...  8.43 us
    ppermute x15, starting transfers between devices, swap(): lax.ppermute(x, axis, [(i, i ^ bit) for i in range(lax.axis_size(axis))])  6.04 us
    unnamed x10, local copies, waits for them, and re-layouts  3.64 us
    ppermute x15, waiting for transfers between devices, swap(): lax.ppermute(x, axis, [(i, i ^ bit) for i in range(lax.axis_size(axis))])  2.74 us
  transfers between devices with their start and end apart: 31, of which 13 were waited for; matrix products, arithmetic and copies ran while one was open for 0% of the time, Pallas kernels for 11%

profile of v3, /device:TPU:0, one launch (start us, length us, event | category | flops | bytes accessed | tf_op | source)
XLA Modules:
  0.0 60.5 jit_solution(8043116148144357675)
XLA Ops:
  0.6 0.5 collective-permute-start.6
  1.1 2.6 %collective-permute-start = (f32[16,4096]{1,0:T(8,128)}, f32[16,4096]{1,0:T(8,128)S(1)}, u32[]{:S(2)}, u32[]{:S(2)}) collective-permute-start(f32[16,4096]{1,0:T(8,128)} %bitcast.7), channel_id=1, source_target_pairs={{0,2},{2,4},{4,6},{6,7},{7,5},{5,3},{3,1},{1,0},{8,9},{10,8},{12,1... | collective-permute-start | bytes 786440 | tf_op jit(solution)/shard_map/gather_star_factors/ppermute | solution.py:331
  3.8 1.7 %collective-permute-start.7 = (f32[16,4096]{1,0:T(8,128)S(1)}, f32[16,4096]{1,0:T(8,128)S(1)}, u32[]{:S(2)}, u32[]{:S(2)}) collective-permute-start(f32[16,4096]{1,0:T(8,128)S(1)} %collective-permute-done.6), channel_id=1, source_target_pairs={{0,2},{2,4},{4,6},{6,7},{7,5},{5,3},{3,1},{1,0},{8,9},{10,8},{12,1... | collective-permute-start | bytes 786440 | tf_op jit(solution)/shard_map/gather_star_factors/ppermute | solution.py:331
  5.5 2.2 %copy-done = f32[4096,256]{1,0:T(8,128)S(1)} copy-done((f32[4096,256]{1,0:T(8,128)S(1)}, f32[4096,256]{1,0:T(8,128)}, u32[]{:S(2)}) %copy-start) | copy-done | bytes 4194328
  7.7 0.8 %copy-done.3 = f32[256,32]{0,1:T(8,128)S(1)} copy-done((f32[256,32]{0,1:T(8,128)S(1)}, f32[256,32]{0,1:T(8,128)}, u32[]{:S(2)}) %copy-start.3) | copy-done | bytes 32792
  8.4 0.7 %copy-done.4 = s32[256]{0:T(256)S(1)} copy-done((s32[256]{0:T(256)S(1)}, s32[256]{0:T(256)}, u32[]{:S(2)}) %copy-start.4) | copy-done | bytes 1048
  9.1 0.3 shard_map.67
  9.4 0.0 copy-start.1
  9.5 1.6 %collective-permute-start.1 = (f32[16,4096]{1,0:T(8,128)S(1)}, f32[16,4096]{1,0:T(8,128)S(1)}, u32[]{:S(2)}, u32[]{:S(2)}) collective-permute-start(f32[16,4096]{1,0:T(8,128)S(1)} %gather_star_factors.3.refs_2_.refs_7_), channel_id=1, source_target_pairs={{0,2},{2,4},{4,6},{6,7},{7,5},{5,3},{3,1},{1,0},{8,9},{10,8},{12,1... | collective-permute-start | bytes 786440 | tf_op jit(solution)/shard_map/gather_star_factors/ppermute | solution.py:331
  11.1 1.5 %collective-permute-start.3 = (f32[32,256]{1,0:T(8,128)S(1)}, f32[32,256]{1,0:T(8,128)S(1)}, u32[]{:S(2)}, u32[]{:S(2)}) collective-permute-start(f32[32,256]{1,0:T(8,128)S(1)} %get-tuple-element.32.refs_7_.refs_4_.refs_15_), channel_id=1, source_target_pairs={{0,16},{8,24},{16,0},{24,8},{1,17},{9,25},{17,1},{25,9},{2,18},{10... | collective-permute-start | bytes 98312 | tf_op jit(solution)/shard_map/gather_cadence_factors/ppermute | solution.py:335
  12.6 0.3 collective-permute-start.4
  12.9 1.6 %collective-permute-start.8 = (f32[16,4096]{1,0:T(8,128)S(1)}, f32[16,4096]{1,0:T(8,128)S(1)}, u32[]{:S(2)}, u32[]{:S(2)}) collective-permute-start(f32[16,4096]{1,0:T(8,128)S(1)} %gather_star_factors.5), channel_id=1, source_target_pairs={{0,2},{2,4},{4,6},{6,7},{7,5},{5,3},{3,1},{1,0},{8,9},{10,8},{12,1... | collective-permute-start | bytes 786440 | tf_op jit(solution)/shard_map/gather_star_factors/ppermute | solution.py:331
  14.5 0.5 collective-permute-done.3.refs_2_.refs_9_.refs_6_.refs_17_
  15.0 0.9 %collective-permute-done.4.refs_3_.refs_10_.refs_7_.refs_18_ = f32[32,256]{1,0:T(8,128)S(1)} collective-permute-done((f32[32,256]{1,0:T(8,128)S(1)}, f32[32,256]{1,0:T(8,128)S(1)}, u32[]{:S(2)}, u32[]{:S(2)}) %collective-permute-start.4) | collective-permute-done | bytes 32800 | tf_op jit(solution)/shard_map/gather_cadence_factors/ppermute | solution.py:335
  15.9 1.6 %collective-permute-start.5 = (f32[16,4096]{1,0:T(8,128)S(1)}, f32[16,4096]{1,0:T(8,128)S(1)}, u32[]{:S(2)}, u32[]{:S(2)}) collective-permute-start(f32[16,4096]{1,0:T(8,128)S(1)} %gather_star_factors.4.refs_3_.refs_8_), channel_id=1, source_target_pairs={{0,2},{2,4},{4,6},{6,7},{7,5},{5,3},{3,1},{1,0},{8,9},{10,8},{12,1... | collective-permute-start | bytes 786440 | tf_op jit(solution)/shard_map/gather_star_factors/ppermute | solution.py:331
  17.5 1.8 %collective-permute-done.8 = f32[16,4096]{1,0:T(8,128)S(1)} collective-permute-done((f32[16,4096]{1,0:T(8,128)S(1)}, f32[16,4096]{1,0:T(8,128)S(1)}, u32[]{:S(2)}, u32[]{:S(2)}) %collective-permute-start.8) | collective-permute-done | bytes 262176 | tf_op jit(solution)/shard_map/gather_star_factors/ppermute | solution.py:331
  19.3 1.7 %collective-permute-start.12 = (f32[16,4096]{1,0:T(8,128)S(1)}, f32[16,4096]{1,0:T(8,128)S(1)}, u32[]{:S(2)}, u32[]{:S(2)}) collective-permute-start(f32[16,4096]{1,0:T(8,128)S(1)} %collective-permute-done.8), channel_id=1, source_target_pairs={{0,10},{2,12},{4,14},{6,15},{7,13},{5,11},{3,9},{1,8},{8,1},{10,0}... | collective-permute-start | bytes 786440 | tf_op jit(solution)/shard_map/gather_star_factors/ppermute | solution.py:331
  21.0 1.3 %collective-permute-done.5.refs_4_.refs_9_ = f32[16,4096]{1,0:T(8,128)S(1)} collective-permute-done((f32[16,4096]{1,0:T(8,128)S(1)}, f32[16,4096]{1,0:T(8,128)S(1)}, u32[]{:S(2)}, u32[]{:S(2)}) %collective-permute-start.5) | collective-permute-done | bytes 262176 | tf_op jit(solution)/shard_map/gather_star_factors/ppermute | solution.py:331
  22.3 1.6 %collective-permute-start.11 = (f32[16,2048]{1,0:T(8,128)S(1)}, f32[16,2048]{1,0:T(8,128)S(1)}, u32[]{:S(2)}, u32[]{:S(2)}) collective-permute-start(f32[16,2048]{1,0:T(8,128)S(1)} %get-tuple-element.60), channel_id=1, source_target_pairs={{0,2},{2,4},{4,6},{6,7},{7,5},{5,3},{3,1},{1,0},{8,9},{10,8},{12,1... | collective-permute-start | bytes 393224 | tf_op jit(solution)/shard_map/gather_star_factors/ppermute | solution.py:331
  24.0 1.5 %collective-permute-start.13 = (f32[16,2048]{1,0:T(8,128)S(1)}, f32[16,2048]{1,0:T(8,128)S(1)}, u32[]{:S(2)}, u32[]{:S(2)}) collective-permute-start(f32[16,2048]{1,0:T(8,128)S(1)} %get-tuple-element.59), channel_id=1, source_target_pairs={{0,2},{2,4},{4,6},{6,7},{7,5},{5,3},{3,1},{1,0},{8,9},{10,8},{12,1... | collective-permute-start | bytes 393224 | tf_op jit(solution)/shard_map/gather_star_factors/ppermute | solution.py:331
  25.5 1.9 %shard_map.68.refs_0_ = f32[4096,256]{1,0:T(8,128)S(1)} custom-call(f32[4096,256]{1,0:T(8,128)S(1)} %get-tuple-element.31.refs_1_.refs_0_, f32[16,4096]{1,0:T(8,128)S(1)} %bitcast.8, f32[16,4096]{1,0:T(8,128)S(1)} %gather_star_factors.3.refs_2_.refs_7_, f32[16,4096]{1,0:T(8,128)S(1)} %gather_star_factors.4.refs_3_.refs_8_, ...), custom_call_target="tpu_custom_call" | custom-call | flops 1610612736 | bytes 1048576 | tf_op jit(solution)/shard_map/pallas_call | solution.py:198
  27.4 1.9 %shard_map.69 = (bf16[2048,256]{1,0:T(8,128)(2,1)S(1)}, bf16[2048,256]{1,0:T(8,128)(2,1)S(1)}, f32[8,256]{1,0:T(8,128)S(1)}, f32[16,2048]{1,0:T(8,128)S(1)}, f32...) custom-call(f32[4096,256]{1,0:T(8,128)S(1)} %shard_map.68.refs_0_, s32[1,256]{1,0:T(1,128)S(1)} %get-tuple-element.33.refs_1_.refs_5_, ...), custom_call_target="tpu_custom_call" | custom-call | flops 536870912 | bytes 1048576 | tf_op jit(solution)/shard_map/pallas_call | solution.py:198
  29.3 1.9 %shard_map.70 = (bf16[2048,256]{1,0:T(8,128)(2,1)S(1)}, bf16[2048,256]{1,0:T(8,128)(2,1)S(1)}, f32[8,128]{1,0:T(8,128)S(1)}, f32[16,4224]{1,0:T(8,128)S(1)}, f32...) custom-call(f32[4096,256]{1,0:T(8,128)S(1)} %shard_map.68.refs_0_, s32[1,256]{1,0:T(1,128)S(1)} %get-tuple-element.33.refs_1_.refs_5_, ...), custom_call_target="tpu_custom_call" | custom-call | flops 536870912 | bytes 1048576 | tf_op jit(solution)/shard_map/pallas_call | solution.py:198
  31.2 0.1 collective-permute-start.14
  31.2 1.6 %collective-permute-start.15 = (f32[16,4224]{1,0:T(8,128)S(1)}, f32[16,4224]{1,0:T(8,128)S(1)}, u32[]{:S(2)}, u32[]{:S(2)}) collective-permute-start(f32[16,4224]{1,0:T(8,128)S(1)} %get-tuple-element.48), channel_id=1, source_target_pairs={{0,2},{2,4},{4,6},{6,7},{7,5},{5,3},{3,1},{1,0},{8,9},{10,8},{12,1... | collective-permute-start | bytes 811016 | tf_op jit(solution)/shard_map/scatter_star_gradient/ppermute | solution.py:331
  32.8 1.5 %collective-permute-start.18 = (f32[16,4224]{1,0:T(8,128)S(1)}, f32[16,4224]{1,0:T(8,128)S(1)}, u32[]{:S(2)}, u32[]{:S(2)}) collective-permute-start(f32[16,4224]{1,0:T(8,128)S(1)} %collective-permute-done.14.refs_1_), channel_id=1, source_target_pairs={{0,2},{2,4},{4,6},{6,7},{7,5},{5,3},{3,1},{1,0},{8,9},{10,8},{12,1... | collective-permute-start | bytes 811016 | tf_op jit(solution)/shard_map/scatter_star_gradient/ppermute | solution.py:331
  34.3 2.8 %shard_map.72 = (f32[16,4224]{1,0:T(8,128)S(1)}, f32[16,4224]{1,0:T(8,128)S(1)}, f32[16,4224]{1,0:T(8,128)S(1)}, f32[16,4224]{1,0:T(8,128)S(1)}, f32[16,4224]{1,...) custom-call(bf16[2048,256]{1,0:T(8,128)(2,1)S(1)} %get-tuple-element.34.refs_0_, ...), custom_call_target="tpu_custom_call" | custom-call | flops 1610612736 | bytes 1048576 | tf_op jit(solution)/shard_map/pallas_call | solution.py:198
  37.1 0.6 %collective-permute-done.15 = f32[16,4224]{1,0:T(8,128)S(1)} collective-permute-done((f32[16,4224]{1,0:T(8,128)S(1)}, f32[16,4224]{1,0:T(8,128)S(1)}, u32[]{:S(2)}, u32[]{:S(2)}) %collective-permute-start.15) | collective-permute-done | bytes 270368 | tf_op jit(solution)/shard_map/scatter_star_gradient/ppermute | solution.py:331
  37.8 1.6 %collective-permute-start.16 = (f32[16,4224]{1,0:T(8,128)S(1)}, f32[16,4224]{1,0:T(8,128)S(1)}, u32[]{:S(2)}, u32[]{:S(2)}) collective-permute-start(f32[16,4224]{1,0:T(8,128)S(1)} %add.15), channel_id=1, source_target_pairs={{0,2},{2,4},{4,6},{6,7},{7,5},{5,3},{3,1},{1,0},{8,9},{10,8},{12,1... | collective-permute-start | bytes 811016 | tf_op jit(solution)/shard_map/scatter_star_gradient/ppermute | solution.py:331
  39.4 1.3 %collective-permute-done.18 = f32[16,4224]{1,0:T(8,128)S(1)} collective-permute-done((f32[16,4224]{1,0:T(8,128)S(1)}, f32[16,4224]{1,0:T(8,128)S(1)}, u32[]{:S(2)}, u32[]{:S(2)}) %collective-permute-start.18) | collective-permute-done | bytes 270368 | tf_op jit(solution)/shard_map/scatter_star_gradient/ppermute | solution.py:331
  40.7 1.6 %collective-permute-start.21 = (f32[16,4224]{1,0:T(8,128)S(1)}, f32[16,4224]{1,0:T(8,128)S(1)}, u32[]{:S(2)}, u32[]{:S(2)}) collective-permute-start(f32[16,4224]{1,0:T(8,128)S(1)} %add.17.refs_1_), channel_id=1, source_target_pairs={{0,2},{2,4},{4,6},{6,7},{7,5},{5,3},{3,1},{1,0},{8,9},{10,8},{12,1... | collective-permute-start | bytes 811016 | tf_op jit(solution)/shard_map/scatter_star_gradient/ppermute | solution.py:331
  42.3 1.5 %collective-permute-start.22 = (f32[64,256]{1,0:T(8,128)S(1)}, f32[64,256]{1,0:T(8,128)S(1)}, u32[]{:S(2)}, u32[]{:S(2)}) collective-permute-start(f32[64,256]{1,0:T(8,128)S(1)} %scatter_star_gradient.10), channel_id=1, source_target_pairs={{0,16},{8,24},{16,0},{24,8},{1,17},{9,25},{17,1},{25,9},{2,18},{10... | collective-permute-start | bytes 196616 | tf_op jit(solution)/shard_map/scatter_star_gradient/ppermute | solution.py:335
  43.8 0.6 collective-permute-done.16
  44.4 1.6 %collective-permute-start.19 = (f32[16,4224]{1,0:T(8,128)S(1)}, f32[16,4224]{1,0:T(8,128)S(1)}, u32[]{:S(2)}, u32[]{:S(2)}) collective-permute-start(f32[16,4224]{1,0:T(8,128)S(1)} %scatter_star_gradient.9), channel_id=1, source_target_pairs={{0,2},{2,4},{4,6},{6,7},{7,5},{5,3},{3,1},{1,0},{8,9},{10,8},{12,1... | collective-permute-start | bytes 811016 | tf_op jit(solution)/shard_map/scatter_star_gradient/ppermute | solution.py:331
  45.9 0.6 collective-permute-done.22.got
  46.6 0.6 %collective-permute-done.21 = f32[16,4224]{1,0:T(8,128)S(1)} collective-permute-done((f32[16,4224]{1,0:T(8,128)S(1)}, f32[16,4224]{1,0:T(8,128)S(1)}, u32[]{:S(2)}, u32[]{:S(2)}) %collective-permute-start.21) | collective-permute-done | bytes 270368 | tf_op jit(solution)/shard_map/scatter_star_gradient/ppermute | solution.py:331
  47.2 1.6 %collective-permute-start.24 = (f32[16,4224]{1,0:T(8,128)S(1)}, f32[16,4224]{1,0:T(8,128)S(1)}, u32[]{:S(2)}, u32[]{:S(2)}) collective-permute-start(f32[16,4224]{1,0:T(8,128)S(1)} %scatter_star_gradient.12.refs_1_), channel_id=1, source_target_pairs={{0,2},{2,4},{4,6},{6,7},{7,5},{5,3},{3,1},{1,0},{8,9},{10,8},{12,1... | collective-permute-start | bytes 811016 | tf_op jit(solution)/shard_map/scatter_star_gradient/ppermute | solution.py:331
  48.8 2.0 %collective-permute-done.19.refs_0_ = f32[16,4224]{1,0:T(8,128)S(1)} collective-permute-done((f32[16,4224]{1,0:T(8,128)S(1)}, f32[16,4224]{1,0:T(8,128)S(1)}, u32[]{:S(2)}, u32[]{:S(2)}) %collective-permute-start.19) | collective-permute-done | bytes 270368 | tf_op jit(solution)/shard_map/scatter_star_gradient/ppermute | solution.py:331
  50.9 1.6 %collective-permute-start.27 = (f32[8,128]{1,0:T(8,128)S(1)}, f32[8,128]{1,0:T(8,128)S(1)}, u32[]{:S(2)}, u32[]{:S(2)}) collective-permute-start(f32[8,128]{1,0:T(8,128)S(1)} %get-tuple-element.56), channel_id=1, source_target_pairs={{0,2},{2,4},{4,6},{6,7},{7,5},{5,3},{3,1},{1,0},{8,9},{10,8},{12,1... | collective-permute-start | bytes 12296 | tf_op jit(solution)/shard_map/scatter_star_gradient/ppermute | solution.py:331
  52.5 0.0 copy-start.2
  52.5 1.6 %collective-permute-start.23 = (f32[16,4224]{1,0:T(8,128)S(1)}, f32[16,4224]{1,0:T(8,128)S(1)}, u32[]{:S(2)}, u32[]{:S(2)}) collective-permute-start(f32[16,4224]{1,0:T(8,128)S(1)} %get-tuple-element.54), channel_id=1, source_target_pairs={{0,2},{2,4},{4,6},{6,7},{7,5},{5,3},{3,1},{1,0},{8,9},{10,8},{12,1... | collective-permute-start | bytes 811016 | tf_op jit(solution)/shard_map/scatter_star_gradient/ppermute | solution.py:331
  54.1 0.5 collective-permute-done.27.near
  54.6 0.1 collective-permute-start.26
  54.7 0.5 collective-permute-start.28
  55.1 1.5 %collective-permute-start.29 = (f32[8,128]{1,0:T(8,128)S(1)}, f32[8,128]{1,0:T(8,128)S(1)}, u32[]{:S(2)}, u32[]{:S(2)}) collective-permute-start(f32[8,128]{1,0:T(8,128)S(1)} %scatter_star_gradient.16.refs_0_), channel_id=1, source_target_pairs={{0,16},{8,24},{16,0},{24,8},{1,17},{9,25},{17,1},{25,9},{2,18},{10... | collective-permute-start | bytes 12296 | tf_op jit(solution)/shard_map/scatter_star_gradient/ppermute | solution.py:335
  56.7 2.3 %collective-permute-done.23.up = f32[16,4224]{1,0:T(8,128)S(1)} collective-permute-done((f32[16,4224]{1,0:T(8,128)S(1)}, f32[16,4224]{1,0:T(8,128)S(1)}, u32[]{:S(2)}, u32[]{:S(2)}) %collective-permute-start.23) | collective-permute-done | bytes 270368 | tf_op jit(solution)/shard_map/scatter_star_gradient/ppermute | solution.py:331
  59.0 0.7 %collective-permute-done.30.refs_3_ = f32[8,128]{1,0:T(8,128)S(1)} collective-permute-done((f32[8,128]{1,0:T(8,128)S(1)}, f32[8,128]{1,0:T(8,128)S(1)}, u32[]{:S(2)}, u32[]{:S(2)}) %collective-permute-start.30) | collective-permute-done | bytes 4128 | tf_op jit(solution)/shard_map/scatter_star_gradient/ppermute | solution.py:335
  59.7 0.8 %scatter_star_gradient.17 = (f32[16,4096]{1,0:T(8,128)}, f32[1,1]{1,0:T(1,128)}) custom-call(f32[16,4224]{1,0:T(8,128)S(1)} %get-tuple-element.44.mine, f32[16,4224]{1,0:T(8,128)S(1)} %collective-permute-done.23.up, f32[16,4224]{1,0:T(8,128)S(1)} %collective-permute-done.26.back, f32[8,128]{1,0:T(8,128)S(1)} %scatter_star_gradient.16.refs_0_, ...), custom_call_target="tpu_custom_call" | custom-call | bytes 1024 | tf_op jit(solution)/shard_map/scatter_star_gradient/pallas_call | solution.py:251
  (48 shorter events, 0.3 us)
Async XLA Ops:
  0.6 3.2 %collective-permute-start.6 = (f32[16,4096]{1,0:T(8,128)}, f32[16,4096]{1,0:T(8,128)S(1)}, u32[]{:S(2)}, u32[]{:S(2)}) collective-permute-start(f32[16,4096]{1,0:T(8,128)} %bitcast.6), channel_id=1, source_target_pairs={{0,8},{8,0},{16,24},{24,16},{1,9},{9,1},{17,25},{25,17},{2,10},{10... | collective-permute-start | bytes 786440 | tf_op jit(solution)/shard_map/gather_star_factors/ppermute | solution.py:335
  1.1 8.3 %collective-permute-start = (f32[16,4096]{1,0:T(8,128)}, f32[16,4096]{1,0:T(8,128)S(1)}, u32[]{:S(2)}, u32[]{:S(2)}) collective-permute-start(f32[16,4096]{1,0:T(8,128)} %bitcast.7), channel_id=1, source_target_pairs={{0,2},{2,4},{4,6},{6,7},{7,5},{5,3},{3,1},{1,0},{8,9},{10,8},{12,1... | collective-permute-start | bytes 786440 | tf_op jit(solution)/shard_map/gather_star_factors/ppermute | solution.py:331
  3.8 9.2 %collective-permute-start.7 = (f32[16,4096]{1,0:T(8,128)S(1)}, f32[16,4096]{1,0:T(8,128)S(1)}, u32[]{:S(2)}, u32[]{:S(2)}) collective-permute-start(f32[16,4096]{1,0:T(8,128)S(1)} %collective-permute-done.6), channel_id=1, source_target_pairs={{0,2},{2,4},{4,6},{6,7},{7,5},{5,3},{3,1},{1,0},{8,9},{10,8},{12,1... | collective-permute-start | bytes 786440 | tf_op jit(solution)/shard_map/gather_star_factors/ppermute | solution.py:331
  5.5 2.2 %copy-start = (f32[4096,256]{1,0:T(8,128)S(1)}, f32[4096,256]{1,0:T(8,128)}, u32[]{:S(2)}) copy-start(f32[4096,256]{1,0:T(8,128)} %light_in.1) | copy-start | bytes 12582916
  7.7 0.8 %copy-start.3 = (f32[256,32]{0,1:T(8,128)S(1)}, f32[256,32]{0,1:T(8,128)}, u32[]{:S(2)}) copy-start(f32[256,32]{0,1:T(8,128)} %param.7) | copy-start | bytes 98308
  8.4 0.7 %copy-start.4 = (s32[256]{0:T(256)S(1)}, s32[256]{0:T(256)}, u32[]{:S(2)}) copy-start(s32[256]{0:T(256)} %param.5) | copy-start | bytes 3076
  9.4 16.1 %copy-start.1 = (f32[4096,16]{0,1:T(8,128)S(1)}, f32[4096,16]{0,1:T(8,128)}, u32[]{:S(2)}) copy-start(f32[4096,16]{0,1:T(8,128)} %param.6) | copy-start | bytes 786436
  9.5 6.5 %collective-permute-start.1 = (f32[16,4096]{1,0:T(8,128)S(1)}, f32[16,4096]{1,0:T(8,128)S(1)}, u32[]{:S(2)}, u32[]{:S(2)}) collective-permute-start(f32[16,4096]{1,0:T(8,128)S(1)} %gather_star_factors.3.refs_2_.refs_7_), channel_id=1, source_target_pairs={{0,2},{2,4},{4,6},{6,7},{7,5},{5,3},{3,1},{1,0},{8,9},{10,8},{12,1... | collective-permute-start | bytes 786440 | tf_op jit(solution)/shard_map/gather_star_factors/ppermute | solution.py:331
  11.1 3.4 %collective-permute-start.2 = (f32[32,256]{1,0:T(8,128)S(1)}, f32[32,256]{1,0:T(8,128)S(1)}, u32[]{:S(2)}, u32[]{:S(2)}) collective-permute-start(f32[32,256]{1,0:T(8,128)S(1)} %get-tuple-element.32.refs_7_.refs_4_.refs_15_), channel_id=1, source_target_pairs={{0,8},{8,0},{16,24},{24,16},{1,9},{9,1},{17,25},{25,17},{2,10},{10... | collective-permute-start | bytes 98312 | tf_op jit(solution)/shard_map/gather_cadence_factors/ppermute | solution.py:335
  11.1 3.9 %collective-permute-start.3 = (f32[32,256]{1,0:T(8,128)S(1)}, f32[32,256]{1,0:T(8,128)S(1)}, u32[]{:S(2)}, u32[]{:S(2)}) collective-permute-start(f32[32,256]{1,0:T(8,128)S(1)} %get-tuple-element.32.refs_7_.refs_4_.refs_15_), channel_id=1, source_target_pairs={{0,16},{8,24},{16,0},{24,8},{1,17},{9,25},{17,1},{25,9},{2,18},{10... | collective-permute-start | bytes 98312 | tf_op jit(solution)/shard_map/gather_cadence_factors/ppermute | solution.py:335
  12.6 3.3 %collective-permute-start.4 = (f32[32,256]{1,0:T(8,128)S(1)}, f32[32,256]{1,0:T(8,128)S(1)}, u32[]{:S(2)}, u32[]{:S(2)}) collective-permute-start(f32[32,256]{1,0:T(8,128)S(1)} %get-tuple-element.32.refs_7_.refs_4_.refs_15_), channel_id=1, source_target_pairs={{0,24},{8,16},{16,8},{24,0},{1,25},{9,17},{17,9},{25,1},{2,26},{10... | collective-permute-start | bytes 98312 | tf_op jit(solution)/shard_map/gather_cadence_factors/ppermute | solution.py:335
  12.9 6.4 %collective-permute-start.8 = (f32[16,4096]{1,0:T(8,128)S(1)}, f32[16,4096]{1,0:T(8,128)S(1)}, u32[]{:S(2)}, u32[]{:S(2)}) collective-permute-start(f32[16,4096]{1,0:T(8,128)S(1)} %gather_star_factors.5), channel_id=1, source_target_pairs={{0,2},{2,4},{4,6},{6,7},{7,5},{5,3},{3,1},{1,0},{8,9},{10,8},{12,1... | collective-permute-start | bytes 786440 | tf_op jit(solution)/shard_map/gather_star_factors/ppermute | solution.py:331
  15.9 6.4 %collective-permute-start.5 = (f32[16,4096]{1,0:T(8,128)S(1)}, f32[16,4096]{1,0:T(8,128)S(1)}, u32[]{:S(2)}, u32[]{:S(2)}) collective-permute-start(f32[16,4096]{1,0:T(8,128)S(1)} %gather_star_factors.4.refs_3_.refs_8_), channel_id=1, source_target_pairs={{0,2},{2,4},{4,6},{6,7},{7,5},{5,3},{3,1},{1,0},{8,9},{10,8},{12,1... | collective-permute-start | bytes 786440 | tf_op jit(solution)/shard_map/gather_star_factors/ppermute | solution.py:331
  17.5 8.0 %collective-permute-start.10 = (f32[16,4096]{1,0:T(8,128)S(1)}, f32[16,4096]{1,0:T(8,128)S(1)}, u32[]{:S(2)}, u32[]{:S(2)}) collective-permute-start(f32[16,4096]{1,0:T(8,128)S(1)} %gather_star_factors.5), channel_id=1, source_target_pairs={{0,8},{8,0},{16,24},{24,16},{1,9},{9,1},{17,25},{25,17},{2,10},{10... | collective-permute-start | bytes 786440 | tf_op jit(solution)/shard_map/gather_star_factors/ppermute | solution.py:335
  19.3 6.2 %collective-permute-start.9 = (f32[16,4096]{1,0:T(8,128)S(1)}, f32[16,4096]{1,0:T(8,128)S(1)}, u32[]{:S(2)}, u32[]{:S(2)}) collective-permute-start(f32[16,4096]{1,0:T(8,128)S(1)} %collective-permute-done.8), channel_id=1, source_target_pairs={{0,8},{8,0},{16,24},{24,16},{1,9},{9,1},{17,25},{25,17},{2,10},{10... | collective-permute-start | bytes 786440 | tf_op jit(solution)/shard_map/gather_star_factors/ppermute | solution.py:335
  19.3 8.1 %collective-permute-start.12 = (f32[16,4096]{1,0:T(8,128)S(1)}, f32[16,4096]{1,0:T(8,128)S(1)}, u32[]{:S(2)}, u32[]{:S(2)}) collective-permute-start(f32[16,4096]{1,0:T(8,128)S(1)} %collective-permute-done.8), channel_id=1, source_target_pairs={{0,10},{2,12},{4,14},{6,15},{7,13},{5,11},{3,9},{1,8},{8,1},{10,0}... | collective-permute-start | bytes 786440 | tf_op jit(solution)/shard_map/gather_star_factors/ppermute | solution.py:331
  22.3 5.1 %collective-permute-start.11 = (f32[16,2048]{1,0:T(8,128)S(1)}, f32[16,2048]{1,0:T(8,128)S(1)}, u32[]{:S(2)}, u32[]{:S(2)}) collective-permute-start(f32[16,2048]{1,0:T(8,128)S(1)} %get-tuple-element.60), channel_id=1, source_target_pairs={{0,2},{2,4},{4,6},{6,7},{7,5},{5,3},{3,1},{1,0},{8,9},{10,8},{12,1... | collective-permute-start | bytes 393224 | tf_op jit(solution)/shard_map/gather_star_factors/ppermute | solution.py:331
  24.0 5.3 %collective-permute-start.13 = (f32[16,2048]{1,0:T(8,128)S(1)}, f32[16,2048]{1,0:T(8,128)S(1)}, u32[]{:S(2)}, u32[]{:S(2)}) collective-permute-start(f32[16,2048]{1,0:T(8,128)S(1)} %get-tuple-element.59), channel_id=1, source_target_pairs={{0,2},{2,4},{4,6},{6,7},{7,5},{5,3},{3,1},{1,0},{8,9},{10,8},{12,1... | collective-permute-start | bytes 393224 | tf_op jit(solution)/shard_map/gather_star_factors/ppermute | solution.py:331
  31.2 1.7 %collective-permute-start.14 = (f32[16,4224]{1,0:T(8,128)S(1)}, f32[16,4224]{1,0:T(8,128)S(1)}, u32[]{:S(2)}, u32[]{:S(2)}) collective-permute-start(f32[16,4224]{1,0:T(8,128)S(1)} %get-tuple-element.43), channel_id=1, source_target_pairs={{0,8},{8,0},{16,24},{24,16},{1,9},{9,1},{17,25},{25,17},{2,10},{10... | collective-permute-start | bytes 811016 | tf_op jit(solution)/shard_map/ppermute | solution.py:335
  31.2 6.5 %collective-permute-start.15 = (f32[16,4224]{1,0:T(8,128)S(1)}, f32[16,4224]{1,0:T(8,128)S(1)}, u32[]{:S(2)}, u32[]{:S(2)}) collective-permute-start(f32[16,4224]{1,0:T(8,128)S(1)} %get-tuple-element.48), channel_id=1, source_target_pairs={{0,2},{2,4},{4,6},{6,7},{7,5},{5,3},{3,1},{1,0},{8,9},{10,8},{12,1... | collective-permute-start | bytes 811016 | tf_op jit(solution)/shard_map/scatter_star_gradient/ppermute | solution.py:331
  32.8 6.6 %collective-permute-start.17 = (f32[16,4224]{1,0:T(8,128)S(1)}, f32[16,4224]{1,0:T(8,128)S(1)}, u32[]{:S(2)}, u32[]{:S(2)}) collective-permute-start(f32[16,4224]{1,0:T(8,128)S(1)} %get-tuple-element.49), channel_id=1, source_target_pairs={{0,8},{8,0},{16,24},{24,16},{1,9},{9,1},{17,25},{25,17},{2,10},{10... | collective-permute-start | bytes 811016 | tf_op jit(solution)/shard_map/ppermute | solution.py:335
  32.8 7.8 %collective-permute-start.18 = (f32[16,4224]{1,0:T(8,128)S(1)}, f32[16,4224]{1,0:T(8,128)S(1)}, u32[]{:S(2)}, u32[]{:S(2)}) collective-permute-start(f32[16,4224]{1,0:T(8,128)S(1)} %collective-permute-done.14.refs_1_), channel_id=1, source_target_pairs={{0,2},{2,4},{4,6},{6,7},{7,5},{5,3},{3,1},{1,0},{8,9},{10,8},{12,1... | collective-permute-start | bytes 811016 | tf_op jit(solution)/shard_map/scatter_star_gradient/ppermute | solution.py:331
  37.8 6.5 %collective-permute-start.16 = (f32[16,4224]{1,0:T(8,128)S(1)}, f32[16,4224]{1,0:T(8,128)S(1)}, u32[]{:S(2)}, u32[]{:S(2)}) collective-permute-start(f32[16,4224]{1,0:T(8,128)S(1)} %add.15), channel_id=1, source_target_pairs={{0,2},{2,4},{4,6},{6,7},{7,5},{5,3},{3,1},{1,0},{8,9},{10,8},{12,1... | collective-permute-start | bytes 811016 | tf_op jit(solution)/shard_map/scatter_star_gradient/ppermute | solution.py:331
  39.4 7.2 %collective-permute-start.20 = (f32[16,4224]{1,0:T(8,128)S(1)}, f32[16,4224]{1,0:T(8,128)S(1)}, u32[]{:S(2)}, u32[]{:S(2)}) collective-permute-start(f32[16,4224]{1,0:T(8,128)S(1)} %get-tuple-element.50), channel_id=1, source_target_pairs={{0,8},{8,0},{16,24},{24,16},{1,9},{9,1},{17,25},{25,17},{2,10},{10... | collective-permute-start | bytes 811016 | tf_op jit(solution)/shard_map/scatter_star_gradient/ppermute | solution.py:335
  40.7 6.5 %collective-permute-start.21 = (f32[16,4224]{1,0:T(8,128)S(1)}, f32[16,4224]{1,0:T(8,128)S(1)}, u32[]{:S(2)}, u32[]{:S(2)}) collective-permute-start(f32[16,4224]{1,0:T(8,128)S(1)} %add.17.refs_1_), channel_id=1, source_target_pairs={{0,2},{2,4},{4,6},{6,7},{7,5},{5,3},{3,1},{1,0},{8,9},{10,8},{12,1... | collective-permute-start | bytes 811016 | tf_op jit(solution)/shard_map/scatter_star_gradient/ppermute | solution.py:331
  42.3 4.3 %collective-permute-start.22 = (f32[64,256]{1,0:T(8,128)S(1)}, f32[64,256]{1,0:T(8,128)S(1)}, u32[]{:S(2)}, u32[]{:S(2)}) collective-permute-start(f32[64,256]{1,0:T(8,128)S(1)} %scatter_star_gradient.10), channel_id=1, source_target_pairs={{0,16},{8,24},{16,0},{24,8},{1,17},{9,25},{17,1},{25,9},{2,18},{10... | collective-permute-start | bytes 196616 | tf_op jit(solution)/shard_map/scatter_star_gradient/ppermute | solution.py:335
  44.4 6.5 %collective-permute-start.19 = (f32[16,4224]{1,0:T(8,128)S(1)}, f32[16,4224]{1,0:T(8,128)S(1)}, u32[]{:S(2)}, u32[]{:S(2)}) collective-permute-start(f32[16,4224]{1,0:T(8,128)S(1)} %scatter_star_gradient.9), channel_id=1, source_target_pairs={{0,2},{2,4},{4,6},{6,7},{7,5},{5,3},{3,1},{1,0},{8,9},{10,8},{12,1... | collective-permute-start | bytes 811016 | tf_op jit(solution)/shard_map/scatter_star_gradient/ppermute | solution.py:331
  47.2 7.3 %collective-permute-start.24 = (f32[16,4224]{1,0:T(8,128)S(1)}, f32[16,4224]{1,0:T(8,128)S(1)}, u32[]{:S(2)}, u32[]{:S(2)}) collective-permute-start(f32[16,4224]{1,0:T(8,128)S(1)} %scatter_star_gradient.12.refs_1_), channel_id=1, source_target_pairs={{0,2},{2,4},{4,6},{6,7},{7,5},{5,3},{3,1},{1,0},{8,9},{10,8},{12,1... | collective-permute-start | bytes 811016 | tf_op jit(solution)/shard_map/scatter_star_gradient/ppermute | solution.py:331
  48.8 3.7 %collective-permute-start.25 = (f32[32,256]{1,0:T(8,128)S(1)}, f32[32,256]{1,0:T(8,128)S(1)}, u32[]{:S(2)}, u32[]{:S(2)}) collective-permute-start(f32[32,256]{1,0:T(8,128)S(1)} %get-tuple-element.55), channel_id=1, source_target_pairs={{0,8},{8,0},{16,24},{24,16},{1,9},{9,1},{17,25},{25,17},{2,10},{10... | collective-permute-start | bytes 98312 | tf_op jit(solution)/shard_map/scatter_star_gradient/ppermute | solution.py:335
  50.9 3.7 %collective-permute-start.27 = (f32[8,128]{1,0:T(8,128)S(1)}, f32[8,128]{1,0:T(8,128)S(1)}, u32[]{:S(2)}, u32[]{:S(2)}) collective-permute-start(f32[8,128]{1,0:T(8,128)S(1)} %get-tuple-element.56), channel_id=1, source_target_pairs={{0,2},{2,4},{4,6},{6,7},{7,5},{5,3},{3,1},{1,0},{8,9},{10,8},{12,1... | collective-permute-start | bytes 12296 | tf_op jit(solution)/shard_map/scatter_star_gradient/ppermute | solution.py:331
  52.5 8.0 %copy-start.2 = (f32[32,256]{1,0:T(8,128)}, f32[32,256]{1,0:T(8,128)S(1)}, u32[]{:S(2)}) copy-start(f32[32,256]{1,0:T(8,128)S(1)} %add.19.refs_1_) | copy-start | bytes 98308
  52.5 6.5 %collective-permute-start.23 = (f32[16,4224]{1,0:T(8,128)S(1)}, f32[16,4224]{1,0:T(8,128)S(1)}, u32[]{:S(2)}, u32[]{:S(2)}) collective-permute-start(f32[16,4224]{1,0:T(8,128)S(1)} %get-tuple-element.54), channel_id=1, source_target_pairs={{0,2},{2,4},{4,6},{6,7},{7,5},{5,3},{3,1},{1,0},{8,9},{10,8},{12,1... | collective-permute-start | bytes 811016 | tf_op jit(solution)/shard_map/scatter_star_gradient/ppermute | solution.py:331
  54.6 5.2 %collective-permute-start.26 = (f32[16,4224]{1,0:T(8,128)S(1)}, f32[16,4224]{1,0:T(8,128)S(1)}, u32[]{:S(2)}, u32[]{:S(2)}) collective-permute-start(f32[16,4224]{1,0:T(8,128)S(1)} %scatter_star_gradient.15), channel_id=1, source_target_pairs={{0,8},{8,0},{16,24},{24,16},{1,9},{9,1},{17,25},{25,17},{2,10},{10... | collective-permute-start | bytes 811016 | tf_op jit(solution)/shard_map/scatter_star_gradient/ppermute | solution.py:335
  54.7 4.4 %collective-permute-start.28 = (f32[8,128]{1,0:T(8,128)S(1)}, f32[8,128]{1,0:T(8,128)S(1)}, u32[]{:S(2)}, u32[]{:S(2)}) collective-permute-start(f32[8,128]{1,0:T(8,128)S(1)} %scatter_star_gradient.16.refs_0_), channel_id=1, source_target_pairs={{0,8},{8,0},{16,24},{24,16},{1,9},{9,1},{17,25},{25,17},{2,10},{10... | collective-permute-start | bytes 12296 | tf_op jit(solution)/shard_map/scatter_star_gradient/ppermute | solution.py:335
  55.1 3.9 %collective-permute-start.29 = (f32[8,128]{1,0:T(8,128)S(1)}, f32[8,128]{1,0:T(8,128)S(1)}, u32[]{:S(2)}, u32[]{:S(2)}) collective-permute-start(f32[8,128]{1,0:T(8,128)S(1)} %scatter_star_gradient.16.refs_0_), channel_id=1, source_target_pairs={{0,16},{8,24},{16,0},{24,8},{1,17},{9,25},{17,1},{25,9},{2,18},{10... | collective-permute-start | bytes 12296 | tf_op jit(solution)/shard_map/scatter_star_gradient/ppermute | solution.py:335
  56.7 3.1 %collective-permute-start.30 = (f32[8,128]{1,0:T(8,128)S(1)}, f32[8,128]{1,0:T(8,128)S(1)}, u32[]{:S(2)}, u32[]{:S(2)}) collective-permute-start(f32[8,128]{1,0:T(8,128)S(1)} %scatter_star_gradient.16.refs_0_), channel_id=1, source_target_pairs={{0,24},{8,16},{16,8},{24,0},{1,25},{9,17},{17,9},{25,1},{2,26},{10... | collective-permute-start | bytes 12296 | tf_op jit(solution)/shard_map/scatter_star_gradient/ppermute | solution.py:335

commit v4 on v3

--- a/solution.py
+++ b/solution.py
@@ -32,26 +32,23 @@
     return pl.ds(pl.multiple_of(k * rows, rows), rows)
 
 
-def stage_body(light_in, quality_in, cad_in, light, quality, cad, sem):
-    copies = [
-        pltpu.make_async_copy(cad_in, cad, sem.at[0]),
-        pltpu.make_async_copy(quality_in, quality, sem.at[1]),
-        pltpu.make_async_copy(light_in, light, sem.at[2]),
-    ]
+def stage_body(*refs):
+    count = len(refs) // 2
+    sem = refs[-1]
+    copies = [pltpu.make_async_copy(refs[i], refs[count + i], sem.at[i]) for i in range(count)]
     for copy in copies:
         copy.start()
     for copy in copies:
         copy.wait()
 
 
-def stage(light, quality, cad_t):
-    given = (light, quality, cad_t)
+def stage(*given):
     return pl.pallas_call(
         stage_body,
-        in_specs=[pl.BlockSpec(memory_space=pl.ANY)] * 3,
-        out_specs=[pl.BlockSpec(memory_space=pltpu.VMEM)] * 3,
+        in_specs=[pl.BlockSpec(memory_space=pl.ANY)] * len(given),
+        out_specs=[pl.BlockSpec(memory_space=pltpu.VMEM)] * len(given),
         out_shape=[jax.ShapeDtypeStruct(x.shape, x.dtype) for x in given],
-        scratch_shapes=[pltpu.SemaphoreType.DMA((3,))],
+        scratch_shapes=[pltpu.SemaphoreType.DMA((len(given),))],
         cost_estimate=pl.CostEstimate(flops=0, bytes_accessed=1 << 10, transcendentals=0),
         compiler_params=pltpu.CompilerParams(vmem_limit_bytes=16 << 20),
     )(*given)
@@ -353,7 +350,8 @@
     def cad_slot(k):
         return jnp.bitwise_xor(lax.axis_index("star"), k)
 
-    light, quality, cad_t = stage(light, quality.reshape(1, -1), cad_t)
+    light = stage(light)[0]
+    quality = quality.reshape(1, -1)
 
     with jax.named_scope("gather_cadence_factors"):
         cads = [cad_t] + [swap(cad_t, "star", bit) for bit in range(1, m)]

time: 60.7 us -> 59.9 us (0.987)
  local copies, waits for them, and re-layouts: 3.65 us -> 2.23 us
    unnamed x10, local copies, waits for them, and re-layouts: 3.64 us -> 2.21 us
  transfers between devices with their start and end apart: 31 -> 31, of which waited for: 13 -> 14; matrix products, arithmetic and copies ran while one was open for 0% -> 0% of each run, Pallas kernels for 11% -> 12%
where the time goes in v4:
time: 59.9 us; the launch traced here: 59.8 us
  starting transfers between devices  32.9 us (55%)
  waiting for transfers between devices  14.2 us (24%)
  Pallas kernels  9.53 us (16%)
  local copies, waits for them, and re-layouts  2.23 us (4%)
  between operations  0.8 us (1%)
    ppermute x16, starting transfers between devices, shift(): return lax.ppermute(x, ('star', 'cad'), pairs)  26.9 us
    ppermute x16, waiting for transfers between devices, shift(): return lax.ppermute(x, ('star', 'cad'), pairs)  11.5 us
    pallas_call x4, Pallas kernels, big_call(): pl.pallas_call(body_of, in_specs=[vmem] * len(given), out_specs=[vmem] *...  8.43 us
    ppermute x15, starting transfers between devices, swap(): lax.ppermute(x, axis, [(i, i ^ bit) for i in range(lax.axis_size(axis))])  6.01 us
    ppermute x15, waiting for transfers between devices, swap(): lax.ppermute(x, axis, [(i, i ^ bit) for i in range(lax.axis_size(axis))])  2.7 us
    unnamed x10, local copies, waits for them, and re-layouts  2.21 us
  transfers between devices with their start and end apart: 31, of which 14 were waited for; matrix products, arithmetic and copies ran while one was open for 0% of the time, Pallas kernels for 12%

profile of v4, /device:TPU:0, one launch (start us, length us, event | category | flops | bytes accessed | tf_op | source)
XLA Modules:
  0.0 59.8 jit_solution(5529915067778646054)
XLA Ops:
  0.6 0.5 collective-permute-start.6
  1.1 2.6 %collective-permute-start = (f32[16,4096]{1,0:T(8,128)}, f32[16,4096]{1,0:T(8,128)S(1)}, u32[]{:S(2)}, u32[]{:S(2)}) collective-permute-start(f32[16,4096]{1,0:T(8,128)} %bitcast.7), channel_id=1, source_target_pairs={{0,2},{2,4},{4,6},{6,7},{7,5},{5,3},{3,1},{1,0},{8,9},{10,8},{12,1... | collective-permute-start | bytes 786440 | tf_op jit(solution)/shard_map/gather_star_factors/ppermute | solution.py:328
  3.8 1.7 %collective-permute-start.7 = (f32[16,4096]{1,0:T(8,128)S(1)}, f32[16,4096]{1,0:T(8,128)S(1)}, u32[]{:S(2)}, u32[]{:S(2)}) collective-permute-start(f32[16,4096]{1,0:T(8,128)S(1)} %collective-permute-done.6), channel_id=1, source_target_pairs={{0,2},{2,4},{4,6},{6,7},{7,5},{5,3},{3,1},{1,0},{8,9},{10,8},{12,1... | collective-permute-start | bytes 786440 | tf_op jit(solution)/shard_map/gather_star_factors/ppermute | solution.py:328
  5.5 2.2 %copy-done = f32[4096,256]{1,0:T(8,128)S(1)} copy-done((f32[4096,256]{1,0:T(8,128)S(1)}, f32[4096,256]{1,0:T(8,128)}, u32[]{:S(2)}) %copy-start) | copy-done | bytes 4194328
  7.7 0.3 shard_map.67.refs_1_.refs_0_
  8.0 0.0 copy-start.2
  8.0 0.0 copy-start.1
  8.0 0.3 collective-permute-done.refs_0_
  8.3 2.1 %collective-permute-start.1 = (f32[16,4096]{1,0:T(8,128)S(1)}, f32[16,4096]{1,0:T(8,128)S(1)}, u32[]{:S(2)}, u32[]{:S(2)}) collective-permute-start(f32[16,4096]{1,0:T(8,128)S(1)} %gather_star_factors.3.refs_2_.refs_7_), channel_id=1, source_target_pairs={{0,2},{2,4},{4,6},{6,7},{7,5},{5,3},{3,1},{1,0},{8,9},{10,8},{12,1... | collective-permute-start | bytes 786440 | tf_op jit(solution)/shard_map/gather_star_factors/ppermute | solution.py:328
  10.4 1.5 %collective-permute-start.3 = (f32[32,256]{1,0:T(8,128)S(1)}, f32[32,256]{1,0:T(8,128)S(1)}, u32[]{:S(2)}, u32[]{:S(2)}) collective-permute-start(f32[32,256]{1,0:T(8,128)S(1)} %bitcast.11), channel_id=1, source_target_pairs={{0,16},{8,24},{16,0},{24,8},{1,17},{9,25},{17,1},{25,9},{2,18},{10... | collective-permute-start | bytes 98312 | tf_op jit(solution)/shard_map/gather_cadence_factors/ppermute | solution.py:332
  11.9 0.3 collective-permute-start.4
  12.2 1.6 %collective-permute-start.8 = (f32[16,4096]{1,0:T(8,128)S(1)}, f32[16,4096]{1,0:T(8,128)S(1)}, u32[]{:S(2)}, u32[]{:S(2)}) collective-permute-start(f32[16,4096]{1,0:T(8,128)S(1)} %gather_star_factors.5), channel_id=1, source_target_pairs={{0,2},{2,4},{4,6},{6,7},{7,5},{5,3},{3,1},{1,0},{8,9},{10,8},{12,1... | collective-permute-start | bytes 786440 | tf_op jit(solution)/shard_map/gather_star_factors/ppermute | solution.py:328
  13.8 0.5 collective-permute-done.3.refs_2_.refs_9_.refs_6_.refs_17_
  14.3 0.9 %collective-permute-done.4.refs_3_.refs_10_.refs_7_.refs_18_ = f32[32,256]{1,0:T(8,128)S(1)} collective-permute-done((f32[32,256]{1,0:T(8,128)S(1)}, f32[32,256]{1,0:T(8,128)S(1)}, u32[]{:S(2)}, u32[]{:S(2)}) %collective-permute-start.4) | collective-permute-done | bytes 32800 | tf_op jit(solution)/shard_map/gather_cadence_factors/ppermute | solution.py:332
  15.2 1.6 %collective-permute-start.5 = (f32[16,4096]{1,0:T(8,128)S(1)}, f32[16,4096]{1,0:T(8,128)S(1)}, u32[]{:S(2)}, u32[]{:S(2)}) collective-permute-start(f32[16,4096]{1,0:T(8,128)S(1)} %gather_star_factors.4.refs_3_.refs_8_), channel_id=1, source_target_pairs={{0,2},{2,4},{4,6},{6,7},{7,5},{5,3},{3,1},{1,0},{8,9},{10,8},{12,1... | collective-permute-start | bytes 786440 | tf_op jit(solution)/shard_map/gather_star_factors/ppermute | solution.py:328
  16.8 1.8 %collective-permute-done.8 = f32[16,4096]{1,0:T(8,128)S(1)} collective-permute-done((f32[16,4096]{1,0:T(8,128)S(1)}, f32[16,4096]{1,0:T(8,128)S(1)}, u32[]{:S(2)}, u32[]{:S(2)}) %collective-permute-start.8) | collective-permute-done | bytes 262176 | tf_op jit(solution)/shard_map/gather_star_factors/ppermute | solution.py:328
  18.6 1.7 %collective-permute-start.12 = (f32[16,4096]{1,0:T(8,128)S(1)}, f32[16,4096]{1,0:T(8,128)S(1)}, u32[]{:S(2)}, u32[]{:S(2)}) collective-permute-start(f32[16,4096]{1,0:T(8,128)S(1)} %collective-permute-done.8), channel_id=1, source_target_pairs={{0,10},{2,12},{4,14},{6,15},{7,13},{5,11},{3,9},{1,8},{8,1},{10,0}... | collective-permute-start | bytes 786440 | tf_op jit(solution)/shard_map/gather_star_factors/ppermute | solution.py:328
  20.3 1.3 %collective-permute-done.5.refs_4_.refs_9_ = f32[16,4096]{1,0:T(8,128)S(1)} collective-permute-done((f32[16,4096]{1,0:T(8,128)S(1)}, f32[16,4096]{1,0:T(8,128)S(1)}, u32[]{:S(2)}, u32[]{:S(2)}) %collective-permute-start.5) | collective-permute-done | bytes 262176 | tf_op jit(solution)/shard_map/gather_star_factors/ppermute | solution.py:328
  21.6 1.6 %collective-permute-start.11 = (f32[16,2048]{1,0:T(8,128)S(1)}, f32[16,2048]{1,0:T(8,128)S(1)}, u32[]{:S(2)}, u32[]{:S(2)}) collective-permute-start(f32[16,2048]{1,0:T(8,128)S(1)} %get-tuple-element.54), channel_id=1, source_target_pairs={{0,2},{2,4},{4,6},{6,7},{7,5},{5,3},{3,1},{1,0},{8,9},{10,8},{12,1... | collective-permute-start | bytes 393224 | tf_op jit(solution)/shard_map/gather_star_factors/ppermute | solution.py:328
  23.3 1.6 %collective-permute-start.13 = (f32[16,2048]{1,0:T(8,128)S(1)}, f32[16,2048]{1,0:T(8,128)S(1)}, u32[]{:S(2)}, u32[]{:S(2)}) collective-permute-start(f32[16,2048]{1,0:T(8,128)S(1)} %get-tuple-element.53), channel_id=1, source_target_pairs={{0,2},{2,4},{4,6},{6,7},{7,5},{5,3},{3,1},{1,0},{8,9},{10,8},{12,1... | collective-permute-start | bytes 393224 | tf_op jit(solution)/shard_map/gather_star_factors/ppermute | solution.py:328
  24.9 1.9 %shard_map.68.refs_0_ = f32[4096,256]{1,0:T(8,128)S(1)} custom-call(f32[4096,256]{1,0:T(8,128)S(1)} %shard_map.67.refs_1_.refs_0_, f32[16,4096]{1,0:T(8,128)S(1)} %bitcast.8, f32[16,4096]{1,0:T(8,128)S(1)} %gather_star_factors.3.refs_2_.refs_7_, f32[16,4096]{1,0:T(8,128)S(1)} %gather_star_factors.4.refs_3_.refs_8_, ...), custom_call_target="tpu_custom_call" | custom-call | flops 1610612736 | bytes 1048576 | tf_op jit(solution)/shard_map/pallas_call | solution.py:195
  26.8 1.9 %shard_map.69 = (bf16[2048,256]{1,0:T(8,128)(2,1)S(1)}, bf16[2048,256]{1,0:T(8,128)(2,1)S(1)}, f32[8,256]{1,0:T(8,128)S(1)}, f32[16,2048]{1,0:T(8,128)S(1)}, f32...) custom-call(f32[4096,256]{1,0:T(8,128)S(1)} %shard_map.68.refs_0_, s32[1,256]{1,0:T(1,128)S(1)} %bitcast.18, ...), custom_call_target="tpu_custom_call" | custom-call | flops 536870912 | bytes 1048576 | tf_op jit(solution)/shard_map/pallas_call | solution.py:195
  28.7 1.9 %shard_map.70 = (bf16[2048,256]{1,0:T(8,128)(2,1)S(1)}, bf16[2048,256]{1,0:T(8,128)(2,1)S(1)}, f32[8,128]{1,0:T(8,128)S(1)}, f32[16,4224]{1,0:T(8,128)S(1)}, f32...) custom-call(f32[4096,256]{1,0:T(8,128)S(1)} %shard_map.68.refs_0_, s32[1,256]{1,0:T(1,128)S(1)} %bitcast.19, ...), custom_call_target="tpu_custom_call" | custom-call | flops 536870912 | bytes 1048576 | tf_op jit(solution)/shard_map/pallas_call | solution.py:195
  30.5 0.1 collective-permute-start.14
  30.6 1.6 %collective-permute-start.15 = (f32[16,4224]{1,0:T(8,128)S(1)}, f32[16,4224]{1,0:T(8,128)S(1)}, u32[]{:S(2)}, u32[]{:S(2)}) collective-permute-start(f32[16,4224]{1,0:T(8,128)S(1)} %get-tuple-element.42), channel_id=1, source_target_pairs={{0,2},{2,4},{4,6},{6,7},{7,5},{5,3},{3,1},{1,0},{8,9},{10,8},{12,1... | collective-permute-start | bytes 811016 | tf_op jit(solution)/shard_map/scatter_star_gradient/ppermute | solution.py:328
  32.2 1.5 %collective-permute-start.18 = (f32[16,4224]{1,0:T(8,128)S(1)}, f32[16,4224]{1,0:T(8,128)S(1)}, u32[]{:S(2)}, u32[]{:S(2)}) collective-permute-start(f32[16,4224]{1,0:T(8,128)S(1)} %collective-permute-done.14.refs_1_), channel_id=1, source_target_pairs={{0,2},{2,4},{4,6},{6,7},{7,5},{5,3},{3,1},{1,0},{8,9},{10,8},{12,1... | collective-permute-start | bytes 811016 | tf_op jit(solution)/shard_map/scatter_star_gradient/ppermute | solution.py:328
  33.7 2.8 %shard_map.72 = (f32[16,4224]{1,0:T(8,128)S(1)}, f32[16,4224]{1,0:T(8,128)S(1)}, f32[16,4224]{1,0:T(8,128)S(1)}, f32[16,4224]{1,0:T(8,128)S(1)}, f32[16,4224]{1,...) custom-call(bf16[2048,256]{1,0:T(8,128)(2,1)S(1)} %get-tuple-element.28.refs_0_, ...), custom_call_target="tpu_custom_call" | custom-call | flops 1610612736 | bytes 1048576 | tf_op jit(solution)/shard_map/pallas_call | solution.py:195
  36.5 0.6 %collective-permute-done.15 = f32[16,4224]{1,0:T(8,128)S(1)} collective-permute-done((f32[16,4224]{1,0:T(8,128)S(1)}, f32[16,4224]{1,0:T(8,128)S(1)}, u32[]{:S(2)}, u32[]{:S(2)}) %collective-permute-start.15) | collective-permute-done | bytes 270368 | tf_op jit(solution)/shard_map/scatter_star_gradient/ppermute | solution.py:328
  37.2 1.6 %collective-permute-start.16 = (f32[16,4224]{1,0:T(8,128)S(1)}, f32[16,4224]{1,0:T(8,128)S(1)}, u32[]{:S(2)}, u32[]{:S(2)}) collective-permute-start(f32[16,4224]{1,0:T(8,128)S(1)} %add.15), channel_id=1, source_target_pairs={{0,2},{2,4},{4,6},{6,7},{7,5},{5,3},{3,1},{1,0},{8,9},{10,8},{12,1... | collective-permute-start | bytes 811016 | tf_op jit(solution)/shard_map/scatter_star_gradient/ppermute | solution.py:328
  38.7 1.3 %collective-permute-done.18 = f32[16,4224]{1,0:T(8,128)S(1)} collective-permute-done((f32[16,4224]{1,0:T(8,128)S(1)}, f32[16,4224]{1,0:T(8,128)S(1)}, u32[]{:S(2)}, u32[]{:S(2)}) %collective-permute-start.18) | collective-permute-done | bytes 270368 | tf_op jit(solution)/shard_map/scatter_star_gradient/ppermute | solution.py:328
  40.1 1.6 %collective-permute-start.21 = (f32[16,4224]{1,0:T(8,128)S(1)}, f32[16,4224]{1,0:T(8,128)S(1)}, u32[]{:S(2)}, u32[]{:S(2)}) collective-permute-start(f32[16,4224]{1,0:T(8,128)S(1)} %add.17.refs_1_), channel_id=1, source_target_pairs={{0,2},{2,4},{4,6},{6,7},{7,5},{5,3},{3,1},{1,0},{8,9},{10,8},{12,1... | collective-permute-start | bytes 811016 | tf_op jit(solution)/shard_map/scatter_star_gradient/ppermute | solution.py:328
  41.6 1.5 %collective-permute-start.22 = (f32[64,256]{1,0:T(8,128)S(1)}, f32[64,256]{1,0:T(8,128)S(1)}, u32[]{:S(2)}, u32[]{:S(2)}) collective-permute-start(f32[64,256]{1,0:T(8,128)S(1)} %scatter_star_gradient.10), channel_id=1, source_target_pairs={{0,16},{8,24},{16,0},{24,8},{1,17},{9,25},{17,1},{25,9},{2,18},{10... | collective-permute-start | bytes 196616 | tf_op jit(solution)/shard_map/scatter_star_gradient/ppermute | solution.py:332
  43.1 0.5 collective-permute-done.16
  43.7 1.6 %collective-permute-start.19 = (f32[16,4224]{1,0:T(8,128)S(1)}, f32[16,4224]{1,0:T(8,128)S(1)}, u32[]{:S(2)}, u32[]{:S(2)}) collective-permute-start(f32[16,4224]{1,0:T(8,128)S(1)} %scatter_star_gradient.9), channel_id=1, source_target_pairs={{0,2},{2,4},{4,6},{6,7},{7,5},{5,3},{3,1},{1,0},{8,9},{10,8},{12,1... | collective-permute-start | bytes 811016 | tf_op jit(solution)/shard_map/scatter_star_gradient/ppermute | solution.py:328
  45.3 0.6 %collective-permute-done.22.got = f32[64,256]{1,0:T(8,128)S(1)} collective-permute-done((f32[64,256]{1,0:T(8,128)S(1)}, f32[64,256]{1,0:T(8,128)S(1)}, u32[]{:S(2)}, u32[]{:S(2)}) %collective-permute-start.22) | collective-permute-done | bytes 65568 | tf_op jit(solution)/shard_map/scatter_star_gradient/ppermute | solution.py:332
  45.9 0.7 %collective-permute-done.21 = f32[16,4224]{1,0:T(8,128)S(1)} collective-permute-done((f32[16,4224]{1,0:T(8,128)S(1)}, f32[16,4224]{1,0:T(8,128)S(1)}, u32[]{:S(2)}, u32[]{:S(2)}) %collective-permute-start.21) | collective-permute-done | bytes 270368 | tf_op jit(solution)/shard_map/scatter_star_gradient/ppermute | solution.py:328
  46.6 1.6 %collective-permute-start.24 = (f32[16,4224]{1,0:T(8,128)S(1)}, f32[16,4224]{1,0:T(8,128)S(1)}, u32[]{:S(2)}, u32[]{:S(2)}) collective-permute-start(f32[16,4224]{1,0:T(8,128)S(1)} %scatter_star_gradient.12.refs_1_), channel_id=1, source_target_pairs={{0,2},{2,4},{4,6},{6,7},{7,5},{5,3},{3,1},{1,0},{8,9},{10,8},{12,1... | collective-permute-start | bytes 811016 | tf_op jit(solution)/shard_map/scatter_star_gradient/ppermute | solution.py:328
  48.2 2.1 %collective-permute-done.19.refs_0_ = f32[16,4224]{1,0:T(8,128)S(1)} collective-permute-done((f32[16,4224]{1,0:T(8,128)S(1)}, f32[16,4224]{1,0:T(8,128)S(1)}, u32[]{:S(2)}, u32[]{:S(2)}) %collective-permute-start.19) | collective-permute-done | bytes 270368 | tf_op jit(solution)/shard_map/scatter_star_gradient/ppermute | solution.py:328
  50.3 1.6 %collective-permute-start.27 = (f32[8,128]{1,0:T(8,128)S(1)}, f32[8,128]{1,0:T(8,128)S(1)}, u32[]{:S(2)}, u32[]{:S(2)}) collective-permute-start(f32[8,128]{1,0:T(8,128)S(1)} %get-tuple-element.50), channel_id=1, source_target_pairs={{0,2},{2,4},{4,6},{6,7},{7,5},{5,3},{3,1},{1,0},{8,9},{10,8},{12,1... | collective-permute-start | bytes 12296 | tf_op jit(solution)/shard_map/scatter_star_gradient/ppermute | solution.py:328
  51.8 0.0 copy-start.3
  51.9 1.6 %collective-permute-start.23 = (f32[16,4224]{1,0:T(8,128)S(1)}, f32[16,4224]{1,0:T(8,128)S(1)}, u32[]{:S(2)}, u32[]{:S(2)}) collective-permute-start(f32[16,4224]{1,0:T(8,128)S(1)} %get-tuple-element.48), channel_id=1, source_target_pairs={{0,2},{2,4},{4,6},{6,7},{7,5},{5,3},{3,1},{1,0},{8,9},{10,8},{12,1... | collective-permute-start | bytes 811016 | tf_op jit(solution)/shard_map/scatter_star_gradient/ppermute | solution.py:328
  53.4 0.5 collective-permute-done.27.near
  53.9 0.1 collective-permute-start.26
  54.0 0.5 collective-permute-start.28
  54.5 1.5 %collective-permute-start.29 = (f32[8,128]{1,0:T(8,128)S(1)}, f32[8,128]{1,0:T(8,128)S(1)}, u32[]{:S(2)}, u32[]{:S(2)}) collective-permute-start(f32[8,128]{1,0:T(8,128)S(1)} %scatter_star_gradient.16.refs_0_), channel_id=1, source_target_pairs={{0,16},{8,24},{16,0},{24,8},{1,17},{9,25},{17,1},{25,9},{2,18},{10... | collective-permute-start | bytes 12296 | tf_op jit(solution)/shard_map/scatter_star_gradient/ppermute | solution.py:332
  56.0 2.4 %collective-permute-done.23.up = f32[16,4224]{1,0:T(8,128)S(1)} collective-permute-done((f32[16,4224]{1,0:T(8,128)S(1)}, f32[16,4224]{1,0:T(8,128)S(1)}, u32[]{:S(2)}, u32[]{:S(2)}) %collective-permute-start.23) | collective-permute-done | bytes 270368 | tf_op jit(solution)/shard_map/scatter_star_gradient/ppermute | solution.py:328
  58.4 0.6 %collective-permute-done.30.refs_3_ = f32[8,128]{1,0:T(8,128)S(1)} collective-permute-done((f32[8,128]{1,0:T(8,128)S(1)}, f32[8,128]{1,0:T(8,128)S(1)}, u32[]{:S(2)}, u32[]{:S(2)}) %collective-permute-start.30) | collective-permute-done | bytes 4128 | tf_op jit(solution)/shard_map/scatter_star_gradient/ppermute | solution.py:332
  59.0 0.8 %scatter_star_gradient.17 = (f32[16,4096]{1,0:T(8,128)}, f32[1,1]{1,0:T(1,128)}) custom-call(f32[16,4224]{1,0:T(8,128)S(1)} %get-tuple-element.38.mine, f32[16,4224]{1,0:T(8,128)S(1)} %collective-permute-done.23.up, f32[16,4224]{1,0:T(8,128)S(1)} %collective-permute-done.26.back, f32[8,128]{1,0:T(8,128)S(1)} %scatter_star_gradient.16.refs_0_, ...), custom_call_target="tpu_custom_call" | custom-call | bytes 1024 | tf_op jit(solution)/shard_map/scatter_star_gradient/pallas_call | solution.py:248
  (48 shorter events, 0.3 us)
Async XLA Ops:
  0.6 3.2 %collective-permute-start.6 = (f32[16,4096]{1,0:T(8,128)}, f32[16,4096]{1,0:T(8,128)S(1)}, u32[]{:S(2)}, u32[]{:S(2)}) collective-permute-start(f32[16,4096]{1,0:T(8,128)} %bitcast.6), channel_id=1, source_target_pairs={{0,8},{8,0},{16,24},{24,16},{1,9},{9,1},{17,25},{25,17},{2,10},{10... | collective-permute-start | bytes 786440 | tf_op jit(solution)/shard_map/gather_star_factors/ppermute | solution.py:332
  1.1 7.1 %collective-permute-start = (f32[16,4096]{1,0:T(8,128)}, f32[16,4096]{1,0:T(8,128)S(1)}, u32[]{:S(2)}, u32[]{:S(2)}) collective-permute-start(f32[16,4096]{1,0:T(8,128)} %bitcast.7), channel_id=1, source_target_pairs={{0,2},{2,4},{4,6},{6,7},{7,5},{5,3},{3,1},{1,0},{8,9},{10,8},{12,1... | collective-permute-start | bytes 786440 | tf_op jit(solution)/shard_map/gather_star_factors/ppermute | solution.py:328
  3.8 8.4 %collective-permute-start.7 = (f32[16,4096]{1,0:T(8,128)S(1)}, f32[16,4096]{1,0:T(8,128)S(1)}, u32[]{:S(2)}, u32[]{:S(2)}) collective-permute-start(f32[16,4096]{1,0:T(8,128)S(1)} %collective-permute-done.6), channel_id=1, source_target_pairs={{0,2},{2,4},{4,6},{6,7},{7,5},{5,3},{3,1},{1,0},{8,9},{10,8},{12,1... | collective-permute-start | bytes 786440 | tf_op jit(solution)/shard_map/gather_star_factors/ppermute | solution.py:328
  5.5 2.2 %copy-start = (f32[4096,256]{1,0:T(8,128)S(1)}, f32[4096,256]{1,0:T(8,128)}, u32[]{:S(2)}) copy-start(f32[4096,256]{1,0:T(8,128)} %refs_0_.1) | copy-start | bytes 12582916
  8.0 2.4 %copy-start.2 = (f32[256,32]{0,1:T(8,128)S(1)}, f32[256,32]{0,1:T(8,128)}, u32[]{:S(2)}) copy-start(f32[256,32]{0,1:T(8,128)} %param.7) | copy-start | bytes 98308
  8.0 16.9 %copy-start.1 = (f32[4096,16]{0,1:T(8,128)S(1)}, f32[4096,16]{0,1:T(8,128)}, u32[]{:S(2)}) copy-start(f32[4096,16]{0,1:T(8,128)} %param.6) | copy-start | bytes 786436
  8.3 7.0 %collective-permute-start.1 = (f32[16,4096]{1,0:T(8,128)S(1)}, f32[16,4096]{1,0:T(8,128)S(1)}, u32[]{:S(2)}, u32[]{:S(2)}) collective-permute-start(f32[16,4096]{1,0:T(8,128)S(1)} %gather_star_factors.3.refs_2_.refs_7_), channel_id=1, source_target_pairs={{0,2},{2,4},{4,6},{6,7},{7,5},{5,3},{3,1},{1,0},{8,9},{10,8},{12,1... | collective-permute-start | bytes 786440 | tf_op jit(solution)/shard_map/gather_star_factors/ppermute | solution.py:328
  10.4 3.4 %collective-permute-start.2 = (f32[32,256]{1,0:T(8,128)S(1)}, f32[32,256]{1,0:T(8,128)S(1)}, u32[]{:S(2)}, u32[]{:S(2)}) collective-permute-start(f32[32,256]{1,0:T(8,128)S(1)} %bitcast.10), channel_id=1, source_target_pairs={{0,8},{8,0},{16,24},{24,16},{1,9},{9,1},{17,25},{25,17},{2,10},{10... | collective-permute-start | bytes 98312 | tf_op jit(solution)/shard_map/gather_cadence_factors/ppermute | solution.py:332
  10.4 3.9 %collective-permute-start.3 = (f32[32,256]{1,0:T(8,128)S(1)}, f32[32,256]{1,0:T(8,128)S(1)}, u32[]{:S(2)}, u32[]{:S(2)}) collective-permute-start(f32[32,256]{1,0:T(8,128)S(1)} %bitcast.11), channel_id=1, source_target_pairs={{0,16},{8,24},{16,0},{24,8},{1,17},{9,25},{17,1},{25,9},{2,18},{10... | collective-permute-start | bytes 98312 | tf_op jit(solution)/shard_map/gather_cadence_factors/ppermute | solution.py:332
  11.9 3.3 %collective-permute-start.4 = (f32[32,256]{1,0:T(8,128)S(1)}, f32[32,256]{1,0:T(8,128)S(1)}, u32[]{:S(2)}, u32[]{:S(2)}) collective-permute-start(f32[32,256]{1,0:T(8,128)S(1)} %bitcast.12), channel_id=1, source_target_pairs={{0,24},{8,16},{16,8},{24,0},{1,25},{9,17},{17,9},{25,1},{2,26},{10... | collective-permute-start | bytes 98312 | tf_op jit(solution)/shard_map/gather_cadence_factors/ppermute | solution.py:332
  12.2 6.4 %collective-permute-start.8 = (f32[16,4096]{1,0:T(8,128)S(1)}, f32[16,4096]{1,0:T(8,128)S(1)}, u32[]{:S(2)}, u32[]{:S(2)}) collective-permute-start(f32[16,4096]{1,0:T(8,128)S(1)} %gather_star_factors.5), channel_id=1, source_target_pairs={{0,2},{2,4},{4,6},{6,7},{7,5},{5,3},{3,1},{1,0},{8,9},{10,8},{12,1... | collective-permute-start | bytes 786440 | tf_op jit(solution)/shard_map/gather_star_factors/ppermute | solution.py:328
  15.2 6.4 %collective-permute-start.5 = (f32[16,4096]{1,0:T(8,128)S(1)}, f32[16,4096]{1,0:T(8,128)S(1)}, u32[]{:S(2)}, u32[]{:S(2)}) collective-permute-start(f32[16,4096]{1,0:T(8,128)S(1)} %gather_star_factors.4.refs_3_.refs_8_), channel_id=1, source_target_pairs={{0,2},{2,4},{4,6},{6,7},{7,5},{5,3},{3,1},{1,0},{8,9},{10,8},{12,1... | collective-permute-start | bytes 786440 | tf_op jit(solution)/shard_map/gather_star_factors/ppermute | solution.py:328
  16.8 8.0 %collective-permute-start.10 = (f32[16,4096]{1,0:T(8,128)S(1)}, f32[16,4096]{1,0:T(8,128)S(1)}, u32[]{:S(2)}, u32[]{:S(2)}) collective-permute-start(f32[16,4096]{1,0:T(8,128)S(1)} %gather_star_factors.5), channel_id=1, source_target_pairs={{0,8},{8,0},{16,24},{24,16},{1,9},{9,1},{17,25},{25,17},{2,10},{10... | collective-permute-start | bytes 786440 | tf_op jit(solution)/shard_map/gather_star_factors/ppermute | solution.py:332
  18.6 6.2 %collective-permute-start.9 = (f32[16,4096]{1,0:T(8,128)S(1)}, f32[16,4096]{1,0:T(8,128)S(1)}, u32[]{:S(2)}, u32[]{:S(2)}) collective-permute-start(f32[16,4096]{1,0:T(8,128)S(1)} %collective-permute-done.8), channel_id=1, source_target_pairs={{0,8},{8,0},{16,24},{24,16},{1,9},{9,1},{17,25},{25,17},{2,10},{10... | collective-permute-start | bytes 786440 | tf_op jit(solution)/shard_map/gather_star_factors/ppermute | solution.py:332
  18.6 8.2 %collective-permute-start.12 = (f32[16,4096]{1,0:T(8,128)S(1)}, f32[16,4096]{1,0:T(8,128)S(1)}, u32[]{:S(2)}, u32[]{:S(2)}) collective-permute-start(f32[16,4096]{1,0:T(8,128)S(1)} %collective-permute-done.8), channel_id=1, source_target_pairs={{0,10},{2,12},{4,14},{6,15},{7,13},{5,11},{3,9},{1,8},{8,1},{10,0}... | collective-permute-start | bytes 786440 | tf_op jit(solution)/shard_map/gather_star_factors/ppermute | solution.py:328
  21.6 5.1 %collective-permute-start.11 = (f32[16,2048]{1,0:T(8,128)S(1)}, f32[16,2048]{1,0:T(8,128)S(1)}, u32[]{:S(2)}, u32[]{:S(2)}) collective-permute-start(f32[16,2048]{1,0:T(8,128)S(1)} %get-tuple-element.54), channel_id=1, source_target_pairs={{0,2},{2,4},{4,6},{6,7},{7,5},{5,3},{3,1},{1,0},{8,9},{10,8},{12,1... | collective-permute-start | bytes 393224 | tf_op jit(solution)/shard_map/gather_star_factors/ppermute | solution.py:328
  23.3 3.5 %copy-start.4 = (s32[256]{0:T(256)S(1)}, s32[256]{0:T(256)}, u32[]{:S(2)}) copy-start(s32[256]{0:T(256)} %param.5) | copy-start | bytes 3076
  23.3 5.4 %collective-permute-start.13 = (f32[16,2048]{1,0:T(8,128)S(1)}, f32[16,2048]{1,0:T(8,128)S(1)}, u32[]{:S(2)}, u32[]{:S(2)}) collective-permute-start(f32[16,2048]{1,0:T(8,128)S(1)} %get-tuple-element.53), channel_id=1, source_target_pairs={{0,2},{2,4},{4,6},{6,7},{7,5},{5,3},{3,1},{1,0},{8,9},{10,8},{12,1... | collective-permute-start | bytes 393224 | tf_op jit(solution)/shard_map/gather_star_factors/ppermute | solution.py:328
  30.5 1.6 %collective-permute-start.14 = (f32[16,4224]{1,0:T(8,128)S(1)}, f32[16,4224]{1,0:T(8,128)S(1)}, u32[]{:S(2)}, u32[]{:S(2)}) collective-permute-start(f32[16,4224]{1,0:T(8,128)S(1)} %get-tuple-element.37), channel_id=1, source_target_pairs={{0,8},{8,0},{16,24},{24,16},{1,9},{9,1},{17,25},{25,17},{2,10},{10... | collective-permute-start | bytes 811016 | tf_op jit(solution)/shard_map/ppermute | solution.py:332
  30.6 6.5 %collective-permute-start.15 = (f32[16,4224]{1,0:T(8,128)S(1)}, f32[16,4224]{1,0:T(8,128)S(1)}, u32[]{:S(2)}, u32[]{:S(2)}) collective-permute-start(f32[16,4224]{1,0:T(8,128)S(1)} %get-tuple-element.42), channel_id=1, source_target_pairs={{0,2},{2,4},{4,6},{6,7},{7,5},{5,3},{3,1},{1,0},{8,9},{10,8},{12,1... | collective-permute-start | bytes 811016 | tf_op jit(solution)/shard_map/scatter_star_gradient/ppermute | solution.py:328
  32.2 6.6 %collective-permute-start.17 = (f32[16,4224]{1,0:T(8,128)S(1)}, f32[16,4224]{1,0:T(8,128)S(1)}, u32[]{:S(2)}, u32[]{:S(2)}) collective-permute-start(f32[16,4224]{1,0:T(8,128)S(1)} %get-tuple-element.43), channel_id=1, source_target_pairs={{0,8},{8,0},{16,24},{24,16},{1,9},{9,1},{17,25},{25,17},{2,10},{10... | collective-permute-start | bytes 811016 | tf_op jit(solution)/shard_map/ppermute | solution.py:332
  32.2 7.8 %collective-permute-start.18 = (f32[16,4224]{1,0:T(8,128)S(1)}, f32[16,4224]{1,0:T(8,128)S(1)}, u32[]{:S(2)}, u32[]{:S(2)}) collective-permute-start(f32[16,4224]{1,0:T(8,128)S(1)} %collective-permute-done.14.refs_1_), channel_id=1, source_target_pairs={{0,2},{2,4},{4,6},{6,7},{7,5},{5,3},{3,1},{1,0},{8,9},{10,8},{12,1... | collective-permute-start | bytes 811016 | tf_op jit(solution)/shard_map/scatter_star_gradient/ppermute | solution.py:328
  37.2 6.5 %collective-permute-start.16 = (f32[16,4224]{1,0:T(8,128)S(1)}, f32[16,4224]{1,0:T(8,128)S(1)}, u32[]{:S(2)}, u32[]{:S(2)}) collective-permute-start(f32[16,4224]{1,0:T(8,128)S(1)} %add.15), channel_id=1, source_target_pairs={{0,2},{2,4},{4,6},{6,7},{7,5},{5,3},{3,1},{1,0},{8,9},{10,8},{12,1... | collective-permute-start | bytes 811016 | tf_op jit(solution)/shard_map/scatter_star_gradient/ppermute | solution.py:328
  38.7 7.2 %collective-permute-start.20 = (f32[16,4224]{1,0:T(8,128)S(1)}, f32[16,4224]{1,0:T(8,128)S(1)}, u32[]{:S(2)}, u32[]{:S(2)}) collective-permute-start(f32[16,4224]{1,0:T(8,128)S(1)} %get-tuple-element.44), channel_id=1, source_target_pairs={{0,8},{8,0},{16,24},{24,16},{1,9},{9,1},{17,25},{25,17},{2,10},{10... | collective-permute-start | bytes 811016 | tf_op jit(solution)/shard_map/scatter_star_gradient/ppermute | solution.py:332
  40.1 6.5 %collective-permute-start.21 = (f32[16,4224]{1,0:T(8,128)S(1)}, f32[16,4224]{1,0:T(8,128)S(1)}, u32[]{:S(2)}, u32[]{:S(2)}) collective-permute-start(f32[16,4224]{1,0:T(8,128)S(1)} %add.17.refs_1_), channel_id=1, source_target_pairs={{0,2},{2,4},{4,6},{6,7},{7,5},{5,3},{3,1},{1,0},{8,9},{10,8},{12,1... | collective-permute-start | bytes 811016 | tf_op jit(solution)/shard_map/scatter_star_gradient/ppermute | solution.py:328
  41.6 4.3 %collective-permute-start.22 = (f32[64,256]{1,0:T(8,128)S(1)}, f32[64,256]{1,0:T(8,128)S(1)}, u32[]{:S(2)}, u32[]{:S(2)}) collective-permute-start(f32[64,256]{1,0:T(8,128)S(1)} %scatter_star_gradient.10), channel_id=1, source_target_pairs={{0,16},{8,24},{16,0},{24,8},{1,17},{9,25},{17,1},{25,9},{2,18},{10... | collective-permute-start | bytes 196616 | tf_op jit(solution)/shard_map/scatter_star_gradient/ppermute | solution.py:332
  43.7 6.5 %collective-permute-start.19 = (f32[16,4224]{1,0:T(8,128)S(1)}, f32[16,4224]{1,0:T(8,128)S(1)}, u32[]{:S(2)}, u32[]{:S(2)}) collective-permute-start(f32[16,4224]{1,0:T(8,128)S(1)} %scatter_star_gradient.9), channel_id=1, source_target_pairs={{0,2},{2,4},{4,6},{6,7},{7,5},{5,3},{3,1},{1,0},{8,9},{10,8},{12,1... | collective-permute-start | bytes 811016 | tf_op jit(solution)/shard_map/scatter_star_gradient/ppermute | solution.py:328
  46.6 7.3 %collective-permute-start.24 = (f32[16,4224]{1,0:T(8,128)S(1)}, f32[16,4224]{1,0:T(8,128)S(1)}, u32[]{:S(2)}, u32[]{:S(2)}) collective-permute-start(f32[16,4224]{1,0:T(8,128)S(1)} %scatter_star_gradient.12.refs_1_), channel_id=1, source_target_pairs={{0,2},{2,4},{4,6},{6,7},{7,5},{5,3},{3,1},{1,0},{8,9},{10,8},{12,1... | collective-permute-start | bytes 811016 | tf_op jit(solution)/shard_map/scatter_star_gradient/ppermute | solution.py:328
  48.2 3.6 %collective-permute-start.25 = (f32[32,256]{1,0:T(8,128)S(1)}, f32[32,256]{1,0:T(8,128)S(1)}, u32[]{:S(2)}, u32[]{:S(2)}) collective-permute-start(f32[32,256]{1,0:T(8,128)S(1)} %get-tuple-element.49), channel_id=1, source_target_pairs={{0,8},{8,0},{16,24},{24,16},{1,9},{9,1},{17,25},{25,17},{2,10},{10... | collective-permute-start | bytes 98312 | tf_op jit(solution)/shard_map/scatter_star_gradient/ppermute | solution.py:332
  50.3 3.7 %collective-permute-start.27 = (f32[8,128]{1,0:T(8,128)S(1)}, f32[8,128]{1,0:T(8,128)S(1)}, u32[]{:S(2)}, u32[]{:S(2)}) collective-permute-start(f32[8,128]{1,0:T(8,128)S(1)} %get-tuple-element.50), channel_id=1, source_target_pairs={{0,2},{2,4},{4,6},{6,7},{7,5},{5,3},{3,1},{1,0},{8,9},{10,8},{12,1... | collective-permute-start | bytes 12296 | tf_op jit(solution)/shard_map/scatter_star_gradient/ppermute | solution.py:328
  51.8 7.9 %copy-start.3 = (f32[32,256]{1,0:T(8,128)}, f32[32,256]{1,0:T(8,128)S(1)}, u32[]{:S(2)}) copy-start(f32[32,256]{1,0:T(8,128)S(1)} %add.19.refs_1_) | copy-start | bytes 98308
  51.9 6.5 %collective-permute-start.23 = (f32[16,4224]{1,0:T(8,128)S(1)}, f32[16,4224]{1,0:T(8,128)S(1)}, u32[]{:S(2)}, u32[]{:S(2)}) collective-permute-start(f32[16,4224]{1,0:T(8,128)S(1)} %get-tuple-element.48), channel_id=1, source_target_pairs={{0,2},{2,4},{4,6},{6,7},{7,5},{5,3},{3,1},{1,0},{8,9},{10,8},{12,1... | collective-permute-start | bytes 811016 | tf_op jit(solution)/shard_map/scatter_star_gradient/ppermute | solution.py:328
  53.9 5.1 %collective-permute-start.26 = (f32[16,4224]{1,0:T(8,128)S(1)}, f32[16,4224]{1,0:T(8,128)S(1)}, u32[]{:S(2)}, u32[]{:S(2)}) collective-permute-start(f32[16,4224]{1,0:T(8,128)S(1)} %scatter_star_gradient.15), channel_id=1, source_target_pairs={{0,8},{8,0},{16,24},{24,16},{1,9},{9,1},{17,25},{25,17},{2,10},{10... | collective-permute-start | bytes 811016 | tf_op jit(solution)/shard_map/scatter_star_gradient/ppermute | solution.py:332
  54.0 4.3 %collective-permute-start.28 = (f32[8,128]{1,0:T(8,128)S(1)}, f32[8,128]{1,0:T(8,128)S(1)}, u32[]{:S(2)}, u32[]{:S(2)}) collective-permute-start(f32[8,128]{1,0:T(8,128)S(1)} %scatter_star_gradient.16.refs_0_), channel_id=1, source_target_pairs={{0,8},{8,0},{16,24},{24,16},{1,9},{9,1},{17,25},{25,17},{2,10},{10... | collective-permute-start | bytes 12296 | tf_op jit(solution)/shard_map/scatter_star_gradient/ppermute | solution.py:332
  54.5 3.9 %collective-permute-start.29 = (f32[8,128]{1,0:T(8,128)S(1)}, f32[8,128]{1,0:T(8,128)S(1)}, u32[]{:S(2)}, u32[]{:S(2)}) collective-permute-start(f32[8,128]{1,0:T(8,128)S(1)} %scatter_star_gradient.16.refs_0_), channel_id=1, source_target_pairs={{0,16},{8,24},{16,0},{24,8},{1,17},{9,25},{17,1},{25,9},{2,18},{10... | collective-permute-start | bytes 12296 | tf_op jit(solution)/shard_map/scatter_star_gradient/ppermute | solution.py:332
  56.0 3.0 %collective-permute-start.30 = (f32[8,128]{1,0:T(8,128)S(1)}, f32[8,128]{1,0:T(8,128)S(1)}, u32[]{:S(2)}, u32[]{:S(2)}) collective-permute-start(f32[8,128]{1,0:T(8,128)S(1)} %scatter_star_gradient.16.refs_0_), channel_id=1, source_target_pairs={{0,24},{8,16},{16,8},{24,0},{1,25},{9,17},{17,9},{25,1},{2,26},{10... | collective-permute-start | bytes 12296 | tf_op jit(solution)/shard_map/scatter_star_gradient/ppermute | solution.py:332

commit v5 on v4

--- a/solution.py
+++ b/solution.py
@@ -243,15 +243,15 @@
     return list(big_call(functools.partial(sums_body, plan), given, out, scratch, 6 * count * nc * rank))
 
 
-def small_call(body_of, given, shapes, limit=4):
+def small_call(body_of, given, shapes, weight=0):
     vmem = pl.BlockSpec(memory_space=pltpu.VMEM)
     return pl.pallas_call(
         body_of,
         in_specs=[vmem] * len(given),
         out_specs=[vmem] * len(shapes),
         out_shape=[jax.ShapeDtypeStruct(shape, F32) for shape in shapes],
-        cost_estimate=pl.CostEstimate(flops=0, bytes_accessed=1 << 10, transcendentals=0),
-        compiler_params=pltpu.CompilerParams(vmem_limit_bytes=limit << 20),
+        cost_estimate=pl.CostEstimate(flops=weight, bytes_accessed=1 << 10, transcendentals=0),
+        compiler_params=pltpu.CompilerParams(vmem_limit_bytes=4 << 20),
     )(*given)
 
 
@@ -297,20 +297,29 @@
 
 
 def loss_part(loss, near, beside):
-    return small_call(loss_part_body, [loss, near, beside], [(8, 128)])[0]
-
-
-def last_stars_body(factor, mine, up, back, *refs):
-    *losses, out, total = refs
+    return small_call(loss_part_body, [loss, near, beside], [(8, 128)], weight=3 * 10**9)[0]
+
+
+def add_losses_body(*refs):
+    refs[-1][...] = sum(ref[...] for ref in refs[:-1])
+
+
+def add_losses(losses):
+    return small_call(add_losses_body, losses, [(8, 128)])[0]
+
+
+def last_sums_body(factor, mine, up, back, keep, got, *refs):
+    *losses, out, cad_out, total = refs
     width = out.shape[1]
     out[...] = mine[:, :width] + up[:, :width] + back[:, :width]
+    cad_out[...] = keep[...] + got[...]
     total[...] = jnp.sum(sum(ref[...] for ref in losses), keepdims=True) * factor
 
 
-def last_stars(mine, up, back, losses, factor):
+def last_sums(mine, up, back, kept, losses, factor):
     rows, width = mine.shape
-    shapes = [(rows, width - 128), (1, 1)]
-    return small_call(functools.partial(last_stars_body, factor), [mine, up, back] + losses, shapes)
+    shapes = [(rows, width - 128), kept[0].shape, (1, 1)]
+    return small_call(functools.partial(last_sums_body, factor), [mine, up, back] + kept + losses, shapes)
 
 
 def ring_order(n):
@@ -394,16 +403,16 @@
         keep, send = halve(keep, swap(hold(send, message), "star", 2))
         beside = shift(message)
         up = shift(hold(terms[far + 2] + up, message))
-        cad_gradient = keep + swap(send, "star", 1)
         message = hold(swap(terms[1], "star", 1) + beside, keep)
-        beside = shift(message)
+        beside = shift(message, 1)
         message, near = add_part(terms[far + 3], hold(up, message))
         near = shift(near)
         up = shift(message)
-        back = swap(hold(beside, cad_gradient), "star", 1)
         part = loss_part(loss, near, beside)
-        losses = [part] + [swap(part, "star", bit) for bit in range(1, m)]
-        star_gradient, total = last_stars(terms[0], up, back, losses, factor)
+        part = add_losses([part, swap(part, "star", 1)])
+        losses = [part, swap(part, "star", 2)]
+        kept = [keep, swap(hold(send, beside), "star", 1)]
+        star_gradient, cad_gradient, total = last_sums(terms[0], up, beside, kept, losses, factor)
     return (star_gradient.T, cad_gradient.T, total[0, 0])
 
 

time: 59.9 us -> 59.6 us (level)
  starting transfers between devices: 32.9 us -> 30.8 us
  waiting for transfers between devices: 14.2 us -> 16 us
    ppermute x16, starting transfers between devices: 26.9 us -> 25.4 us  [shift(): return lax.ppermute(x, ('star', 'cad'), pairs)]
    ppermute x15 -> x13, waiting for transfers between devices: 2.7 us -> 3.63 us  [swap(): lax.ppermute(x, axis, [(i, i ^ bit) for i in range(lax.axis_size(axis))])]
    ppermute x16, waiting for transfers between devices: 11.5 us -> 12.4 us  [shift(): return lax.ppermute(x, ('star', 'cad'), pairs)]
    ppermute x15 -> x13, starting transfers between devices: 6.01 us -> 5.43 us  [swap(): lax.ppermute(x, axis, [(i, i ^ bit) for i in range(lax.axis_size(axis))])]
    unnamed x10 -> x8, local copies, waits for them, and re-layouts: 2.21 us -> 2.2 us
  transfers between devices with their start and end apart: 31 -> 29, of which waited for: 14 -> 15; matrix products, arithmetic and copies ran while one was open for 0% -> 0% of each run, Pallas kernels for 12% -> 12%
where the time goes in v5:
time: 59.6 us; the launch traced here: 59.5 us
  starting transfers between devices  30.8 us (52%)
  waiting for transfers between devices  16 us (27%)
  Pallas kernels  9.53 us (16%)
  local copies, waits for them, and re-layouts  2.22 us (4%)
  between operations  0.79 us (1%)
    ppermute x16, starting transfers between devices, shift(): return lax.ppermute(x, ('star', 'cad'), pairs)  25.4 us
    ppermute x16, waiting for transfers between devices, shift(): return lax.ppermute(x, ('star', 'cad'), pairs)  12.4 us
    pallas_call x4, Pallas kernels, big_call(): pl.pallas_call(body_of, in_specs=[vmem] * len(given), out_specs=[vmem] *...  8.43 us
    ppermute x13, starting transfers between devices, swap(): lax.ppermute(x, axis, [(i, i ^ bit) for i in range(lax.axis_size(axis))])  5.43 us
    ppermute x13, waiting for transfers between devices, swap(): lax.ppermute(x, axis, [(i, i ^ bit) for i in range(lax.axis_size(axis))])  3.63 us
    unnamed x8, local copies, waits for them, and re-layouts  2.2 us
  transfers between devices with their start and end apart: 29, of which 15 were waited for; matrix products, arithmetic and copies ran while one was open for 0% of the time, Pallas kernels for 12%

profile of v5, /device:TPU:0, one launch (start us, length us, event | category | flops | bytes accessed | tf_op | source)
XLA Modules:
  0.0 59.5 jit_solution(1063337247385367957)
XLA Ops:
  0.6 0.5 collective-permute-start.6
  1.1 2.6 %collective-permute-start = (f32[16,4096]{1,0:T(8,128)}, f32[16,4096]{1,0:T(8,128)S(1)}, u32[]{:S(2)}, u32[]{:S(2)}) collective-permute-start(f32[16,4096]{1,0:T(8,128)} %bitcast.7), channel_id=1, source_target_pairs={{0,2},{2,4},{4,6},{6,7},{7,5},{5,3},{3,1},{1,0},{8,9},{10,8},{12,1... | collective-permute-start | bytes 786440 | tf_op jit(solution)/shard_map/gather_star_factors/ppermute | solution.py:337
  3.8 0.0 collective-permute-done.6
  3.8 1.7 %collective-permute-start.7 = (f32[16,4096]{1,0:T(8,128)S(1)}, f32[16,4096]{1,0:T(8,128)S(1)}, u32[]{:S(2)}, u32[]{:S(2)}) collective-permute-start(f32[16,4096]{1,0:T(8,128)S(1)} %collective-permute-done.6), channel_id=1, source_target_pairs={{0,2},{2,4},{4,6},{6,7},{7,5},{5,3},{3,1},{1,0},{8,9},{10,8},{12,1... | collective-permute-start | bytes 786440 | tf_op jit(solution)/shard_map/gather_star_factors/ppermute | solution.py:337
  5.5 2.2 %copy-done = f32[4096,256]{1,0:T(8,128)S(1)} copy-done((f32[4096,256]{1,0:T(8,128)S(1)}, f32[4096,256]{1,0:T(8,128)}, u32[]{:S(2)}) %copy-start) | copy-done | bytes 4194328
  7.7 0.3 shard_map.67.refs_1_.refs_0_
  8.0 0.0 copy-start.2
  8.0 0.0 copy-start.1
  8.0 0.3 collective-permute-done.refs_0_
  8.3 2.1 %collective-permute-start.1 = (f32[16,4096]{1,0:T(8,128)S(1)}, f32[16,4096]{1,0:T(8,128)S(1)}, u32[]{:S(2)}, u32[]{:S(2)}) collective-permute-start(f32[16,4096]{1,0:T(8,128)S(1)} %gather_star_factors.3.refs_2_.refs_7_), channel_id=1, source_target_pairs={{0,2},{2,4},{4,6},{6,7},{7,5},{5,3},{3,1},{1,0},{8,9},{10,8},{12,1... | collective-permute-start | bytes 786440 | tf_op jit(solution)/shard_map/gather_star_factors/ppermute | solution.py:337
  10.4 0.0 collective-permute-start.2
  10.4 1.5 %collective-permute-start.3 = (f32[32,256]{1,0:T(8,128)S(1)}, f32[32,256]{1,0:T(8,128)S(1)}, u32[]{:S(2)}, u32[]{:S(2)}) collective-permute-start(f32[32,256]{1,0:T(8,128)S(1)} %bitcast.11), channel_id=1, source_target_pairs={{0,16},{8,24},{16,0},{24,8},{1,17},{9,25},{17,1},{25,9},{2,18},{10... | collective-permute-start | bytes 98312 | tf_op jit(solution)/shard_map/gather_cadence_factors/ppermute | solution.py:341
  11.9 0.3 collective-permute-start.4
  12.2 1.6 %collective-permute-start.8 = (f32[16,4096]{1,0:T(8,128)S(1)}, f32[16,4096]{1,0:T(8,128)S(1)}, u32[]{:S(2)}, u32[]{:S(2)}) collective-permute-start(f32[16,4096]{1,0:T(8,128)S(1)} %gather_star_factors.5), channel_id=1, source_target_pairs={{0,2},{2,4},{4,6},{6,7},{7,5},{5,3},{3,1},{1,0},{8,9},{10,8},{12,1... | collective-permute-start | bytes 786440 | tf_op jit(solution)/shard_map/gather_star_factors/ppermute | solution.py:337
  13.8 0.5 collective-permute-done.3.refs_2_.refs_9_.refs_6_.refs_17_
  14.3 0.9 %collective-permute-done.4.refs_3_.refs_10_.refs_7_.refs_18_ = f32[32,256]{1,0:T(8,128)S(1)} collective-permute-done((f32[32,256]{1,0:T(8,128)S(1)}, f32[32,256]{1,0:T(8,128)S(1)}, u32[]{:S(2)}, u32[]{:S(2)}) %collective-permute-start.4) | collective-permute-done | bytes 32800 | tf_op jit(solution)/shard_map/gather_cadence_factors/ppermute | solution.py:341
  15.2 1.6 %collective-permute-start.5 = (f32[16,4096]{1,0:T(8,128)S(1)}, f32[16,4096]{1,0:T(8,128)S(1)}, u32[]{:S(2)}, u32[]{:S(2)}) collective-permute-start(f32[16,4096]{1,0:T(8,128)S(1)} %gather_star_factors.4.refs_3_.refs_8_), channel_id=1, source_target_pairs={{0,2},{2,4},{4,6},{6,7},{7,5},{5,3},{3,1},{1,0},{8,9},{10,8},{12,1... | collective-permute-start | bytes 786440 | tf_op jit(solution)/shard_map/gather_star_factors/ppermute | solution.py:337
  16.8 1.8 %collective-permute-done.8 = f32[16,4096]{1,0:T(8,128)S(1)} collective-permute-done((f32[16,4096]{1,0:T(8,128)S(1)}, f32[16,4096]{1,0:T(8,128)S(1)}, u32[]{:S(2)}, u32[]{:S(2)}) %collective-permute-start.8) | collective-permute-done | bytes 262176 | tf_op jit(solution)/shard_map/gather_star_factors/ppermute | solution.py:337
  18.6 1.7 %collective-permute-start.12 = (f32[16,4096]{1,0:T(8,128)S(1)}, f32[16,4096]{1,0:T(8,128)S(1)}, u32[]{:S(2)}, u32[]{:S(2)}) collective-permute-start(f32[16,4096]{1,0:T(8,128)S(1)} %collective-permute-done.8), channel_id=1, source_target_pairs={{0,10},{2,12},{4,14},{6,15},{7,13},{5,11},{3,9},{1,8},{8,1},{10,0}... | collective-permute-start | bytes 786440 | tf_op jit(solution)/shard_map/gather_star_factors/ppermute | solution.py:337
  20.3 1.3 %collective-permute-done.5.refs_4_.refs_9_ = f32[16,4096]{1,0:T(8,128)S(1)} collective-permute-done((f32[16,4096]{1,0:T(8,128)S(1)}, f32[16,4096]{1,0:T(8,128)S(1)}, u32[]{:S(2)}, u32[]{:S(2)}) %collective-permute-start.5) | collective-permute-done | bytes 262176 | tf_op jit(solution)/shard_map/gather_star_factors/ppermute | solution.py:337
  21.6 1.6 %collective-permute-start.11 = (f32[16,2048]{1,0:T(8,128)S(1)}, f32[16,2048]{1,0:T(8,128)S(1)}, u32[]{:S(2)}, u32[]{:S(2)}) collective-permute-start(f32[16,2048]{1,0:T(8,128)S(1)} %get-tuple-element.56), channel_id=1, source_target_pairs={{0,2},{2,4},{4,6},{6,7},{7,5},{5,3},{3,1},{1,0},{8,9},{10,8},{12,1... | collective-permute-start | bytes 393224 | tf_op jit(solution)/shard_map/gather_star_factors/ppermute | solution.py:337
  23.3 1.6 %collective-permute-start.13 = (f32[16,2048]{1,0:T(8,128)S(1)}, f32[16,2048]{1,0:T(8,128)S(1)}, u32[]{:S(2)}, u32[]{:S(2)}) collective-permute-start(f32[16,2048]{1,0:T(8,128)S(1)} %get-tuple-element.55), channel_id=1, source_target_pairs={{0,2},{2,4},{4,6},{6,7},{7,5},{5,3},{3,1},{1,0},{8,9},{10,8},{12,1... | collective-permute-start | bytes 393224 | tf_op jit(solution)/shard_map/gather_star_factors/ppermute | solution.py:337
  24.9 1.9 %shard_map.68.refs_0_ = f32[4096,256]{1,0:T(8,128)S(1)} custom-call(f32[4096,256]{1,0:T(8,128)S(1)} %shard_map.67.refs_1_.refs_0_, f32[16,4096]{1,0:T(8,128)S(1)} %bitcast.8, f32[16,4096]{1,0:T(8,128)S(1)} %gather_star_factors.3.refs_2_.refs_7_, f32[16,4096]{1,0:T(8,128)S(1)} %gather_star_factors.4.refs_3_.refs_8_, ...), custom_call_target="tpu_custom_call" | custom-call | flops 1610612736 | bytes 1048576 | tf_op jit(solution)/shard_map/pallas_call | solution.py:195
  26.8 1.9 %shard_map.69 = (bf16[2048,256]{1,0:T(8,128)(2,1)S(1)}, bf16[2048,256]{1,0:T(8,128)(2,1)S(1)}, f32[8,256]{1,0:T(8,128)S(1)}, f32[16,2048]{1,0:T(8,128)S(1)}, f32...) custom-call(f32[4096,256]{1,0:T(8,128)S(1)} %shard_map.68.refs_0_, s32[1,256]{1,0:T(1,128)S(1)} %bitcast.17, ...), custom_call_target="tpu_custom_call" | custom-call | flops 536870912 | bytes 1048576 | tf_op jit(solution)/shard_map/pallas_call | solution.py:195
  28.7 1.9 %shard_map.70 = (bf16[2048,256]{1,0:T(8,128)(2,1)S(1)}, bf16[2048,256]{1,0:T(8,128)(2,1)S(1)}, f32[8,128]{1,0:T(8,128)S(1)}, f32[16,4224]{1,0:T(8,128)S(1)}, f32...) custom-call(f32[4096,256]{1,0:T(8,128)S(1)} %shard_map.68.refs_0_, s32[1,256]{1,0:T(1,128)S(1)} %bitcast.18, ...), custom_call_target="tpu_custom_call" | custom-call | flops 536870912 | bytes 1048576 | tf_op jit(solution)/shard_map/pallas_call | solution.py:195
  30.5 0.1 collective-permute-start.14
  30.6 1.6 %collective-permute-start.15 = (f32[16,4224]{1,0:T(8,128)S(1)}, f32[16,4224]{1,0:T(8,128)S(1)}, u32[]{:S(2)}, u32[]{:S(2)}) collective-permute-start(f32[16,4224]{1,0:T(8,128)S(1)} %get-tuple-element.43), channel_id=1, source_target_pairs={{0,2},{2,4},{4,6},{6,7},{7,5},{5,3},{3,1},{1,0},{8,9},{10,8},{12,1... | collective-permute-start | bytes 811016 | tf_op jit(solution)/shard_map/scatter_star_gradient/ppermute | solution.py:337
  32.2 1.5 %collective-permute-start.18 = (f32[16,4224]{1,0:T(8,128)S(1)}, f32[16,4224]{1,0:T(8,128)S(1)}, u32[]{:S(2)}, u32[]{:S(2)}) collective-permute-start(f32[16,4224]{1,0:T(8,128)S(1)} %collective-permute-done.14.refs_1_), channel_id=1, source_target_pairs={{0,2},{2,4},{4,6},{6,7},{7,5},{5,3},{3,1},{1,0},{8,9},{10,8},{12,1... | collective-permute-start | bytes 811016 | tf_op jit(solution)/shard_map/scatter_star_gradient/ppermute | solution.py:337
  33.7 2.8 %shard_map.72 = (f32[16,4224]{1,0:T(8,128)S(1)}, f32[16,4224]{1,0:T(8,128)S(1)}, f32[16,4224]{1,0:T(8,128)S(1)}, f32[16,4224]{1,0:T(8,128)S(1)}, f32[16,4224]{1,...) custom-call(bf16[2048,256]{1,0:T(8,128)(2,1)S(1)} %get-tuple-element.29.refs_0_, ...), custom_call_target="tpu_custom_call" | custom-call | flops 1610612736 | bytes 1048576 | tf_op jit(solution)/shard_map/pallas_call | solution.py:195
  36.5 0.6 %collective-permute-done.15 = f32[16,4224]{1,0:T(8,128)S(1)} collective-permute-done((f32[16,4224]{1,0:T(8,128)S(1)}, f32[16,4224]{1,0:T(8,128)S(1)}, u32[]{:S(2)}, u32[]{:S(2)}) %collective-permute-start.15) | collective-permute-done | bytes 270368 | tf_op jit(solution)/shard_map/scatter_star_gradient/ppermute | solution.py:337
  37.2 1.6 %collective-permute-start.16 = (f32[16,4224]{1,0:T(8,128)S(1)}, f32[16,4224]{1,0:T(8,128)S(1)}, u32[]{:S(2)}, u32[]{:S(2)}) collective-permute-start(f32[16,4224]{1,0:T(8,128)S(1)} %add.12), channel_id=1, source_target_pairs={{0,2},{2,4},{4,6},{6,7},{7,5},{5,3},{3,1},{1,0},{8,9},{10,8},{12,1... | collective-permute-start | bytes 811016 | tf_op jit(solution)/shard_map/scatter_star_gradient/ppermute | solution.py:337
  38.7 1.3 %collective-permute-done.18 = f32[16,4224]{1,0:T(8,128)S(1)} collective-permute-done((f32[16,4224]{1,0:T(8,128)S(1)}, f32[16,4224]{1,0:T(8,128)S(1)}, u32[]{:S(2)}, u32[]{:S(2)}) %collective-permute-start.18) | collective-permute-done | bytes 270368 | tf_op jit(solution)/shard_map/scatter_star_gradient/ppermute | solution.py:337
  40.1 1.6 %collective-permute-start.21 = (f32[16,4224]{1,0:T(8,128)S(1)}, f32[16,4224]{1,0:T(8,128)S(1)}, u32[]{:S(2)}, u32[]{:S(2)}) collective-permute-start(f32[16,4224]{1,0:T(8,128)S(1)} %add.14.refs_1_), channel_id=1, source_target_pairs={{0,2},{2,4},{4,6},{6,7},{7,5},{5,3},{3,1},{1,0},{8,9},{10,8},{12,1... | collective-permute-start | bytes 811016 | tf_op jit(solution)/shard_map/scatter_star_gradient/ppermute | solution.py:337
  41.6 1.5 %collective-permute-start.22 = (f32[64,256]{1,0:T(8,128)S(1)}, f32[64,256]{1,0:T(8,128)S(1)}, u32[]{:S(2)}, u32[]{:S(2)}) collective-permute-start(f32[64,256]{1,0:T(8,128)S(1)} %scatter_star_gradient.11), channel_id=1, source_target_pairs={{0,16},{8,24},{16,0},{24,8},{1,17},{9,25},{17,1},{25,9},{2,18},{10... | collective-permute-start | bytes 196616 | tf_op jit(solution)/shard_map/scatter_star_gradient/ppermute | solution.py:341
  43.1 0.5 collective-permute-done.16
  43.7 1.6 %collective-permute-start.19 = (f32[16,4224]{1,0:T(8,128)S(1)}, f32[16,4224]{1,0:T(8,128)S(1)}, u32[]{:S(2)}, u32[]{:S(2)}) collective-permute-start(f32[16,4224]{1,0:T(8,128)S(1)} %scatter_star_gradient.10), channel_id=1, source_target_pairs={{0,2},{2,4},{4,6},{6,7},{7,5},{5,3},{3,1},{1,0},{8,9},{10,8},{12,1... | collective-permute-start | bytes 811016 | tf_op jit(solution)/shard_map/scatter_star_gradient/ppermute | solution.py:337
  45.3 0.6 %collective-permute-done.22.got = f32[64,256]{1,0:T(8,128)S(1)} collective-permute-done((f32[64,256]{1,0:T(8,128)S(1)}, f32[64,256]{1,0:T(8,128)S(1)}, u32[]{:S(2)}, u32[]{:S(2)}) %collective-permute-start.22) | collective-permute-done | bytes 65568 | tf_op jit(solution)/shard_map/scatter_star_gradient/ppermute | solution.py:341
  45.9 0.7 %collective-permute-done.21 = f32[16,4224]{1,0:T(8,128)S(1)} collective-permute-done((f32[16,4224]{1,0:T(8,128)S(1)}, f32[16,4224]{1,0:T(8,128)S(1)}, u32[]{:S(2)}, u32[]{:S(2)}) %collective-permute-start.21) | collective-permute-done | bytes 270368 | tf_op jit(solution)/shard_map/scatter_star_gradient/ppermute | solution.py:337
  46.6 0.1 collective-permute-start.24
  46.7 3.5 %collective-permute-done.19.refs_0_ = f32[16,4224]{1,0:T(8,128)S(1)} collective-permute-done((f32[16,4224]{1,0:T(8,128)S(1)}, f32[16,4224]{1,0:T(8,128)S(1)}, u32[]{:S(2)}, u32[]{:S(2)}) %collective-permute-start.19) | collective-permute-done | bytes 270368 | tf_op jit(solution)/shard_map/scatter_star_gradient/ppermute | solution.py:337
  50.3 1.6 %collective-permute-start.26 = (f32[8,128]{1,0:T(8,128)S(1)}, f32[8,128]{1,0:T(8,128)S(1)}, u32[]{:S(2)}, u32[]{:S(2)}) collective-permute-start(f32[8,128]{1,0:T(8,128)S(1)} %get-tuple-element.51), channel_id=1, source_target_pairs={{0,2},{2,4},{4,6},{6,7},{7,5},{5,3},{3,1},{1,0},{8,9},{10,8},{12,1... | collective-permute-start | bytes 12296 | tf_op jit(solution)/shard_map/scatter_star_gradient/ppermute | solution.py:337
  51.8 1.5 %collective-permute-start.23 = (f32[16,4224]{1,0:T(8,128)S(1)}, f32[16,4224]{1,0:T(8,128)S(1)}, u32[]{:S(2)}, u32[]{:S(2)}) collective-permute-start(f32[16,4224]{1,0:T(8,128)S(1)} %get-tuple-element.49), channel_id=1, source_target_pairs={{0,2},{2,4},{4,6},{6,7},{7,5},{5,3},{3,1},{1,0},{8,9},{10,8},{12,1... | collective-permute-start | bytes 811016 | tf_op jit(solution)/shard_map/scatter_star_gradient/ppermute | solution.py:337
  53.4 0.6 collective-permute-done.26.near
  53.9 1.2 %collective-permute-done.27.refs_1_ = f32[8,128]{1,0:T(8,128)S(1)} collective-permute-done((f32[8,128]{1,0:T(8,128)S(1)}, f32[8,128]{1,0:T(8,128)S(1)}, u32[]{:S(2)}, u32[]{:S(2)}) %collective-permute-start.27) | collective-permute-done | bytes 4128 | tf_op jit(solution)/shard_map/scatter_star_gradient/ppermute | solution.py:341
  55.1 1.4 %collective-permute-start.28 = (f32[8,128]{1,0:T(8,128)S(1)}, f32[8,128]{1,0:T(8,128)S(1)}, u32[]{:S(2)}, u32[]{:S(2)}) collective-permute-start(f32[8,128]{1,0:T(8,128)S(1)} %scatter_star_gradient.18.refs_0_), channel_id=1, source_target_pairs={{0,16},{8,24},{16,0},{24,8},{1,17},{9,25},{17,1},{25,9},{2,18},{10... | collective-permute-start | bytes 12296 | tf_op jit(solution)/shard_map/scatter_star_gradient/ppermute | solution.py:341
  56.5 1.7 %collective-permute-done.23.up = f32[16,4224]{1,0:T(8,128)S(1)} collective-permute-done((f32[16,4224]{1,0:T(8,128)S(1)}, f32[16,4224]{1,0:T(8,128)S(1)}, u32[]{:S(2)}, u32[]{:S(2)}) %collective-permute-start.23) | collective-permute-done | bytes 270368 | tf_op jit(solution)/shard_map/scatter_star_gradient/ppermute | solution.py:337
  58.3 0.4 collective-permute-done.28.refs_1_
  58.7 0.8 %scatter_star_gradient.19 = (f32[16,4096]{1,0:T(8,128)}, f32[32,256]{1,0:T(8,128)}, f32[1,1]{1,0:T(1,128)}) custom-call(f32[16,4224]{1,0:T(8,128)S(1)} %get-tuple-element.39.mine, f32[16,4224]{1,0:T(8,128)S(1)} %collective-permute-done.23.up, f32[16,4224]{1,0:T(8,128)S(1)} %collective-permute-done.24.refs_1_.beside.back, ...), custom_call_target="tpu_custom_call" | custom-call | bytes 1024 | tf_op jit(solution)/shard_map/scatter_star_gradient/pallas_call | solution.py:248
  (42 shorter events, 0.3 us)
Async XLA Ops:
  0.6 3.2 %collective-permute-start.6 = (f32[16,4096]{1,0:T(8,128)}, f32[16,4096]{1,0:T(8,128)S(1)}, u32[]{:S(2)}, u32[]{:S(2)}) collective-permute-start(f32[16,4096]{1,0:T(8,128)} %bitcast.6), channel_id=1, source_target_pairs={{0,8},{8,0},{16,24},{24,16},{1,9},{9,1},{17,25},{25,17},{2,10},{10... | collective-permute-start | bytes 786440 | tf_op jit(solution)/shard_map/gather_star_factors/ppermute | solution.py:341
  1.1 7.1 %collective-permute-start = (f32[16,4096]{1,0:T(8,128)}, f32[16,4096]{1,0:T(8,128)S(1)}, u32[]{:S(2)}, u32[]{:S(2)}) collective-permute-start(f32[16,4096]{1,0:T(8,128)} %bitcast.7), channel_id=1, source_target_pairs={{0,2},{2,4},{4,6},{6,7},{7,5},{5,3},{3,1},{1,0},{8,9},{10,8},{12,1... | collective-permute-start | bytes 786440 | tf_op jit(solution)/shard_map/gather_star_factors/ppermute | solution.py:337
  3.8 8.4 %collective-permute-start.7 = (f32[16,4096]{1,0:T(8,128)S(1)}, f32[16,4096]{1,0:T(8,128)S(1)}, u32[]{:S(2)}, u32[]{:S(2)}) collective-permute-start(f32[16,4096]{1,0:T(8,128)S(1)} %collective-permute-done.6), channel_id=1, source_target_pairs={{0,2},{2,4},{4,6},{6,7},{7,5},{5,3},{3,1},{1,0},{8,9},{10,8},{12,1... | collective-permute-start | bytes 786440 | tf_op jit(solution)/shard_map/gather_star_factors/ppermute | solution.py:337
  5.5 2.2 %copy-start = (f32[4096,256]{1,0:T(8,128)S(1)}, f32[4096,256]{1,0:T(8,128)}, u32[]{:S(2)}) copy-start(f32[4096,256]{1,0:T(8,128)} %refs_0_.1) | copy-start | bytes 12582916
  8.0 2.4 %copy-start.2 = (f32[256,32]{0,1:T(8,128)S(1)}, f32[256,32]{0,1:T(8,128)}, u32[]{:S(2)}) copy-start(f32[256,32]{0,1:T(8,128)} %param.7) | copy-start | bytes 98308
  8.0 16.9 %copy-start.1 = (f32[4096,16]{0,1:T(8,128)S(1)}, f32[4096,16]{0,1:T(8,128)}, u32[]{:S(2)}) copy-start(f32[4096,16]{0,1:T(8,128)} %param.6) | copy-start | bytes 786436
  8.3 7.0 %collective-permute-start.1 = (f32[16,4096]{1,0:T(8,128)S(1)}, f32[16,4096]{1,0:T(8,128)S(1)}, u32[]{:S(2)}, u32[]{:S(2)}) collective-permute-start(f32[16,4096]{1,0:T(8,128)S(1)} %gather_star_factors.3.refs_2_.refs_7_), channel_id=1, source_target_pairs={{0,2},{2,4},{4,6},{6,7},{7,5},{5,3},{3,1},{1,0},{8,9},{10,8},{12,1... | collective-permute-start | bytes 786440 | tf_op jit(solution)/shard_map/gather_star_factors/ppermute | solution.py:337
  10.4 3.4 %collective-permute-start.2 = (f32[32,256]{1,0:T(8,128)S(1)}, f32[32,256]{1,0:T(8,128)S(1)}, u32[]{:S(2)}, u32[]{:S(2)}) collective-permute-start(f32[32,256]{1,0:T(8,128)S(1)} %bitcast.10), channel_id=1, source_target_pairs={{0,8},{8,0},{16,24},{24,16},{1,9},{9,1},{17,25},{25,17},{2,10},{10... | collective-permute-start | bytes 98312 | tf_op jit(solution)/shard_map/gather_cadence_factors/ppermute | solution.py:341
  10.4 3.9 %collective-permute-start.3 = (f32[32,256]{1,0:T(8,128)S(1)}, f32[32,256]{1,0:T(8,128)S(1)}, u32[]{:S(2)}, u32[]{:S(2)}) collective-permute-start(f32[32,256]{1,0:T(8,128)S(1)} %bitcast.11), channel_id=1, source_target_pairs={{0,16},{8,24},{16,0},{24,8},{1,17},{9,25},{17,1},{25,9},{2,18},{10... | collective-permute-start | bytes 98312 | tf_op jit(solution)/shard_map/gather_cadence_factors/ppermute | solution.py:341
  11.9 3.3 %collective-permute-start.4 = (f32[32,256]{1,0:T(8,128)S(1)}, f32[32,256]{1,0:T(8,128)S(1)}, u32[]{:S(2)}, u32[]{:S(2)}) collective-permute-start(f32[32,256]{1,0:T(8,128)S(1)} %bitcast.12), channel_id=1, source_target_pairs={{0,24},{8,16},{16,8},{24,0},{1,25},{9,17},{17,9},{25,1},{2,26},{10... | collective-permute-start | bytes 98312 | tf_op jit(solution)/shard_map/gather_cadence_factors/ppermute | solution.py:341
  12.2 6.4 %collective-permute-start.8 = (f32[16,4096]{1,0:T(8,128)S(1)}, f32[16,4096]{1,0:T(8,128)S(1)}, u32[]{:S(2)}, u32[]{:S(2)}) collective-permute-start(f32[16,4096]{1,0:T(8,128)S(1)} %gather_star_factors.5), channel_id=1, source_target_pairs={{0,2},{2,4},{4,6},{6,7},{7,5},{5,3},{3,1},{1,0},{8,9},{10,8},{12,1... | collective-permute-start | bytes 786440 | tf_op jit(solution)/shard_map/gather_star_factors/ppermute | solution.py:337
  15.2 6.4 %collective-permute-start.5 = (f32[16,4096]{1,0:T(8,128)S(1)}, f32[16,4096]{1,0:T(8,128)S(1)}, u32[]{:S(2)}, u32[]{:S(2)}) collective-permute-start(f32[16,4096]{1,0:T(8,128)S(1)} %gather_star_factors.4.refs_3_.refs_8_), channel_id=1, source_target_pairs={{0,2},{2,4},{4,6},{6,7},{7,5},{5,3},{3,1},{1,0},{8,9},{10,8},{12,1... | collective-permute-start | bytes 786440 | tf_op jit(solution)/shard_map/gather_star_factors/ppermute | solution.py:337
  16.8 8.0 %collective-permute-start.10 = (f32[16,4096]{1,0:T(8,128)S(1)}, f32[16,4096]{1,0:T(8,128)S(1)}, u32[]{:S(2)}, u32[]{:S(2)}) collective-permute-start(f32[16,4096]{1,0:T(8,128)S(1)} %gather_star_factors.5), channel_id=1, source_target_pairs={{0,8},{8,0},{16,24},{24,16},{1,9},{9,1},{17,25},{25,17},{2,10},{10... | collective-permute-start | bytes 786440 | tf_op jit(solution)/shard_map/gather_star_factors/ppermute | solution.py:341
  18.6 6.2 %collective-permute-start.9 = (f32[16,4096]{1,0:T(8,128)S(1)}, f32[16,4096]{1,0:T(8,128)S(1)}, u32[]{:S(2)}, u32[]{:S(2)}) collective-permute-start(f32[16,4096]{1,0:T(8,128)S(1)} %collective-permute-done.8), channel_id=1, source_target_pairs={{0,8},{8,0},{16,24},{24,16},{1,9},{9,1},{17,25},{25,17},{2,10},{10... | collective-permute-start | bytes 786440 | tf_op jit(solution)/shard_map/gather_star_factors/ppermute | solution.py:341
  18.6 8.2 %collective-permute-start.12 = (f32[16,4096]{1,0:T(8,128)S(1)}, f32[16,4096]{1,0:T(8,128)S(1)}, u32[]{:S(2)}, u32[]{:S(2)}) collective-permute-start(f32[16,4096]{1,0:T(8,128)S(1)} %collective-permute-done.8), channel_id=1, source_target_pairs={{0,10},{2,12},{4,14},{6,15},{7,13},{5,11},{3,9},{1,8},{8,1},{10,0}... | collective-permute-start | bytes 786440 | tf_op jit(solution)/shard_map/gather_star_factors/ppermute | solution.py:337
  21.6 5.1 %collective-permute-start.11 = (f32[16,2048]{1,0:T(8,128)S(1)}, f32[16,2048]{1,0:T(8,128)S(1)}, u32[]{:S(2)}, u32[]{:S(2)}) collective-permute-start(f32[16,2048]{1,0:T(8,128)S(1)} %get-tuple-element.56), channel_id=1, source_target_pairs={{0,2},{2,4},{4,6},{6,7},{7,5},{5,3},{3,1},{1,0},{8,9},{10,8},{12,1... | collective-permute-start | bytes 393224 | tf_op jit(solution)/shard_map/gather_star_factors/ppermute | solution.py:337
  23.3 3.5 %copy-start.3 = (s32[256]{0:T(256)S(1)}, s32[256]{0:T(256)}, u32[]{:S(2)}) copy-start(s32[256]{0:T(256)} %param.5) | copy-start | bytes 3076
  23.3 5.4 %collective-permute-start.13 = (f32[16,2048]{1,0:T(8,128)S(1)}, f32[16,2048]{1,0:T(8,128)S(1)}, u32[]{:S(2)}, u32[]{:S(2)}) collective-permute-start(f32[16,2048]{1,0:T(8,128)S(1)} %get-tuple-element.55), channel_id=1, source_target_pairs={{0,2},{2,4},{4,6},{6,7},{7,5},{5,3},{3,1},{1,0},{8,9},{10,8},{12,1... | collective-permute-start | bytes 393224 | tf_op jit(solution)/shard_map/gather_star_factors/ppermute | solution.py:337
  30.5 1.6 %collective-permute-start.14 = (f32[16,4224]{1,0:T(8,128)S(1)}, f32[16,4224]{1,0:T(8,128)S(1)}, u32[]{:S(2)}, u32[]{:S(2)}) collective-permute-start(f32[16,4224]{1,0:T(8,128)S(1)} %get-tuple-element.38), channel_id=1, source_target_pairs={{0,8},{8,0},{16,24},{24,16},{1,9},{9,1},{17,25},{25,17},{2,10},{10... | collective-permute-start | bytes 811016 | tf_op jit(solution)/shard_map/ppermute | solution.py:341
  30.6 6.5 %collective-permute-start.15 = (f32[16,4224]{1,0:T(8,128)S(1)}, f32[16,4224]{1,0:T(8,128)S(1)}, u32[]{:S(2)}, u32[]{:S(2)}) collective-permute-start(f32[16,4224]{1,0:T(8,128)S(1)} %get-tuple-element.43), channel_id=1, source_target_pairs={{0,2},{2,4},{4,6},{6,7},{7,5},{5,3},{3,1},{1,0},{8,9},{10,8},{12,1... | collective-permute-start | bytes 811016 | tf_op jit(solution)/shard_map/scatter_star_gradient/ppermute | solution.py:337
  32.2 6.6 %collective-permute-start.17 = (f32[16,4224]{1,0:T(8,128)S(1)}, f32[16,4224]{1,0:T(8,128)S(1)}, u32[]{:S(2)}, u32[]{:S(2)}) collective-permute-start(f32[16,4224]{1,0:T(8,128)S(1)} %get-tuple-element.44), channel_id=1, source_target_pairs={{0,8},{8,0},{16,24},{24,16},{1,9},{9,1},{17,25},{25,17},{2,10},{10... | collective-permute-start | bytes 811016 | tf_op jit(solution)/shard_map/ppermute | solution.py:341
  32.2 7.8 %collective-permute-start.18 = (f32[16,4224]{1,0:T(8,128)S(1)}, f32[16,4224]{1,0:T(8,128)S(1)}, u32[]{:S(2)}, u32[]{:S(2)}) collective-permute-start(f32[16,4224]{1,0:T(8,128)S(1)} %collective-permute-done.14.refs_1_), channel_id=1, source_target_pairs={{0,2},{2,4},{4,6},{6,7},{7,5},{5,3},{3,1},{1,0},{8,9},{10,8},{12,1... | collective-permute-start | bytes 811016 | tf_op jit(solution)/shard_map/scatter_star_gradient/ppermute | solution.py:337
  37.2 6.5 %collective-permute-start.16 = (f32[16,4224]{1,0:T(8,128)S(1)}, f32[16,4224]{1,0:T(8,128)S(1)}, u32[]{:S(2)}, u32[]{:S(2)}) collective-permute-start(f32[16,4224]{1,0:T(8,128)S(1)} %add.12), channel_id=1, source_target_pairs={{0,2},{2,4},{4,6},{6,7},{7,5},{5,3},{3,1},{1,0},{8,9},{10,8},{12,1... | collective-permute-start | bytes 811016 | tf_op jit(solution)/shard_map/scatter_star_gradient/ppermute | solution.py:337
  38.7 7.2 %collective-permute-start.20 = (f32[16,4224]{1,0:T(8,128)S(1)}, f32[16,4224]{1,0:T(8,128)S(1)}, u32[]{:S(2)}, u32[]{:S(2)}) collective-permute-start(f32[16,4224]{1,0:T(8,128)S(1)} %get-tuple-element.45), channel_id=1, source_target_pairs={{0,8},{8,0},{16,24},{24,16},{1,9},{9,1},{17,25},{25,17},{2,10},{10... | collective-permute-start | bytes 811016 | tf_op jit(solution)/shard_map/scatter_star_gradient/ppermute | solution.py:341
  40.1 6.5 %collective-permute-start.21 = (f32[16,4224]{1,0:T(8,128)S(1)}, f32[16,4224]{1,0:T(8,128)S(1)}, u32[]{:S(2)}, u32[]{:S(2)}) collective-permute-start(f32[16,4224]{1,0:T(8,128)S(1)} %add.14.refs_1_), channel_id=1, source_target_pairs={{0,2},{2,4},{4,6},{6,7},{7,5},{5,3},{3,1},{1,0},{8,9},{10,8},{12,1... | collective-permute-start | bytes 811016 | tf_op jit(solution)/shard_map/scatter_star_gradient/ppermute | solution.py:337
  41.6 4.3 %collective-permute-start.22 = (f32[64,256]{1,0:T(8,128)S(1)}, f32[64,256]{1,0:T(8,128)S(1)}, u32[]{:S(2)}, u32[]{:S(2)}) collective-permute-start(f32[64,256]{1,0:T(8,128)S(1)} %scatter_star_gradient.11), channel_id=1, source_target_pairs={{0,16},{8,24},{16,0},{24,8},{1,17},{9,25},{17,1},{25,9},{2,18},{10... | collective-permute-start | bytes 196616 | tf_op jit(solution)/shard_map/scatter_star_gradient/ppermute | solution.py:341
  43.7 6.5 %collective-permute-start.19 = (f32[16,4224]{1,0:T(8,128)S(1)}, f32[16,4224]{1,0:T(8,128)S(1)}, u32[]{:S(2)}, u32[]{:S(2)}) collective-permute-start(f32[16,4224]{1,0:T(8,128)S(1)} %scatter_star_gradient.10), channel_id=1, source_target_pairs={{0,2},{2,4},{4,6},{6,7},{7,5},{5,3},{3,1},{1,0},{8,9},{10,8},{12,1... | collective-permute-start | bytes 811016 | tf_op jit(solution)/shard_map/scatter_star_gradient/ppermute | solution.py:337
  46.6 6.7 %collective-permute-start.24 = (f32[16,4224]{1,0:T(8,128)S(1)}, f32[16,4224]{1,0:T(8,128)S(1)}, u32[]{:S(2)}, u32[]{:S(2)}) collective-permute-start(f32[16,4224]{1,0:T(8,128)S(1)} %scatter_star_gradient.13.refs_1_), channel_id=1, source_target_pairs={{0,10},{2,12},{4,14},{6,15},{7,13},{5,11},{3,9},{1,8},{8,1},{10,0}... | collective-permute-start | bytes 811016 | tf_op jit(solution)/shard_map/scatter_star_gradient/ppermute | solution.py:337
  50.3 3.7 %collective-permute-start.26 = (f32[8,128]{1,0:T(8,128)S(1)}, f32[8,128]{1,0:T(8,128)S(1)}, u32[]{:S(2)}, u32[]{:S(2)}) collective-permute-start(f32[8,128]{1,0:T(8,128)S(1)} %get-tuple-element.51), channel_id=1, source_target_pairs={{0,2},{2,4},{4,6},{6,7},{7,5},{5,3},{3,1},{1,0},{8,9},{10,8},{12,1... | collective-permute-start | bytes 12296 | tf_op jit(solution)/shard_map/scatter_star_gradient/ppermute | solution.py:337
  51.8 6.5 %collective-permute-start.23 = (f32[16,4224]{1,0:T(8,128)S(1)}, f32[16,4224]{1,0:T(8,128)S(1)}, u32[]{:S(2)}, u32[]{:S(2)}) collective-permute-start(f32[16,4224]{1,0:T(8,128)S(1)} %get-tuple-element.49), channel_id=1, source_target_pairs={{0,2},{2,4},{4,6},{6,7},{7,5},{5,3},{3,1},{1,0},{8,9},{10,8},{12,1... | collective-permute-start | bytes 811016 | tf_op jit(solution)/shard_map/scatter_star_gradient/ppermute | solution.py:337
  53.4 5.4 %collective-permute-start.25 = (f32[32,256]{1,0:T(8,128)S(1)}, f32[32,256]{1,0:T(8,128)S(1)}, u32[]{:S(2)}, u32[]{:S(2)}) collective-permute-start(f32[32,256]{1,0:T(8,128)S(1)} %scatter_star_gradient.16), channel_id=1, source_target_pairs={{0,8},{8,0},{16,24},{24,16},{1,9},{9,1},{17,25},{25,17},{2,10},{10... | collective-permute-start | bytes 98312 | tf_op jit(solution)/shard_map/scatter_star_gradient/ppermute | solution.py:341
  53.9 1.2 %collective-permute-start.27 = (f32[8,128]{1,0:T(8,128)S(1)}, f32[8,128]{1,0:T(8,128)S(1)}, u32[]{:S(2)}, u32[]{:S(2)}) collective-permute-start(f32[8,128]{1,0:T(8,128)S(1)} %scatter_star_gradient.17.refs_0_), channel_id=1, source_target_pairs={{0,8},{8,0},{16,24},{24,16},{1,9},{9,1},{17,25},{25,17},{2,10},{10... | collective-permute-start | bytes 12296 | tf_op jit(solution)/shard_map/scatter_star_gradient/ppermute | solution.py:341
  55.1 3.6 %collective-permute-start.28 = (f32[8,128]{1,0:T(8,128)S(1)}, f32[8,128]{1,0:T(8,128)S(1)}, u32[]{:S(2)}, u32[]{:S(2)}) collective-permute-start(f32[8,128]{1,0:T(8,128)S(1)} %scatter_star_gradient.18.refs_0_), channel_id=1, source_target_pairs={{0,16},{8,24},{16,0},{24,8},{1,17},{9,25},{17,1},{25,9},{2,18},{10... | collective-permute-start | bytes 12296 | tf_op jit(solution)/shard_map/scatter_star_gradient/ppermute | solution.py:341

commit v6 on v5

--- a/solution.py
+++ b/solution.py
@@ -284,12 +284,13 @@
 
 
 def add_part_body(mine, got, out, part):
-    out[...] = mine[...] + got[...]
-    part[...] = out[:8, out.shape[1] - 128 :]
+    width = out.shape[1]
+    out[...] = mine[:, :width] + got[:, :width]
+    part[...] = mine[:8, width:] + got[:8, width:]
 
 
 def add_part(mine, got):
-    return small_call(add_part_body, [mine, got], [mine.shape, (8, 128)])
+    return small_call(add_part_body, [mine, got], [(mine.shape[0], mine.shape[1] - 128), (8, 128)])
 
 
 def loss_part_body(loss, near, beside, out):

time: 59.6 us -> 59.6 us (level)
  no operation moved by 1% of the time
where the time goes in v6:
time: 59.6 us; the launch traced here: 59.5 us
  starting transfers between devices  30.8 us (52%)
  waiting for transfers between devices  16 us (27%)
  Pallas kernels  9.52 us (16%)
  local copies, waits for them, and re-layouts  2.22 us (4%)
  between operations  0.79 us (1%)
    ppermute x16, starting transfers between devices, shift(): return lax.ppermute(x, ('star', 'cad'), pairs)  25.4 us
    ppermute x16, waiting for transfers between devices, shift(): return lax.ppermute(x, ('star', 'cad'), pairs)  12.3 us
    pallas_call x4, Pallas kernels, big_call(): pl.pallas_call(body_of, in_specs=[vmem] * len(given), out_specs=[vmem] *...  8.43 us
    ppermute x13, starting transfers between devices, swap(): lax.ppermute(x, axis, [(i, i ^ bit) for i in range(lax.axis_size(axis))])  5.43 us
    ppermute x13, waiting for transfers between devices, swap(): lax.ppermute(x, axis, [(i, i ^ bit) for i in range(lax.axis_size(axis))])  3.72 us
    unnamed x8, local copies, waits for them, and re-layouts  2.2 us
  transfers between devices with their start and end apart: 29, of which 15 were waited for; matrix products, arithmetic and copies ran while one was open for 0% of the time, Pallas kernels for 12%

profile of v6, /device:TPU:0, one launch (start us, length us, event | category | flops | bytes accessed | tf_op | source)
XLA Modules:
  0.0 59.5 jit_solution(10062130910578083520)
XLA Ops:
  0.6 0.5 collective-permute-start.6
  1.1 2.6 %collective-permute-start = (f32[16,4096]{1,0:T(8,128)}, f32[16,4096]{1,0:T(8,128)S(1)}, u32[]{:S(2)}, u32[]{:S(2)}) collective-permute-start(f32[16,4096]{1,0:T(8,128)} %bitcast.7), channel_id=1, source_target_pairs={{0,2},{2,4},{4,6},{6,7},{7,5},{5,3},{3,1},{1,0},{8,9},{10,8},{12,1... | collective-permute-start | bytes 786440 | tf_op jit(solution)/shard_map/gather_star_factors/ppermute | solution.py:338
  3.8 0.0 collective-permute-done.6
  3.8 1.7 %collective-permute-start.7 = (f32[16,4096]{1,0:T(8,128)S(1)}, f32[16,4096]{1,0:T(8,128)S(1)}, u32[]{:S(2)}, u32[]{:S(2)}) collective-permute-start(f32[16,4096]{1,0:T(8,128)S(1)} %collective-permute-done.6), channel_id=1, source_target_pairs={{0,2},{2,4},{4,6},{6,7},{7,5},{5,3},{3,1},{1,0},{8,9},{10,8},{12,1... | collective-permute-start | bytes 786440 | tf_op jit(solution)/shard_map/gather_star_factors/ppermute | solution.py:338
  5.5 2.2 %copy-done = f32[4096,256]{1,0:T(8,128)S(1)} copy-done((f32[4096,256]{1,0:T(8,128)S(1)}, f32[4096,256]{1,0:T(8,128)}, u32[]{:S(2)}) %copy-start) | copy-done | bytes 4194328
  7.7 0.3 shard_map.67.refs_1_.refs_0_
  8.0 0.0 copy-start.2
  8.0 0.0 copy-start.1
  8.0 0.3 collective-permute-done.refs_0_
  8.3 2.1 %collective-permute-start.1 = (f32[16,4096]{1,0:T(8,128)S(1)}, f32[16,4096]{1,0:T(8,128)S(1)}, u32[]{:S(2)}, u32[]{:S(2)}) collective-permute-start(f32[16,4096]{1,0:T(8,128)S(1)} %gather_star_factors.3.refs_2_.refs_7_), channel_id=1, source_target_pairs={{0,2},{2,4},{4,6},{6,7},{7,5},{5,3},{3,1},{1,0},{8,9},{10,8},{12,1... | collective-permute-start | bytes 786440 | tf_op jit(solution)/shard_map/gather_star_factors/ppermute | solution.py:338
  10.4 0.0 collective-permute-start.2
  10.4 1.5 %collective-permute-start.3 = (f32[32,256]{1,0:T(8,128)S(1)}, f32[32,256]{1,0:T(8,128)S(1)}, u32[]{:S(2)}, u32[]{:S(2)}) collective-permute-start(f32[32,256]{1,0:T(8,128)S(1)} %bitcast.11), channel_id=1, source_target_pairs={{0,16},{8,24},{16,0},{24,8},{1,17},{9,25},{17,1},{25,9},{2,18},{10... | collective-permute-start | bytes 98312 | tf_op jit(solution)/shard_map/gather_cadence_factors/ppermute | solution.py:342
  11.9 0.3 collective-permute-start.4
  12.2 1.6 %collective-permute-start.8 = (f32[16,4096]{1,0:T(8,128)S(1)}, f32[16,4096]{1,0:T(8,128)S(1)}, u32[]{:S(2)}, u32[]{:S(2)}) collective-permute-start(f32[16,4096]{1,0:T(8,128)S(1)} %gather_star_factors.5), channel_id=1, source_target_pairs={{0,2},{2,4},{4,6},{6,7},{7,5},{5,3},{3,1},{1,0},{8,9},{10,8},{12,1... | collective-permute-start | bytes 786440 | tf_op jit(solution)/shard_map/gather_star_factors/ppermute | solution.py:338
  13.8 0.5 collective-permute-done.3.refs_2_.refs_9_.refs_6_.refs_17_
  14.3 0.9 %collective-permute-done.4.refs_3_.refs_10_.refs_7_.refs_18_ = f32[32,256]{1,0:T(8,128)S(1)} collective-permute-done((f32[32,256]{1,0:T(8,128)S(1)}, f32[32,256]{1,0:T(8,128)S(1)}, u32[]{:S(2)}, u32[]{:S(2)}) %collective-permute-start.4) | collective-permute-done | bytes 32800 | tf_op jit(solution)/shard_map/gather_cadence_factors/ppermute | solution.py:342
  15.2 1.6 %collective-permute-start.5 = (f32[16,4096]{1,0:T(8,128)S(1)}, f32[16,4096]{1,0:T(8,128)S(1)}, u32[]{:S(2)}, u32[]{:S(2)}) collective-permute-start(f32[16,4096]{1,0:T(8,128)S(1)} %gather_star_factors.4.refs_3_.refs_8_), channel_id=1, source_target_pairs={{0,2},{2,4},{4,6},{6,7},{7,5},{5,3},{3,1},{1,0},{8,9},{10,8},{12,1... | collective-permute-start | bytes 786440 | tf_op jit(solution)/shard_map/gather_star_factors/ppermute | solution.py:338
  16.8 1.8 %collective-permute-done.8 = f32[16,4096]{1,0:T(8,128)S(1)} collective-permute-done((f32[16,4096]{1,0:T(8,128)S(1)}, f32[16,4096]{1,0:T(8,128)S(1)}, u32[]{:S(2)}, u32[]{:S(2)}) %collective-permute-start.8) | collective-permute-done | bytes 262176 | tf_op jit(solution)/shard_map/gather_star_factors/ppermute | solution.py:338
  18.6 1.7 %collective-permute-start.12 = (f32[16,4096]{1,0:T(8,128)S(1)}, f32[16,4096]{1,0:T(8,128)S(1)}, u32[]{:S(2)}, u32[]{:S(2)}) collective-permute-start(f32[16,4096]{1,0:T(8,128)S(1)} %collective-permute-done.8), channel_id=1, source_target_pairs={{0,10},{2,12},{4,14},{6,15},{7,13},{5,11},{3,9},{1,8},{8,1},{10,0}... | collective-permute-start | bytes 786440 | tf_op jit(solution)/shard_map/gather_star_factors/ppermute | solution.py:338
  20.3 1.3 %collective-permute-done.5.refs_4_.refs_9_ = f32[16,4096]{1,0:T(8,128)S(1)} collective-permute-done((f32[16,4096]{1,0:T(8,128)S(1)}, f32[16,4096]{1,0:T(8,128)S(1)}, u32[]{:S(2)}, u32[]{:S(2)}) %collective-permute-start.5) | collective-permute-done | bytes 262176 | tf_op jit(solution)/shard_map/gather_star_factors/ppermute | solution.py:338
  21.6 1.6 %collective-permute-start.11 = (f32[16,2048]{1,0:T(8,128)S(1)}, f32[16,2048]{1,0:T(8,128)S(1)}, u32[]{:S(2)}, u32[]{:S(2)}) collective-permute-start(f32[16,2048]{1,0:T(8,128)S(1)} %get-tuple-element.56), channel_id=1, source_target_pairs={{0,2},{2,4},{4,6},{6,7},{7,5},{5,3},{3,1},{1,0},{8,9},{10,8},{12,1... | collective-permute-start | bytes 393224 | tf_op jit(solution)/shard_map/gather_star_factors/ppermute | solution.py:338
  23.3 1.6 %collective-permute-start.13 = (f32[16,2048]{1,0:T(8,128)S(1)}, f32[16,2048]{1,0:T(8,128)S(1)}, u32[]{:S(2)}, u32[]{:S(2)}) collective-permute-start(f32[16,2048]{1,0:T(8,128)S(1)} %get-tuple-element.55), channel_id=1, source_target_pairs={{0,2},{2,4},{4,6},{6,7},{7,5},{5,3},{3,1},{1,0},{8,9},{10,8},{12,1... | collective-permute-start | bytes 393224 | tf_op jit(solution)/shard_map/gather_star_factors/ppermute | solution.py:338
  24.9 1.9 %shard_map.68.refs_0_ = f32[4096,256]{1,0:T(8,128)S(1)} custom-call(f32[4096,256]{1,0:T(8,128)S(1)} %shard_map.67.refs_1_.refs_0_, f32[16,4096]{1,0:T(8,128)S(1)} %bitcast.8, f32[16,4096]{1,0:T(8,128)S(1)} %gather_star_factors.3.refs_2_.refs_7_, f32[16,4096]{1,0:T(8,128)S(1)} %gather_star_factors.4.refs_3_.refs_8_, ...), custom_call_target="tpu_custom_call" | custom-call | flops 1610612736 | bytes 1048576 | tf_op jit(solution)/shard_map/pallas_call | solution.py:195
  26.8 1.9 %shard_map.69 = (bf16[2048,256]{1,0:T(8,128)(2,1)S(1)}, bf16[2048,256]{1,0:T(8,128)(2,1)S(1)}, f32[8,256]{1,0:T(8,128)S(1)}, f32[16,2048]{1,0:T(8,128)S(1)}, f32...) custom-call(f32[4096,256]{1,0:T(8,128)S(1)} %shard_map.68.refs_0_, s32[1,256]{1,0:T(1,128)S(1)} %bitcast.17, ...), custom_call_target="tpu_custom_call" | custom-call | flops 536870912 | bytes 1048576 | tf_op jit(solution)/shard_map/pallas_call | solution.py:195
  28.7 1.9 %shard_map.70 = (bf16[2048,256]{1,0:T(8,128)(2,1)S(1)}, bf16[2048,256]{1,0:T(8,128)(2,1)S(1)}, f32[8,128]{1,0:T(8,128)S(1)}, f32[16,4224]{1,0:T(8,128)S(1)}, f32...) custom-call(f32[4096,256]{1,0:T(8,128)S(1)} %shard_map.68.refs_0_, s32[1,256]{1,0:T(1,128)S(1)} %bitcast.18, ...), custom_call_target="tpu_custom_call" | custom-call | flops 536870912 | bytes 1048576 | tf_op jit(solution)/shard_map/pallas_call | solution.py:195
  30.5 0.1 collective-permute-start.14
  30.6 1.6 %collective-permute-start.15 = (f32[16,4224]{1,0:T(8,128)S(1)}, f32[16,4224]{1,0:T(8,128)S(1)}, u32[]{:S(2)}, u32[]{:S(2)}) collective-permute-start(f32[16,4224]{1,0:T(8,128)S(1)} %get-tuple-element.43), channel_id=1, source_target_pairs={{0,2},{2,4},{4,6},{6,7},{7,5},{5,3},{3,1},{1,0},{8,9},{10,8},{12,1... | collective-permute-start | bytes 811016 | tf_op jit(solution)/shard_map/scatter_star_gradient/ppermute | solution.py:338
  32.2 1.5 %collective-permute-start.18 = (f32[16,4224]{1,0:T(8,128)S(1)}, f32[16,4224]{1,0:T(8,128)S(1)}, u32[]{:S(2)}, u32[]{:S(2)}) collective-permute-start(f32[16,4224]{1,0:T(8,128)S(1)} %collective-permute-done.14.refs_1_), channel_id=1, source_target_pairs={{0,2},{2,4},{4,6},{6,7},{7,5},{5,3},{3,1},{1,0},{8,9},{10,8},{12,1... | collective-permute-start | bytes 811016 | tf_op jit(solution)/shard_map/scatter_star_gradient/ppermute | solution.py:338
  33.7 2.8 %shard_map.72 = (f32[16,4224]{1,0:T(8,128)S(1)}, f32[16,4224]{1,0:T(8,128)S(1)}, f32[16,4224]{1,0:T(8,128)S(1)}, f32[16,4224]{1,0:T(8,128)S(1)}, f32[16,4224]{1,...) custom-call(bf16[2048,256]{1,0:T(8,128)(2,1)S(1)} %get-tuple-element.29.refs_0_, ...), custom_call_target="tpu_custom_call" | custom-call | flops 1610612736 | bytes 1048576 | tf_op jit(solution)/shard_map/pallas_call | solution.py:195
  36.5 0.6 %collective-permute-done.15 = f32[16,4224]{1,0:T(8,128)S(1)} collective-permute-done((f32[16,4224]{1,0:T(8,128)S(1)}, f32[16,4224]{1,0:T(8,128)S(1)}, u32[]{:S(2)}, u32[]{:S(2)}) %collective-permute-start.15) | collective-permute-done | bytes 270368 | tf_op jit(solution)/shard_map/scatter_star_gradient/ppermute | solution.py:338
  37.2 1.6 %collective-permute-start.16 = (f32[16,4224]{1,0:T(8,128)S(1)}, f32[16,4224]{1,0:T(8,128)S(1)}, u32[]{:S(2)}, u32[]{:S(2)}) collective-permute-start(f32[16,4224]{1,0:T(8,128)S(1)} %add.12), channel_id=1, source_target_pairs={{0,2},{2,4},{4,6},{6,7},{7,5},{5,3},{3,1},{1,0},{8,9},{10,8},{12,1... | collective-permute-start | bytes 811016 | tf_op jit(solution)/shard_map/scatter_star_gradient/ppermute | solution.py:338
  38.7 1.3 %collective-permute-done.18 = f32[16,4224]{1,0:T(8,128)S(1)} collective-permute-done((f32[16,4224]{1,0:T(8,128)S(1)}, f32[16,4224]{1,0:T(8,128)S(1)}, u32[]{:S(2)}, u32[]{:S(2)}) %collective-permute-start.18) | collective-permute-done | bytes 270368 | tf_op jit(solution)/shard_map/scatter_star_gradient/ppermute | solution.py:338
  40.1 1.6 %collective-permute-start.21 = (f32[16,4224]{1,0:T(8,128)S(1)}, f32[16,4224]{1,0:T(8,128)S(1)}, u32[]{:S(2)}, u32[]{:S(2)}) collective-permute-start(f32[16,4224]{1,0:T(8,128)S(1)} %add.14.refs_1_), channel_id=1, source_target_pairs={{0,2},{2,4},{4,6},{6,7},{7,5},{5,3},{3,1},{1,0},{8,9},{10,8},{12,1... | collective-permute-start | bytes 811016 | tf_op jit(solution)/shard_map/scatter_star_gradient/ppermute | solution.py:338
  41.6 1.5 %collective-permute-start.22 = (f32[64,256]{1,0:T(8,128)S(1)}, f32[64,256]{1,0:T(8,128)S(1)}, u32[]{:S(2)}, u32[]{:S(2)}) collective-permute-start(f32[64,256]{1,0:T(8,128)S(1)} %scatter_star_gradient.11), channel_id=1, source_target_pairs={{0,16},{8,24},{16,0},{24,8},{1,17},{9,25},{17,1},{25,9},{2,18},{10... | collective-permute-start | bytes 196616 | tf_op jit(solution)/shard_map/scatter_star_gradient/ppermute | solution.py:342
  43.1 0.5 collective-permute-done.16
  43.7 1.6 %collective-permute-start.19 = (f32[16,4224]{1,0:T(8,128)S(1)}, f32[16,4224]{1,0:T(8,128)S(1)}, u32[]{:S(2)}, u32[]{:S(2)}) collective-permute-start(f32[16,4224]{1,0:T(8,128)S(1)} %scatter_star_gradient.10), channel_id=1, source_target_pairs={{0,2},{2,4},{4,6},{6,7},{7,5},{5,3},{3,1},{1,0},{8,9},{10,8},{12,1... | collective-permute-start | bytes 811016 | tf_op jit(solution)/shard_map/scatter_star_gradient/ppermute | solution.py:338
  45.3 0.6 %collective-permute-done.22.got = f32[64,256]{1,0:T(8,128)S(1)} collective-permute-done((f32[64,256]{1,0:T(8,128)S(1)}, f32[64,256]{1,0:T(8,128)S(1)}, u32[]{:S(2)}, u32[]{:S(2)}) %collective-permute-start.22) | collective-permute-done | bytes 65568 | tf_op jit(solution)/shard_map/scatter_star_gradient/ppermute | solution.py:342
  45.9 0.7 %collective-permute-done.21 = f32[16,4224]{1,0:T(8,128)S(1)} collective-permute-done((f32[16,4224]{1,0:T(8,128)S(1)}, f32[16,4224]{1,0:T(8,128)S(1)}, u32[]{:S(2)}, u32[]{:S(2)}) %collective-permute-start.21) | collective-permute-done | bytes 270368 | tf_op jit(solution)/shard_map/scatter_star_gradient/ppermute | solution.py:338
  46.6 0.1 collective-permute-start.24
  46.7 3.5 %collective-permute-done.19.refs_0_ = f32[16,4224]{1,0:T(8,128)S(1)} collective-permute-done((f32[16,4224]{1,0:T(8,128)S(1)}, f32[16,4224]{1,0:T(8,128)S(1)}, u32[]{:S(2)}, u32[]{:S(2)}) %collective-permute-start.19) | collective-permute-done | bytes 270368 | tf_op jit(solution)/shard_map/scatter_star_gradient/ppermute | solution.py:338
  50.3 1.6 %collective-permute-start.26 = (f32[8,128]{1,0:T(8,128)S(1)}, f32[8,128]{1,0:T(8,128)S(1)}, u32[]{:S(2)}, u32[]{:S(2)}) collective-permute-start(f32[8,128]{1,0:T(8,128)S(1)} %get-tuple-element.51), channel_id=1, source_target_pairs={{0,2},{2,4},{4,6},{6,7},{7,5},{5,3},{3,1},{1,0},{8,9},{10,8},{12,1... | collective-permute-start | bytes 12296 | tf_op jit(solution)/shard_map/scatter_star_gradient/ppermute | solution.py:338
  51.8 1.5 %collective-permute-start.23 = (f32[16,4096]{1,0:T(8,128)S(1)}, f32[16,4096]{1,0:T(8,128)S(1)}, u32[]{:S(2)}, u32[]{:S(2)}) collective-permute-start(f32[16,4096]{1,0:T(8,128)S(1)} %get-tuple-element.49), channel_id=1, source_target_pairs={{0,2},{2,4},{4,6},{6,7},{7,5},{5,3},{3,1},{1,0},{8,9},{10,8},{12,1... | collective-permute-start | bytes 786440 | tf_op jit(solution)/shard_map/scatter_star_gradient/ppermute | solution.py:338
  53.4 0.6 collective-permute-done.26.near
  53.9 1.2 %collective-permute-done.27.refs_1_ = f32[8,128]{1,0:T(8,128)S(1)} collective-permute-done((f32[8,128]{1,0:T(8,128)S(1)}, f32[8,128]{1,0:T(8,128)S(1)}, u32[]{:S(2)}, u32[]{:S(2)}) %collective-permute-start.27) | collective-permute-done | bytes 4128 | tf_op jit(solution)/shard_map/scatter_star_gradient/ppermute | solution.py:342
  55.1 1.4 %collective-permute-start.28 = (f32[8,128]{1,0:T(8,128)S(1)}, f32[8,128]{1,0:T(8,128)S(1)}, u32[]{:S(2)}, u32[]{:S(2)}) collective-permute-start(f32[8,128]{1,0:T(8,128)S(1)} %scatter_star_gradient.18.refs_0_), channel_id=1, source_target_pairs={{0,16},{8,24},{16,0},{24,8},{1,17},{9,25},{17,1},{25,9},{2,18},{10... | collective-permute-start | bytes 12296 | tf_op jit(solution)/shard_map/scatter_star_gradient/ppermute | solution.py:342
  56.5 1.7 %collective-permute-done.23.up = f32[16,4096]{1,0:T(8,128)S(1)} collective-permute-done((f32[16,4096]{1,0:T(8,128)S(1)}, f32[16,4096]{1,0:T(8,128)S(1)}, u32[]{:S(2)}, u32[]{:S(2)}) %collective-permute-start.23) | collective-permute-done | bytes 262176 | tf_op jit(solution)/shard_map/scatter_star_gradient/ppermute | solution.py:338
  58.2 0.5 collective-permute-done.28.refs_1_
  58.7 0.8 %scatter_star_gradient.19 = (f32[16,4096]{1,0:T(8,128)}, f32[32,256]{1,0:T(8,128)}, f32[1,1]{1,0:T(1,128)}) custom-call(f32[16,4224]{1,0:T(8,128)S(1)} %get-tuple-element.39.mine, f32[16,4096]{1,0:T(8,128)S(1)} %collective-permute-done.23.up, f32[16,4224]{1,0:T(8,128)S(1)} %collective-permute-done.24.refs_1_.beside.back, ...), custom_call_target="tpu_custom_call" | custom-call | bytes 1024 | tf_op jit(solution)/shard_map/scatter_star_gradient/pallas_call | solution.py:248
  (42 shorter events, 0.3 us)
Async XLA Ops:
  0.6 3.2 %collective-permute-start.6 = (f32[16,4096]{1,0:T(8,128)}, f32[16,4096]{1,0:T(8,128)S(1)}, u32[]{:S(2)}, u32[]{:S(2)}) collective-permute-start(f32[16,4096]{1,0:T(8,128)} %bitcast.6), channel_id=1, source_target_pairs={{0,8},{8,0},{16,24},{24,16},{1,9},{9,1},{17,25},{25,17},{2,10},{10... | collective-permute-start | bytes 786440 | tf_op jit(solution)/shard_map/gather_star_factors/ppermute | solution.py:342
  1.1 7.1 %collective-permute-start = (f32[16,4096]{1,0:T(8,128)}, f32[16,4096]{1,0:T(8,128)S(1)}, u32[]{:S(2)}, u32[]{:S(2)}) collective-permute-start(f32[16,4096]{1,0:T(8,128)} %bitcast.7), channel_id=1, source_target_pairs={{0,2},{2,4},{4,6},{6,7},{7,5},{5,3},{3,1},{1,0},{8,9},{10,8},{12,1... | collective-permute-start | bytes 786440 | tf_op jit(solution)/shard_map/gather_star_factors/ppermute | solution.py:338
  3.8 8.4 %collective-permute-start.7 = (f32[16,4096]{1,0:T(8,128)S(1)}, f32[16,4096]{1,0:T(8,128)S(1)}, u32[]{:S(2)}, u32[]{:S(2)}) collective-permute-start(f32[16,4096]{1,0:T(8,128)S(1)} %collective-permute-done.6), channel_id=1, source_target_pairs={{0,2},{2,4},{4,6},{6,7},{7,5},{5,3},{3,1},{1,0},{8,9},{10,8},{12,1... | collective-permute-start | bytes 786440 | tf_op jit(solution)/shard_map/gather_star_factors/ppermute | solution.py:338
  5.5 2.2 %copy-start = (f32[4096,256]{1,0:T(8,128)S(1)}, f32[4096,256]{1,0:T(8,128)}, u32[]{:S(2)}) copy-start(f32[4096,256]{1,0:T(8,128)} %refs_0_.1) | copy-start | bytes 12582916
  8.0 2.4 %copy-start.2 = (f32[256,32]{0,1:T(8,128)S(1)}, f32[256,32]{0,1:T(8,128)}, u32[]{:S(2)}) copy-start(f32[256,32]{0,1:T(8,128)} %param.7) | copy-start | bytes 98308
  8.0 16.9 %copy-start.1 = (f32[4096,16]{0,1:T(8,128)S(1)}, f32[4096,16]{0,1:T(8,128)}, u32[]{:S(2)}) copy-start(f32[4096,16]{0,1:T(8,128)} %param.6) | copy-start | bytes 786436
  8.3 7.0 %collective-permute-start.1 = (f32[16,4096]{1,0:T(8,128)S(1)}, f32[16,4096]{1,0:T(8,128)S(1)}, u32[]{:S(2)}, u32[]{:S(2)}) collective-permute-start(f32[16,4096]{1,0:T(8,128)S(1)} %gather_star_factors.3.refs_2_.refs_7_), channel_id=1, source_target_pairs={{0,2},{2,4},{4,6},{6,7},{7,5},{5,3},{3,1},{1,0},{8,9},{10,8},{12,1... | collective-permute-start | bytes 786440 | tf_op jit(solution)/shard_map/gather_star_factors/ppermute | solution.py:338
  10.4 3.4 %collective-permute-start.2 = (f32[32,256]{1,0:T(8,128)S(1)}, f32[32,256]{1,0:T(8,128)S(1)}, u32[]{:S(2)}, u32[]{:S(2)}) collective-permute-start(f32[32,256]{1,0:T(8,128)S(1)} %bitcast.10), channel_id=1, source_target_pairs={{0,8},{8,0},{16,24},{24,16},{1,9},{9,1},{17,25},{25,17},{2,10},{10... | collective-permute-start | bytes 98312 | tf_op jit(solution)/shard_map/gather_cadence_factors/ppermute | solution.py:342
  10.4 3.9 %collective-permute-start.3 = (f32[32,256]{1,0:T(8,128)S(1)}, f32[32,256]{1,0:T(8,128)S(1)}, u32[]{:S(2)}, u32[]{:S(2)}) collective-permute-start(f32[32,256]{1,0:T(8,128)S(1)} %bitcast.11), channel_id=1, source_target_pairs={{0,16},{8,24},{16,0},{24,8},{1,17},{9,25},{17,1},{25,9},{2,18},{10... | collective-permute-start | bytes 98312 | tf_op jit(solution)/shard_map/gather_cadence_factors/ppermute | solution.py:342
  11.9 3.3 %collective-permute-start.4 = (f32[32,256]{1,0:T(8,128)S(1)}, f32[32,256]{1,0:T(8,128)S(1)}, u32[]{:S(2)}, u32[]{:S(2)}) collective-permute-start(f32[32,256]{1,0:T(8,128)S(1)} %bitcast.12), channel_id=1, source_target_pairs={{0,24},{8,16},{16,8},{24,0},{1,25},{9,17},{17,9},{25,1},{2,26},{10... | collective-permute-start | bytes 98312 | tf_op jit(solution)/shard_map/gather_cadence_factors/ppermute | solution.py:342
  12.2 6.4 %collective-permute-start.8 = (f32[16,4096]{1,0:T(8,128)S(1)}, f32[16,4096]{1,0:T(8,128)S(1)}, u32[]{:S(2)}, u32[]{:S(2)}) collective-permute-start(f32[16,4096]{1,0:T(8,128)S(1)} %gather_star_factors.5), channel_id=1, source_target_pairs={{0,2},{2,4},{4,6},{6,7},{7,5},{5,3},{3,1},{1,0},{8,9},{10,8},{12,1... | collective-permute-start | bytes 786440 | tf_op jit(solution)/shard_map/gather_star_factors/ppermute | solution.py:338
  15.2 6.4 %collective-permute-start.5 = (f32[16,4096]{1,0:T(8,128)S(1)}, f32[16,4096]{1,0:T(8,128)S(1)}, u32[]{:S(2)}, u32[]{:S(2)}) collective-permute-start(f32[16,4096]{1,0:T(8,128)S(1)} %gather_star_factors.4.refs_3_.refs_8_), channel_id=1, source_target_pairs={{0,2},{2,4},{4,6},{6,7},{7,5},{5,3},{3,1},{1,0},{8,9},{10,8},{12,1... | collective-permute-start | bytes 786440 | tf_op jit(solution)/shard_map/gather_star_factors/ppermute | solution.py:338
  16.8 8.0 %collective-permute-start.10 = (f32[16,4096]{1,0:T(8,128)S(1)}, f32[16,4096]{1,0:T(8,128)S(1)}, u32[]{:S(2)}, u32[]{:S(2)}) collective-permute-start(f32[16,4096]{1,0:T(8,128)S(1)} %gather_star_factors.5), channel_id=1, source_target_pairs={{0,8},{8,0},{16,24},{24,16},{1,9},{9,1},{17,25},{25,17},{2,10},{10... | collective-permute-start | bytes 786440 | tf_op jit(solution)/shard_map/gather_star_factors/ppermute | solution.py:342
  18.6 6.2 %collective-permute-start.9 = (f32[16,4096]{1,0:T(8,128)S(1)}, f32[16,4096]{1,0:T(8,128)S(1)}, u32[]{:S(2)}, u32[]{:S(2)}) collective-permute-start(f32[16,4096]{1,0:T(8,128)S(1)} %collective-permute-done.8), channel_id=1, source_target_pairs={{0,8},{8,0},{16,24},{24,16},{1,9},{9,1},{17,25},{25,17},{2,10},{10... | collective-permute-start | bytes 786440 | tf_op jit(solution)/shard_map/gather_star_factors/ppermute | solution.py:342
  18.6 8.2 %collective-permute-start.12 = (f32[16,4096]{1,0:T(8,128)S(1)}, f32[16,4096]{1,0:T(8,128)S(1)}, u32[]{:S(2)}, u32[]{:S(2)}) collective-permute-start(f32[16,4096]{1,0:T(8,128)S(1)} %collective-permute-done.8), channel_id=1, source_target_pairs={{0,10},{2,12},{4,14},{6,15},{7,13},{5,11},{3,9},{1,8},{8,1},{10,0}... | collective-permute-start | bytes 786440 | tf_op jit(solution)/shard_map/gather_star_factors/ppermute | solution.py:338
  21.6 5.1 %collective-permute-start.11 = (f32[16,2048]{1,0:T(8,128)S(1)}, f32[16,2048]{1,0:T(8,128)S(1)}, u32[]{:S(2)}, u32[]{:S(2)}) collective-permute-start(f32[16,2048]{1,0:T(8,128)S(1)} %get-tuple-element.56), channel_id=1, source_target_pairs={{0,2},{2,4},{4,6},{6,7},{7,5},{5,3},{3,1},{1,0},{8,9},{10,8},{12,1... | collective-permute-start | bytes 393224 | tf_op jit(solution)/shard_map/gather_star_factors/ppermute | solution.py:338
  23.3 3.5 %copy-start.3 = (s32[256]{0:T(256)S(1)}, s32[256]{0:T(256)}, u32[]{:S(2)}) copy-start(s32[256]{0:T(256)} %param.5) | copy-start | bytes 3076
  23.3 5.4 %collective-permute-start.13 = (f32[16,2048]{1,0:T(8,128)S(1)}, f32[16,2048]{1,0:T(8,128)S(1)}, u32[]{:S(2)}, u32[]{:S(2)}) collective-permute-start(f32[16,2048]{1,0:T(8,128)S(1)} %get-tuple-element.55), channel_id=1, source_target_pairs={{0,2},{2,4},{4,6},{6,7},{7,5},{5,3},{3,1},{1,0},{8,9},{10,8},{12,1... | collective-permute-start | bytes 393224 | tf_op jit(solution)/shard_map/gather_star_factors/ppermute | solution.py:338
  30.5 1.6 %collective-permute-start.14 = (f32[16,4224]{1,0:T(8,128)S(1)}, f32[16,4224]{1,0:T(8,128)S(1)}, u32[]{:S(2)}, u32[]{:S(2)}) collective-permute-start(f32[16,4224]{1,0:T(8,128)S(1)} %get-tuple-element.38), channel_id=1, source_target_pairs={{0,8},{8,0},{16,24},{24,16},{1,9},{9,1},{17,25},{25,17},{2,10},{10... | collective-permute-start | bytes 811016 | tf_op jit(solution)/shard_map/ppermute | solution.py:342
  30.6 6.5 %collective-permute-start.15 = (f32[16,4224]{1,0:T(8,128)S(1)}, f32[16,4224]{1,0:T(8,128)S(1)}, u32[]{:S(2)}, u32[]{:S(2)}) collective-permute-start(f32[16,4224]{1,0:T(8,128)S(1)} %get-tuple-element.43), channel_id=1, source_target_pairs={{0,2},{2,4},{4,6},{6,7},{7,5},{5,3},{3,1},{1,0},{8,9},{10,8},{12,1... | collective-permute-start | bytes 811016 | tf_op jit(solution)/shard_map/scatter_star_gradient/ppermute | solution.py:338
  32.2 6.6 %collective-permute-start.17 = (f32[16,4224]{1,0:T(8,128)S(1)}, f32[16,4224]{1,0:T(8,128)S(1)}, u32[]{:S(2)}, u32[]{:S(2)}) collective-permute-start(f32[16,4224]{1,0:T(8,128)S(1)} %get-tuple-element.44), channel_id=1, source_target_pairs={{0,8},{8,0},{16,24},{24,16},{1,9},{9,1},{17,25},{25,17},{2,10},{10... | collective-permute-start | bytes 811016 | tf_op jit(solution)/shard_map/ppermute | solution.py:342
  32.2 7.8 %collective-permute-start.18 = (f32[16,4224]{1,0:T(8,128)S(1)}, f32[16,4224]{1,0:T(8,128)S(1)}, u32[]{:S(2)}, u32[]{:S(2)}) collective-permute-start(f32[16,4224]{1,0:T(8,128)S(1)} %collective-permute-done.14.refs_1_), channel_id=1, source_target_pairs={{0,2},{2,4},{4,6},{6,7},{7,5},{5,3},{3,1},{1,0},{8,9},{10,8},{12,1... | collective-permute-start | bytes 811016 | tf_op jit(solution)/shard_map/scatter_star_gradient/ppermute | solution.py:338
  37.2 6.5 %collective-permute-start.16 = (f32[16,4224]{1,0:T(8,128)S(1)}, f32[16,4224]{1,0:T(8,128)S(1)}, u32[]{:S(2)}, u32[]{:S(2)}) collective-permute-start(f32[16,4224]{1,0:T(8,128)S(1)} %add.12), channel_id=1, source_target_pairs={{0,2},{2,4},{4,6},{6,7},{7,5},{5,3},{3,1},{1,0},{8,9},{10,8},{12,1... | collective-permute-start | bytes 811016 | tf_op jit(solution)/shard_map/scatter_star_gradient/ppermute | solution.py:338
  38.7 7.2 %collective-permute-start.20 = (f32[16,4224]{1,0:T(8,128)S(1)}, f32[16,4224]{1,0:T(8,128)S(1)}, u32[]{:S(2)}, u32[]{:S(2)}) collective-permute-start(f32[16,4224]{1,0:T(8,128)S(1)} %get-tuple-element.45), channel_id=1, source_target_pairs={{0,8},{8,0},{16,24},{24,16},{1,9},{9,1},{17,25},{25,17},{2,10},{10... | collective-permute-start | bytes 811016 | tf_op jit(solution)/shard_map/scatter_star_gradient/ppermute | solution.py:342
  40.1 6.5 %collective-permute-start.21 = (f32[16,4224]{1,0:T(8,128)S(1)}, f32[16,4224]{1,0:T(8,128)S(1)}, u32[]{:S(2)}, u32[]{:S(2)}) collective-permute-start(f32[16,4224]{1,0:T(8,128)S(1)} %add.14.refs_1_), channel_id=1, source_target_pairs={{0,2},{2,4},{4,6},{6,7},{7,5},{5,3},{3,1},{1,0},{8,9},{10,8},{12,1... | collective-permute-start | bytes 811016 | tf_op jit(solution)/shard_map/scatter_star_gradient/ppermute | solution.py:338
  41.6 4.3 %collective-permute-start.22 = (f32[64,256]{1,0:T(8,128)S(1)}, f32[64,256]{1,0:T(8,128)S(1)}, u32[]{:S(2)}, u32[]{:S(2)}) collective-permute-start(f32[64,256]{1,0:T(8,128)S(1)} %scatter_star_gradient.11), channel_id=1, source_target_pairs={{0,16},{8,24},{16,0},{24,8},{1,17},{9,25},{17,1},{25,9},{2,18},{10... | collective-permute-start | bytes 196616 | tf_op jit(solution)/shard_map/scatter_star_gradient/ppermute | solution.py:342
  43.7 6.5 %collective-permute-start.19 = (f32[16,4224]{1,0:T(8,128)S(1)}, f32[16,4224]{1,0:T(8,128)S(1)}, u32[]{:S(2)}, u32[]{:S(2)}) collective-permute-start(f32[16,4224]{1,0:T(8,128)S(1)} %scatter_star_gradient.10), channel_id=1, source_target_pairs={{0,2},{2,4},{4,6},{6,7},{7,5},{5,3},{3,1},{1,0},{8,9},{10,8},{12,1... | collective-permute-start | bytes 811016 | tf_op jit(solution)/shard_map/scatter_star_gradient/ppermute | solution.py:338
  46.6 6.7 %collective-permute-start.24 = (f32[16,4224]{1,0:T(8,128)S(1)}, f32[16,4224]{1,0:T(8,128)S(1)}, u32[]{:S(2)}, u32[]{:S(2)}) collective-permute-start(f32[16,4224]{1,0:T(8,128)S(1)} %scatter_star_gradient.13.refs_1_), channel_id=1, source_target_pairs={{0,10},{2,12},{4,14},{6,15},{7,13},{5,11},{3,9},{1,8},{8,1},{10,0}... | collective-permute-start | bytes 811016 | tf_op jit(solution)/shard_map/scatter_star_gradient/ppermute | solution.py:338
  50.3 3.7 %collective-permute-start.26 = (f32[8,128]{1,0:T(8,128)S(1)}, f32[8,128]{1,0:T(8,128)S(1)}, u32[]{:S(2)}, u32[]{:S(2)}) collective-permute-start(f32[8,128]{1,0:T(8,128)S(1)} %get-tuple-element.51), channel_id=1, source_target_pairs={{0,2},{2,4},{4,6},{6,7},{7,5},{5,3},{3,1},{1,0},{8,9},{10,8},{12,1... | collective-permute-start | bytes 12296 | tf_op jit(solution)/shard_map/scatter_star_gradient/ppermute | solution.py:338
  51.8 6.4 %collective-permute-start.23 = (f32[16,4096]{1,0:T(8,128)S(1)}, f32[16,4096]{1,0:T(8,128)S(1)}, u32[]{:S(2)}, u32[]{:S(2)}) collective-permute-start(f32[16,4096]{1,0:T(8,128)S(1)} %get-tuple-element.49), channel_id=1, source_target_pairs={{0,2},{2,4},{4,6},{6,7},{7,5},{5,3},{3,1},{1,0},{8,9},{10,8},{12,1... | collective-permute-start | bytes 786440 | tf_op jit(solution)/shard_map/scatter_star_gradient/ppermute | solution.py:338
  53.4 5.4 %collective-permute-start.25 = (f32[32,256]{1,0:T(8,128)S(1)}, f32[32,256]{1,0:T(8,128)S(1)}, u32[]{:S(2)}, u32[]{:S(2)}) collective-permute-start(f32[32,256]{1,0:T(8,128)S(1)} %scatter_star_gradient.16), channel_id=1, source_target_pairs={{0,8},{8,0},{16,24},{24,16},{1,9},{9,1},{17,25},{25,17},{2,10},{10... | collective-permute-start | bytes 98312 | tf_op jit(solution)/shard_map/scatter_star_gradient/ppermute | solution.py:342
  53.9 1.2 %collective-permute-start.27 = (f32[8,128]{1,0:T(8,128)S(1)}, f32[8,128]{1,0:T(8,128)S(1)}, u32[]{:S(2)}, u32[]{:S(2)}) collective-permute-start(f32[8,128]{1,0:T(8,128)S(1)} %scatter_star_gradient.17.refs_0_), channel_id=1, source_target_pairs={{0,8},{8,0},{16,24},{24,16},{1,9},{9,1},{17,25},{25,17},{2,10},{10... | collective-permute-start | bytes 12296 | tf_op jit(solution)/shard_map/scatter_star_gradient/ppermute | solution.py:342
  55.1 3.6 %collective-permute-start.28 = (f32[8,128]{1,0:T(8,128)S(1)}, f32[8,128]{1,0:T(8,128)S(1)}, u32[]{:S(2)}, u32[]{:S(2)}) collective-permute-start(f32[8,128]{1,0:T(8,128)S(1)} %scatter_star_gradient.18.refs_0_), channel_id=1, source_target_pairs={{0,16},{8,24},{16,0},{24,8},{1,17},{9,25},{17,1},{25,9},{2,18},{10... | collective-permute-start | bytes 12296 | tf_op jit(solution)/shard_map/scatter_star_gradient/ppermute | solution.py:342

commit v7 on v6

--- a/solution.py
+++ b/solution.py
@@ -9,7 +9,7 @@
 
 F32 = jnp.float32
 BF16 = jnp.bfloat16
-SUB = 512
+SUB = 1024
 
 
 def two(x):
@@ -374,7 +374,7 @@
             pieces[s] = shift(pieces[s - 1])
             if s == 1:
                 beside = shift(beside)
-                pieces[s], beside = hold(pieces[s], light), hold(beside, light)
+                pieces[s], beside = hold(pieces[s], light, cads[1]), hold(beside, light)
             elif s < far - 1:
                 beside = shift(beside)
                 pieces[s] = hold(pieces[s], *cads[1:])

time: 59.6 us -> 59.5 us (level)
  no operation moved by 1% of the time
where the time goes in v7:
time: 59.5 us; the launch traced here: 59.4 us
  starting transfers between devices  30.5 us (51%)
  waiting for transfers between devices  16.3 us (27%)
  Pallas kernels  9.46 us (16%)
  local copies, waits for them, and re-layouts  2.22 us (4%)
  between operations  0.8 us (1%)
    ppermute x16, starting transfers between devices, shift(): return lax.ppermute(x, ('star', 'cad'), pairs)  25.3 us
    ppermute x16, waiting for transfers between devices, shift(): return lax.ppermute(x, ('star', 'cad'), pairs)  12.2 us
    pallas_call x4, Pallas kernels, big_call(): pl.pallas_call(body_of, in_specs=[vmem] * len(given), out_specs=[vmem] *...  8.37 us
    ppermute x13, starting transfers between devices, swap(): lax.ppermute(x, axis, [(i, i ^ bit) for i in range(lax.axis_size(axis))])  5.17 us
    ppermute x13, waiting for transfers between devices, swap(): lax.ppermute(x, axis, [(i, i ^ bit) for i in range(lax.axis_size(axis))])  4.06 us
    unnamed x8, local copies, waits for them, and re-layouts  2.2 us
  transfers between devices with their start and end apart: 29, of which 15 were waited for; matrix products, arithmetic and copies ran while one was open for 0% of the time, Pallas kernels for 12%

profile of v7, /device:TPU:0, one launch (start us, length us, event | category | flops | bytes accessed | tf_op | source)
XLA Modules:
  0.0 59.4 jit_solution(3402003322193101642)
XLA Ops:
  0.6 0.5 collective-permute-start.6
  1.1 2.6 %collective-permute-start = (f32[16,4096]{1,0:T(8,128)}, f32[16,4096]{1,0:T(8,128)S(1)}, u32[]{:S(2)}, u32[]{:S(2)}) collective-permute-start(f32[16,4096]{1,0:T(8,128)} %bitcast.7), channel_id=1, source_target_pairs={{0,2},{2,4},{4,6},{6,7},{7,5},{5,3},{3,1},{1,0},{8,9},{10,8},{12,1... | collective-permute-start | bytes 786440 | tf_op jit(solution)/shard_map/gather_star_factors/ppermute | solution.py:338
  3.8 0.1 collective-permute-start.1
  3.9 0.0 collective-permute-done.6
  3.9 1.6 %collective-permute-start.7 = (f32[16,4096]{1,0:T(8,128)S(1)}, f32[16,4096]{1,0:T(8,128)S(1)}, u32[]{:S(2)}, u32[]{:S(2)}) collective-permute-start(f32[16,4096]{1,0:T(8,128)S(1)} %collective-permute-done.6), channel_id=1, source_target_pairs={{0,2},{2,4},{4,6},{6,7},{7,5},{5,3},{3,1},{1,0},{8,9},{10,8},{12,1... | collective-permute-start | bytes 786440 | tf_op jit(solution)/shard_map/gather_star_factors/ppermute | solution.py:338
  5.5 2.2 %copy-done = f32[4096,256]{1,0:T(8,128)S(1)} copy-done((f32[4096,256]{1,0:T(8,128)S(1)}, f32[4096,256]{1,0:T(8,128)}, u32[]{:S(2)}) %copy-start) | copy-done | bytes 4194328
  7.7 0.3 shard_map.67.refs_1_.refs_0_
  8.0 0.0 copy-start.2
  8.0 0.0 copy-start.1
  8.0 0.0 collective-permute-done.1.refs_2_.refs_1_.refs_8_.refs_5_.refs_16_
  8.0 0.3 collective-permute-done.refs_0_
  8.3 2.1 %collective-permute-start.2 = (f32[16,4096]{1,0:T(8,128)S(1)}, f32[16,4096]{1,0:T(8,128)S(1)}, u32[]{:S(2)}, u32[]{:S(2)}) collective-permute-start(f32[16,4096]{1,0:T(8,128)S(1)} %gather_star_factors.3.refs_2_.refs_7_), channel_id=1, source_target_pairs={{0,2},{2,4},{4,6},{6,7},{7,5},{5,3},{3,1},{1,0},{8,9},{10,8},{12,1... | collective-permute-start | bytes 786440 | tf_op jit(solution)/shard_map/gather_star_factors/ppermute | solution.py:338
  10.4 1.5 %collective-permute-start.3 = (f32[32,256]{1,0:T(8,128)S(1)}, f32[32,256]{1,0:T(8,128)S(1)}, u32[]{:S(2)}, u32[]{:S(2)}) collective-permute-start(f32[32,256]{1,0:T(8,128)S(1)} %bitcast.11), channel_id=1, source_target_pairs={{0,16},{8,24},{16,0},{24,8},{1,17},{9,25},{17,1},{25,9},{2,18},{10... | collective-permute-start | bytes 98312 | tf_op jit(solution)/shard_map/gather_cadence_factors/ppermute | solution.py:342
  11.9 1.6 %collective-permute-start.8 = (f32[16,4096]{1,0:T(8,128)S(1)}, f32[16,4096]{1,0:T(8,128)S(1)}, u32[]{:S(2)}, u32[]{:S(2)}) collective-permute-start(f32[16,4096]{1,0:T(8,128)S(1)} %gather_star_factors.5), channel_id=1, source_target_pairs={{0,2},{2,4},{4,6},{6,7},{7,5},{5,3},{3,1},{1,0},{8,9},{10,8},{12,1... | collective-permute-start | bytes 786440 | tf_op jit(solution)/shard_map/gather_star_factors/ppermute | solution.py:338
  13.5 0.8 %collective-permute-done.3.refs_2_.refs_9_.refs_6_.refs_17_ = f32[32,256]{1,0:T(8,128)S(1)} collective-permute-done((f32[32,256]{1,0:T(8,128)S(1)}, f32[32,256]{1,0:T(8,128)S(1)}, u32[]{:S(2)}, u32[]{:S(2)}) %collective-permute-start.3) | collective-permute-done | bytes 32800 | tf_op jit(solution)/shard_map/gather_cadence_factors/ppermute | solution.py:342
  14.3 0.9 %collective-permute-done.4.refs_3_.refs_10_.refs_7_.refs_18_ = f32[32,256]{1,0:T(8,128)S(1)} collective-permute-done((f32[32,256]{1,0:T(8,128)S(1)}, f32[32,256]{1,0:T(8,128)S(1)}, u32[]{:S(2)}, u32[]{:S(2)}) %collective-permute-start.4) | collective-permute-done | bytes 32800 | tf_op jit(solution)/shard_map/gather_cadence_factors/ppermute | solution.py:342
  15.2 1.6 %collective-permute-start.5 = (f32[16,4096]{1,0:T(8,128)S(1)}, f32[16,4096]{1,0:T(8,128)S(1)}, u32[]{:S(2)}, u32[]{:S(2)}) collective-permute-start(f32[16,4096]{1,0:T(8,128)S(1)} %gather_star_factors.4.refs_3_.refs_8_), channel_id=1, source_target_pairs={{0,2},{2,4},{4,6},{6,7},{7,5},{5,3},{3,1},{1,0},{8,9},{10,8},{12,1... | collective-permute-start | bytes 786440 | tf_op jit(solution)/shard_map/gather_star_factors/ppermute | solution.py:338
  16.8 1.5 %collective-permute-done.8 = f32[16,4096]{1,0:T(8,128)S(1)} collective-permute-done((f32[16,4096]{1,0:T(8,128)S(1)}, f32[16,4096]{1,0:T(8,128)S(1)}, u32[]{:S(2)}, u32[]{:S(2)}) %collective-permute-start.8) | collective-permute-done | bytes 262176 | tf_op jit(solution)/shard_map/gather_star_factors/ppermute | solution.py:338
  18.3 1.7 %collective-permute-start.12 = (f32[16,4096]{1,0:T(8,128)S(1)}, f32[16,4096]{1,0:T(8,128)S(1)}, u32[]{:S(2)}, u32[]{:S(2)}) collective-permute-start(f32[16,4096]{1,0:T(8,128)S(1)} %collective-permute-done.8), channel_id=1, source_target_pairs={{0,10},{2,12},{4,14},{6,15},{7,13},{5,11},{3,9},{1,8},{8,1},{10,0}... | collective-permute-start | bytes 786440 | tf_op jit(solution)/shard_map/gather_star_factors/ppermute | solution.py:338
  20.0 1.6 %collective-permute-done.5.refs_4_.refs_9_ = f32[16,4096]{1,0:T(8,128)S(1)} collective-permute-done((f32[16,4096]{1,0:T(8,128)S(1)}, f32[16,4096]{1,0:T(8,128)S(1)}, u32[]{:S(2)}, u32[]{:S(2)}) %collective-permute-start.5) | collective-permute-done | bytes 262176 | tf_op jit(solution)/shard_map/gather_star_factors/ppermute | solution.py:338
  21.6 1.6 %collective-permute-start.11 = (f32[16,2048]{1,0:T(8,128)S(1)}, f32[16,2048]{1,0:T(8,128)S(1)}, u32[]{:S(2)}, u32[]{:S(2)}) collective-permute-start(f32[16,2048]{1,0:T(8,128)S(1)} %get-tuple-element.56), channel_id=1, source_target_pairs={{0,2},{2,4},{4,6},{6,7},{7,5},{5,3},{3,1},{1,0},{8,9},{10,8},{12,1... | collective-permute-start | bytes 393224 | tf_op jit(solution)/shard_map/gather_star_factors/ppermute | solution.py:338
  23.3 1.6 %collective-permute-start.13 = (f32[16,2048]{1,0:T(8,128)S(1)}, f32[16,2048]{1,0:T(8,128)S(1)}, u32[]{:S(2)}, u32[]{:S(2)}) collective-permute-start(f32[16,2048]{1,0:T(8,128)S(1)} %get-tuple-element.55), channel_id=1, source_target_pairs={{0,2},{2,4},{4,6},{6,7},{7,5},{5,3},{3,1},{1,0},{8,9},{10,8},{12,1... | collective-permute-start | bytes 393224 | tf_op jit(solution)/shard_map/gather_star_factors/ppermute | solution.py:338
  24.9 1.9 %shard_map.68.refs_0_ = f32[4096,256]{1,0:T(8,128)S(1)} custom-call(f32[4096,256]{1,0:T(8,128)S(1)} %shard_map.67.refs_1_.refs_0_, f32[16,4096]{1,0:T(8,128)S(1)} %bitcast.8, f32[16,4096]{1,0:T(8,128)S(1)} %gather_star_factors.3.refs_2_.refs_7_, f32[16,4096]{1,0:T(8,128)S(1)} %gather_star_factors.4.refs_3_.refs_8_, ...), custom_call_target="tpu_custom_call" | custom-call | flops 1610612736 | bytes 1048576 | tf_op jit(solution)/shard_map/pallas_call | solution.py:195
  26.8 1.8 %shard_map.69 = (bf16[2048,256]{1,0:T(8,128)(2,1)S(1)}, bf16[2048,256]{1,0:T(8,128)(2,1)S(1)}, f32[8,256]{1,0:T(8,128)S(1)}, f32[16,2048]{1,0:T(8,128)S(1)}, f32...) custom-call(f32[4096,256]{1,0:T(8,128)S(1)} %shard_map.68.refs_0_, s32[1,256]{1,0:T(1,128)S(1)} %bitcast.17, ...), custom_call_target="tpu_custom_call" | custom-call | flops 536870912 | bytes 1048576 | tf_op jit(solution)/shard_map/pallas_call | solution.py:195
  28.6 1.8 %shard_map.70 = (bf16[2048,256]{1,0:T(8,128)(2,1)S(1)}, bf16[2048,256]{1,0:T(8,128)(2,1)S(1)}, f32[8,128]{1,0:T(8,128)S(1)}, f32[16,4224]{1,0:T(8,128)S(1)}, f32...) custom-call(f32[4096,256]{1,0:T(8,128)S(1)} %shard_map.68.refs_0_, s32[1,256]{1,0:T(1,128)S(1)} %bitcast.18, ...), custom_call_target="tpu_custom_call" | custom-call | flops 536870912 | bytes 1048576 | tf_op jit(solution)/shard_map/pallas_call | solution.py:195
  30.5 0.1 collective-permute-start.14
  30.5 1.6 %collective-permute-start.15 = (f32[16,4224]{1,0:T(8,128)S(1)}, f32[16,4224]{1,0:T(8,128)S(1)}, u32[]{:S(2)}, u32[]{:S(2)}) collective-permute-start(f32[16,4224]{1,0:T(8,128)S(1)} %get-tuple-element.43), channel_id=1, source_target_pairs={{0,2},{2,4},{4,6},{6,7},{7,5},{5,3},{3,1},{1,0},{8,9},{10,8},{12,1... | collective-permute-start | bytes 811016 | tf_op jit(solution)/shard_map/scatter_star_gradient/ppermute | solution.py:338
  32.1 1.5 %collective-permute-start.18 = (f32[16,4224]{1,0:T(8,128)S(1)}, f32[16,4224]{1,0:T(8,128)S(1)}, u32[]{:S(2)}, u32[]{:S(2)}) collective-permute-start(f32[16,4224]{1,0:T(8,128)S(1)} %collective-permute-done.14.refs_1_), channel_id=1, source_target_pairs={{0,2},{2,4},{4,6},{6,7},{7,5},{5,3},{3,1},{1,0},{8,9},{10,8},{12,1... | collective-permute-start | bytes 811016 | tf_op jit(solution)/shard_map/scatter_star_gradient/ppermute | solution.py:338
  33.6 2.8 %shard_map.72 = (f32[16,4224]{1,0:T(8,128)S(1)}, f32[16,4224]{1,0:T(8,128)S(1)}, f32[16,4224]{1,0:T(8,128)S(1)}, f32[16,4224]{1,0:T(8,128)S(1)}, f32[16,4224]{1,...) custom-call(bf16[2048,256]{1,0:T(8,128)(2,1)S(1)} %get-tuple-element.29.refs_0_, ...), custom_call_target="tpu_custom_call" | custom-call | flops 1610612736 | bytes 1048576 | tf_op jit(solution)/shard_map/pallas_call | solution.py:195
  36.4 0.6 collective-permute-done.15
  37.1 1.6 %collective-permute-start.16 = (f32[16,4224]{1,0:T(8,128)S(1)}, f32[16,4224]{1,0:T(8,128)S(1)}, u32[]{:S(2)}, u32[]{:S(2)}) collective-permute-start(f32[16,4224]{1,0:T(8,128)S(1)} %add.12), channel_id=1, source_target_pairs={{0,2},{2,4},{4,6},{6,7},{7,5},{5,3},{3,1},{1,0},{8,9},{10,8},{12,1... | collective-permute-start | bytes 811016 | tf_op jit(solution)/shard_map/scatter_star_gradient/ppermute | solution.py:338
  38.6 1.3 %collective-permute-done.18 = f32[16,4224]{1,0:T(8,128)S(1)} collective-permute-done((f32[16,4224]{1,0:T(8,128)S(1)}, f32[16,4224]{1,0:T(8,128)S(1)}, u32[]{:S(2)}, u32[]{:S(2)}) %collective-permute-start.18) | collective-permute-done | bytes 270368 | tf_op jit(solution)/shard_map/scatter_star_gradient/ppermute | solution.py:338
  40.0 1.6 %collective-permute-start.21 = (f32[16,4224]{1,0:T(8,128)S(1)}, f32[16,4224]{1,0:T(8,128)S(1)}, u32[]{:S(2)}, u32[]{:S(2)}) collective-permute-start(f32[16,4224]{1,0:T(8,128)S(1)} %add.14.refs_1_), channel_id=1, source_target_pairs={{0,2},{2,4},{4,6},{6,7},{7,5},{5,3},{3,1},{1,0},{8,9},{10,8},{12,1... | collective-permute-start | bytes 811016 | tf_op jit(solution)/shard_map/scatter_star_gradient/ppermute | solution.py:338
  41.5 1.5 %collective-permute-start.22 = (f32[64,256]{1,0:T(8,128)S(1)}, f32[64,256]{1,0:T(8,128)S(1)}, u32[]{:S(2)}, u32[]{:S(2)}) collective-permute-start(f32[64,256]{1,0:T(8,128)S(1)} %scatter_star_gradient.11), channel_id=1, source_target_pairs={{0,16},{8,24},{16,0},{24,8},{1,17},{9,25},{17,1},{25,9},{2,18},{10... | collective-permute-start | bytes 196616 | tf_op jit(solution)/shard_map/scatter_star_gradient/ppermute | solution.py:342
  43.1 0.5 collective-permute-done.16
  43.6 1.6 %collective-permute-start.19 = (f32[16,4224]{1,0:T(8,128)S(1)}, f32[16,4224]{1,0:T(8,128)S(1)}, u32[]{:S(2)}, u32[]{:S(2)}) collective-permute-start(f32[16,4224]{1,0:T(8,128)S(1)} %scatter_star_gradient.10), channel_id=1, source_target_pairs={{0,2},{2,4},{4,6},{6,7},{7,5},{5,3},{3,1},{1,0},{8,9},{10,8},{12,1... | collective-permute-start | bytes 811016 | tf_op jit(solution)/shard_map/scatter_star_gradient/ppermute | solution.py:338
  45.2 0.6 %collective-permute-done.22.got = f32[64,256]{1,0:T(8,128)S(1)} collective-permute-done((f32[64,256]{1,0:T(8,128)S(1)}, f32[64,256]{1,0:T(8,128)S(1)}, u32[]{:S(2)}, u32[]{:S(2)}) %collective-permute-start.22) | collective-permute-done | bytes 65568 | tf_op jit(solution)/shard_map/scatter_star_gradient/ppermute | solution.py:342
  45.8 0.7 %collective-permute-done.21 = f32[16,4224]{1,0:T(8,128)S(1)} collective-permute-done((f32[16,4224]{1,0:T(8,128)S(1)}, f32[16,4224]{1,0:T(8,128)S(1)}, u32[]{:S(2)}, u32[]{:S(2)}) %collective-permute-start.21) | collective-permute-done | bytes 270368 | tf_op jit(solution)/shard_map/scatter_star_gradient/ppermute | solution.py:338
  46.5 0.1 collective-permute-start.24
  46.6 3.5 %collective-permute-done.19.refs_0_ = f32[16,4224]{1,0:T(8,128)S(1)} collective-permute-done((f32[16,4224]{1,0:T(8,128)S(1)}, f32[16,4224]{1,0:T(8,128)S(1)}, u32[]{:S(2)}, u32[]{:S(2)}) %collective-permute-start.19) | collective-permute-done | bytes 270368 | tf_op jit(solution)/shard_map/scatter_star_gradient/ppermute | solution.py:338
  50.2 1.6 %collective-permute-start.26 = (f32[8,128]{1,0:T(8,128)S(1)}, f32[8,128]{1,0:T(8,128)S(1)}, u32[]{:S(2)}, u32[]{:S(2)}) collective-permute-start(f32[8,128]{1,0:T(8,128)S(1)} %get-tuple-element.51), channel_id=1, source_target_pairs={{0,2},{2,4},{4,6},{6,7},{7,5},{5,3},{3,1},{1,0},{8,9},{10,8},{12,1... | collective-permute-start | bytes 12296 | tf_op jit(solution)/shard_map/scatter_star_gradient/ppermute | solution.py:338
  51.7 1.5 %collective-permute-start.23 = (f32[16,4096]{1,0:T(8,128)S(1)}, f32[16,4096]{1,0:T(8,128)S(1)}, u32[]{:S(2)}, u32[]{:S(2)}) collective-permute-start(f32[16,4096]{1,0:T(8,128)S(1)} %get-tuple-element.49), channel_id=1, source_target_pairs={{0,2},{2,4},{4,6},{6,7},{7,5},{5,3},{3,1},{1,0},{8,9},{10,8},{12,1... | collective-permute-start | bytes 786440 | tf_op jit(solution)/shard_map/scatter_star_gradient/ppermute | solution.py:338
  53.3 0.6 collective-permute-done.26.near
  53.8 1.2 %collective-permute-done.27.refs_1_ = f32[8,128]{1,0:T(8,128)S(1)} collective-permute-done((f32[8,128]{1,0:T(8,128)S(1)}, f32[8,128]{1,0:T(8,128)S(1)}, u32[]{:S(2)}, u32[]{:S(2)}) %collective-permute-start.27) | collective-permute-done | bytes 4128 | tf_op jit(solution)/shard_map/scatter_star_gradient/ppermute | solution.py:342
  55.0 1.4 %collective-permute-start.28 = (f32[8,128]{1,0:T(8,128)S(1)}, f32[8,128]{1,0:T(8,128)S(1)}, u32[]{:S(2)}, u32[]{:S(2)}) collective-permute-start(f32[8,128]{1,0:T(8,128)S(1)} %scatter_star_gradient.18.refs_0_), channel_id=1, source_target_pairs={{0,16},{8,24},{16,0},{24,8},{1,17},{9,25},{17,1},{25,9},{2,18},{10... | collective-permute-start | bytes 12296 | tf_op jit(solution)/shard_map/scatter_star_gradient/ppermute | solution.py:342
  56.5 1.6 %collective-permute-done.23.up = f32[16,4096]{1,0:T(8,128)S(1)} collective-permute-done((f32[16,4096]{1,0:T(8,128)S(1)}, f32[16,4096]{1,0:T(8,128)S(1)}, u32[]{:S(2)}, u32[]{:S(2)}) %collective-permute-start.23) | collective-permute-done | bytes 262176 | tf_op jit(solution)/shard_map/scatter_star_gradient/ppermute | solution.py:338
  58.1 0.5 collective-permute-done.28.refs_1_
  58.6 0.8 %scatter_star_gradient.19 = (f32[16,4096]{1,0:T(8,128)}, f32[32,256]{1,0:T(8,128)}, f32[1,1]{1,0:T(1,128)}) custom-call(f32[16,4224]{1,0:T(8,128)S(1)} %get-tuple-element.39.mine, f32[16,4096]{1,0:T(8,128)S(1)} %collective-permute-done.23.up, f32[16,4224]{1,0:T(8,128)S(1)} %collective-permute-done.24.refs_1_.beside.back, ...), custom_call_target="tpu_custom_call" | custom-call | bytes 1024 | tf_op jit(solution)/shard_map/scatter_star_gradient/pallas_call | solution.py:248
  (42 shorter events, 0.3 us)
Async XLA Ops:
  0.6 3.2 %collective-permute-start.6 = (f32[16,4096]{1,0:T(8,128)}, f32[16,4096]{1,0:T(8,128)S(1)}, u32[]{:S(2)}, u32[]{:S(2)}) collective-permute-start(f32[16,4096]{1,0:T(8,128)} %bitcast.6), channel_id=1, source_target_pairs={{0,8},{8,0},{16,24},{24,16},{1,9},{9,1},{17,25},{25,17},{2,10},{10... | collective-permute-start | bytes 786440 | tf_op jit(solution)/shard_map/gather_star_factors/ppermute | solution.py:342
  1.1 7.1 %collective-permute-start = (f32[16,4096]{1,0:T(8,128)}, f32[16,4096]{1,0:T(8,128)S(1)}, u32[]{:S(2)}, u32[]{:S(2)}) collective-permute-start(f32[16,4096]{1,0:T(8,128)} %bitcast.7), channel_id=1, source_target_pairs={{0,2},{2,4},{4,6},{6,7},{7,5},{5,3},{3,1},{1,0},{8,9},{10,8},{12,1... | collective-permute-start | bytes 786440 | tf_op jit(solution)/shard_map/gather_star_factors/ppermute | solution.py:338
  3.8 4.2 %collective-permute-start.1 = (f32[32,256]{1,0:T(8,128)}, f32[32,256]{1,0:T(8,128)S(1)}, u32[]{:S(2)}, u32[]{:S(2)}) collective-permute-start(f32[32,256]{1,0:T(8,128)} %bitcast.10), channel_id=1, source_target_pairs={{0,8},{8,0},{16,24},{24,16},{1,9},{9,1},{17,25},{25,17},{2,10},{10... | collective-permute-start | bytes 98312 | tf_op jit(solution)/shard_map/gather_cadence_factors/ppermute | solution.py:342
  3.9 8.0 %collective-permute-start.7 = (f32[16,4096]{1,0:T(8,128)S(1)}, f32[16,4096]{1,0:T(8,128)S(1)}, u32[]{:S(2)}, u32[]{:S(2)}) collective-permute-start(f32[16,4096]{1,0:T(8,128)S(1)} %collective-permute-done.6), channel_id=1, source_target_pairs={{0,2},{2,4},{4,6},{6,7},{7,5},{5,3},{3,1},{1,0},{8,9},{10,8},{12,1... | collective-permute-start | bytes 786440 | tf_op jit(solution)/shard_map/gather_star_factors/ppermute | solution.py:338
  5.5 2.2 %copy-start = (f32[4096,256]{1,0:T(8,128)S(1)}, f32[4096,256]{1,0:T(8,128)}, u32[]{:S(2)}) copy-start(f32[4096,256]{1,0:T(8,128)} %refs_0_.1) | copy-start | bytes 12582916
  8.0 2.4 %copy-start.2 = (f32[256,32]{0,1:T(8,128)S(1)}, f32[256,32]{0,1:T(8,128)}, u32[]{:S(2)}) copy-start(f32[256,32]{0,1:T(8,128)} %param.7) | copy-start | bytes 98308
  8.0 16.9 %copy-start.1 = (f32[4096,16]{0,1:T(8,128)S(1)}, f32[4096,16]{0,1:T(8,128)}, u32[]{:S(2)}) copy-start(f32[4096,16]{0,1:T(8,128)} %param.6) | copy-start | bytes 786436
  8.3 7.0 %collective-permute-start.2 = (f32[16,4096]{1,0:T(8,128)S(1)}, f32[16,4096]{1,0:T(8,128)S(1)}, u32[]{:S(2)}, u32[]{:S(2)}) collective-permute-start(f32[16,4096]{1,0:T(8,128)S(1)} %gather_star_factors.3.refs_2_.refs_7_), channel_id=1, source_target_pairs={{0,2},{2,4},{4,6},{6,7},{7,5},{5,3},{3,1},{1,0},{8,9},{10,8},{12,1... | collective-permute-start | bytes 786440 | tf_op jit(solution)/shard_map/gather_star_factors/ppermute | solution.py:338
  10.4 3.9 %collective-permute-start.3 = (f32[32,256]{1,0:T(8,128)S(1)}, f32[32,256]{1,0:T(8,128)S(1)}, u32[]{:S(2)}, u32[]{:S(2)}) collective-permute-start(f32[32,256]{1,0:T(8,128)S(1)} %bitcast.11), channel_id=1, source_target_pairs={{0,16},{8,24},{16,0},{24,8},{1,17},{9,25},{17,1},{25,9},{2,18},{10... | collective-permute-start | bytes 98312 | tf_op jit(solution)/shard_map/gather_cadence_factors/ppermute | solution.py:342
  11.9 3.3 %collective-permute-start.4 = (f32[32,256]{1,0:T(8,128)S(1)}, f32[32,256]{1,0:T(8,128)S(1)}, u32[]{:S(2)}, u32[]{:S(2)}) collective-permute-start(f32[32,256]{1,0:T(8,128)S(1)} %bitcast.12), channel_id=1, source_target_pairs={{0,24},{8,16},{16,8},{24,0},{1,25},{9,17},{17,9},{25,1},{2,26},{10... | collective-permute-start | bytes 98312 | tf_op jit(solution)/shard_map/gather_cadence_factors/ppermute | solution.py:342
  11.9 6.4 %collective-permute-start.8 = (f32[16,4096]{1,0:T(8,128)S(1)}, f32[16,4096]{1,0:T(8,128)S(1)}, u32[]{:S(2)}, u32[]{:S(2)}) collective-permute-start(f32[16,4096]{1,0:T(8,128)S(1)} %gather_star_factors.5), channel_id=1, source_target_pairs={{0,2},{2,4},{4,6},{6,7},{7,5},{5,3},{3,1},{1,0},{8,9},{10,8},{12,1... | collective-permute-start | bytes 786440 | tf_op jit(solution)/shard_map/gather_star_factors/ppermute | solution.py:338
  15.2 6.4 %collective-permute-start.5 = (f32[16,4096]{1,0:T(8,128)S(1)}, f32[16,4096]{1,0:T(8,128)S(1)}, u32[]{:S(2)}, u32[]{:S(2)}) collective-permute-start(f32[16,4096]{1,0:T(8,128)S(1)} %gather_star_factors.4.refs_3_.refs_8_), channel_id=1, source_target_pairs={{0,2},{2,4},{4,6},{6,7},{7,5},{5,3},{3,1},{1,0},{8,9},{10,8},{12,1... | collective-permute-start | bytes 786440 | tf_op jit(solution)/shard_map/gather_star_factors/ppermute | solution.py:338
  16.8 8.0 %collective-permute-start.10 = (f32[16,4096]{1,0:T(8,128)S(1)}, f32[16,4096]{1,0:T(8,128)S(1)}, u32[]{:S(2)}, u32[]{:S(2)}) collective-permute-start(f32[16,4096]{1,0:T(8,128)S(1)} %gather_star_factors.5), channel_id=1, source_target_pairs={{0,8},{8,0},{16,24},{24,16},{1,9},{9,1},{17,25},{25,17},{2,10},{10... | collective-permute-start | bytes 786440 | tf_op jit(solution)/shard_map/gather_star_factors/ppermute | solution.py:342
  18.3 6.6 %collective-permute-start.9 = (f32[16,4096]{1,0:T(8,128)S(1)}, f32[16,4096]{1,0:T(8,128)S(1)}, u32[]{:S(2)}, u32[]{:S(2)}) collective-permute-start(f32[16,4096]{1,0:T(8,128)S(1)} %collective-permute-done.8), channel_id=1, source_target_pairs={{0,8},{8,0},{16,24},{24,16},{1,9},{9,1},{17,25},{25,17},{2,10},{10... | collective-permute-start | bytes 786440 | tf_op jit(solution)/shard_map/gather_star_factors/ppermute | solution.py:342
  18.3 8.5 %collective-permute-start.12 = (f32[16,4096]{1,0:T(8,128)S(1)}, f32[16,4096]{1,0:T(8,128)S(1)}, u32[]{:S(2)}, u32[]{:S(2)}) collective-permute-start(f32[16,4096]{1,0:T(8,128)S(1)} %collective-permute-done.8), channel_id=1, source_target_pairs={{0,10},{2,12},{4,14},{6,15},{7,13},{5,11},{3,9},{1,8},{8,1},{10,0}... | collective-permute-start | bytes 786440 | tf_op jit(solution)/shard_map/gather_star_factors/ppermute | solution.py:338
  21.6 5.1 %collective-permute-start.11 = (f32[16,2048]{1,0:T(8,128)S(1)}, f32[16,2048]{1,0:T(8,128)S(1)}, u32[]{:S(2)}, u32[]{:S(2)}) collective-permute-start(f32[16,2048]{1,0:T(8,128)S(1)} %get-tuple-element.56), channel_id=1, source_target_pairs={{0,2},{2,4},{4,6},{6,7},{7,5},{5,3},{3,1},{1,0},{8,9},{10,8},{12,1... | collective-permute-start | bytes 393224 | tf_op jit(solution)/shard_map/gather_star_factors/ppermute | solution.py:338
  23.3 3.5 %copy-start.3 = (s32[256]{0:T(256)S(1)}, s32[256]{0:T(256)}, u32[]{:S(2)}) copy-start(s32[256]{0:T(256)} %param.5) | copy-start | bytes 3076
  23.3 5.3 %collective-permute-start.13 = (f32[16,2048]{1,0:T(8,128)S(1)}, f32[16,2048]{1,0:T(8,128)S(1)}, u32[]{:S(2)}, u32[]{:S(2)}) collective-permute-start(f32[16,2048]{1,0:T(8,128)S(1)} %get-tuple-element.55), channel_id=1, source_target_pairs={{0,2},{2,4},{4,6},{6,7},{7,5},{5,3},{3,1},{1,0},{8,9},{10,8},{12,1... | collective-permute-start | bytes 393224 | tf_op jit(solution)/shard_map/gather_star_factors/ppermute | solution.py:338
  30.5 1.6 %collective-permute-start.14 = (f32[16,4224]{1,0:T(8,128)S(1)}, f32[16,4224]{1,0:T(8,128)S(1)}, u32[]{:S(2)}, u32[]{:S(2)}) collective-permute-start(f32[16,4224]{1,0:T(8,128)S(1)} %get-tuple-element.38), channel_id=1, source_target_pairs={{0,8},{8,0},{16,24},{24,16},{1,9},{9,1},{17,25},{25,17},{2,10},{10... | collective-permute-start | bytes 811016 | tf_op jit(solution)/shard_map/ppermute | solution.py:342
  30.5 6.5 %collective-permute-start.15 = (f32[16,4224]{1,0:T(8,128)S(1)}, f32[16,4224]{1,0:T(8,128)S(1)}, u32[]{:S(2)}, u32[]{:S(2)}) collective-permute-start(f32[16,4224]{1,0:T(8,128)S(1)} %get-tuple-element.43), channel_id=1, source_target_pairs={{0,2},{2,4},{4,6},{6,7},{7,5},{5,3},{3,1},{1,0},{8,9},{10,8},{12,1... | collective-permute-start | bytes 811016 | tf_op jit(solution)/shard_map/scatter_star_gradient/ppermute | solution.py:338
  32.1 6.6 %collective-permute-start.17 = (f32[16,4224]{1,0:T(8,128)S(1)}, f32[16,4224]{1,0:T(8,128)S(1)}, u32[]{:S(2)}, u32[]{:S(2)}) collective-permute-start(f32[16,4224]{1,0:T(8,128)S(1)} %get-tuple-element.44), channel_id=1, source_target_pairs={{0,8},{8,0},{16,24},{24,16},{1,9},{9,1},{17,25},{25,17},{2,10},{10... | collective-permute-start | bytes 811016 | tf_op jit(solution)/shard_map/ppermute | solution.py:342
  32.1 7.8 %collective-permute-start.18 = (f32[16,4224]{1,0:T(8,128)S(1)}, f32[16,4224]{1,0:T(8,128)S(1)}, u32[]{:S(2)}, u32[]{:S(2)}) collective-permute-start(f32[16,4224]{1,0:T(8,128)S(1)} %collective-permute-done.14.refs_1_), channel_id=1, source_target_pairs={{0,2},{2,4},{4,6},{6,7},{7,5},{5,3},{3,1},{1,0},{8,9},{10,8},{12,1... | collective-permute-start | bytes 811016 | tf_op jit(solution)/shard_map/scatter_star_gradient/ppermute | solution.py:338
  37.1 6.5 %collective-permute-start.16 = (f32[16,4224]{1,0:T(8,128)S(1)}, f32[16,4224]{1,0:T(8,128)S(1)}, u32[]{:S(2)}, u32[]{:S(2)}) collective-permute-start(f32[16,4224]{1,0:T(8,128)S(1)} %add.12), channel_id=1, source_target_pairs={{0,2},{2,4},{4,6},{6,7},{7,5},{5,3},{3,1},{1,0},{8,9},{10,8},{12,1... | collective-permute-start | bytes 811016 | tf_op jit(solution)/shard_map/scatter_star_gradient/ppermute | solution.py:338
  38.6 7.2 %collective-permute-start.20 = (f32[16,4224]{1,0:T(8,128)S(1)}, f32[16,4224]{1,0:T(8,128)S(1)}, u32[]{:S(2)}, u32[]{:S(2)}) collective-permute-start(f32[16,4224]{1,0:T(8,128)S(1)} %get-tuple-element.45), channel_id=1, source_target_pairs={{0,8},{8,0},{16,24},{24,16},{1,9},{9,1},{17,25},{25,17},{2,10},{10... | collective-permute-start | bytes 811016 | tf_op jit(solution)/shard_map/scatter_star_gradient/ppermute | solution.py:342
  40.0 6.5 %collective-permute-start.21 = (f32[16,4224]{1,0:T(8,128)S(1)}, f32[16,4224]{1,0:T(8,128)S(1)}, u32[]{:S(2)}, u32[]{:S(2)}) collective-permute-start(f32[16,4224]{1,0:T(8,128)S(1)} %add.14.refs_1_), channel_id=1, source_target_pairs={{0,2},{2,4},{4,6},{6,7},{7,5},{5,3},{3,1},{1,0},{8,9},{10,8},{12,1... | collective-permute-start | bytes 811016 | tf_op jit(solution)/shard_map/scatter_star_gradient/ppermute | solution.py:338
  41.5 4.3 %collective-permute-start.22 = (f32[64,256]{1,0:T(8,128)S(1)}, f32[64,256]{1,0:T(8,128)S(1)}, u32[]{:S(2)}, u32[]{:S(2)}) collective-permute-start(f32[64,256]{1,0:T(8,128)S(1)} %scatter_star_gradient.11), channel_id=1, source_target_pairs={{0,16},{8,24},{16,0},{24,8},{1,17},{9,25},{17,1},{25,9},{2,18},{10... | collective-permute-start | bytes 196616 | tf_op jit(solution)/shard_map/scatter_star_gradient/ppermute | solution.py:342
  43.6 6.5 %collective-permute-start.19 = (f32[16,4224]{1,0:T(8,128)S(1)}, f32[16,4224]{1,0:T(8,128)S(1)}, u32[]{:S(2)}, u32[]{:S(2)}) collective-permute-start(f32[16,4224]{1,0:T(8,128)S(1)} %scatter_star_gradient.10), channel_id=1, source_target_pairs={{0,2},{2,4},{4,6},{6,7},{7,5},{5,3},{3,1},{1,0},{8,9},{10,8},{12,1... | collective-permute-start | bytes 811016 | tf_op jit(solution)/shard_map/scatter_star_gradient/ppermute | solution.py:338
  46.5 6.7 %collective-permute-start.24 = (f32[16,4224]{1,0:T(8,128)S(1)}, f32[16,4224]{1,0:T(8,128)S(1)}, u32[]{:S(2)}, u32[]{:S(2)}) collective-permute-start(f32[16,4224]{1,0:T(8,128)S(1)} %scatter_star_gradient.13.refs_1_), channel_id=1, source_target_pairs={{0,10},{2,12},{4,14},{6,15},{7,13},{5,11},{3,9},{1,8},{8,1},{10,0}... | collective-permute-start | bytes 811016 | tf_op jit(solution)/shard_map/scatter_star_gradient/ppermute | solution.py:338
  50.2 3.7 %collective-permute-start.26 = (f32[8,128]{1,0:T(8,128)S(1)}, f32[8,128]{1,0:T(8,128)S(1)}, u32[]{:S(2)}, u32[]{:S(2)}) collective-permute-start(f32[8,128]{1,0:T(8,128)S(1)} %get-tuple-element.51), channel_id=1, source_target_pairs={{0,2},{2,4},{4,6},{6,7},{7,5},{5,3},{3,1},{1,0},{8,9},{10,8},{12,1... | collective-permute-start | bytes 12296 | tf_op jit(solution)/shard_map/scatter_star_gradient/ppermute | solution.py:338
  51.7 6.4 %collective-permute-start.23 = (f32[16,4096]{1,0:T(8,128)S(1)}, f32[16,4096]{1,0:T(8,128)S(1)}, u32[]{:S(2)}, u32[]{:S(2)}) collective-permute-start(f32[16,4096]{1,0:T(8,128)S(1)} %get-tuple-element.49), channel_id=1, source_target_pairs={{0,2},{2,4},{4,6},{6,7},{7,5},{5,3},{3,1},{1,0},{8,9},{10,8},{12,1... | collective-permute-start | bytes 786440 | tf_op jit(solution)/shard_map/scatter_star_gradient/ppermute | solution.py:338
  53.3 5.3 %collective-permute-start.25 = (f32[32,256]{1,0:T(8,128)S(1)}, f32[32,256]{1,0:T(8,128)S(1)}, u32[]{:S(2)}, u32[]{:S(2)}) collective-permute-start(f32[32,256]{1,0:T(8,128)S(1)} %scatter_star_gradient.16), channel_id=1, source_target_pairs={{0,8},{8,0},{16,24},{24,16},{1,9},{9,1},{17,25},{25,17},{2,10},{10... | collective-permute-start | bytes 98312 | tf_op jit(solution)/shard_map/scatter_star_gradient/ppermute | solution.py:342
  53.8 1.2 %collective-permute-start.27 = (f32[8,128]{1,0:T(8,128)S(1)}, f32[8,128]{1,0:T(8,128)S(1)}, u32[]{:S(2)}, u32[]{:S(2)}) collective-permute-start(f32[8,128]{1,0:T(8,128)S(1)} %scatter_star_gradient.17.refs_0_), channel_id=1, source_target_pairs={{0,8},{8,0},{16,24},{24,16},{1,9},{9,1},{17,25},{25,17},{2,10},{10... | collective-permute-start | bytes 12296 | tf_op jit(solution)/shard_map/scatter_star_gradient/ppermute | solution.py:342
  55.0 3.6 %collective-permute-start.28 = (f32[8,128]{1,0:T(8,128)S(1)}, f32[8,128]{1,0:T(8,128)S(1)}, u32[]{:S(2)}, u32[]{:S(2)}) collective-permute-start(f32[8,128]{1,0:T(8,128)S(1)} %scatter_star_gradient.18.refs_0_), channel_id=1, source_target_pairs={{0,16},{8,24},{16,0},{24,8},{1,17},{9,25},{17,1},{25,9},{2,18},{10... | collective-permute-start | bytes 12296 | tf_op jit(solution)/shard_map/scatter_star_gradient/ppermute | solution.py:342
